TPU v7x, 512 devices: a whole 4x8x8 slice. The times are simulated.
512 devices in a mesh: row: 16 (over y, core), col: 32 (over x, z).
Axes of the slice: x: 4, y: 8, z: 8, core: 2. Of those that a mesh axis runs over, the one named last changes fastest.
Arguments:
- image_embeddings: float32 [16384, 512], P('row', 'col'), as said below
- text_embeddings: float32 [16384, 512], P('col', 'row'), as said below
- negatives_mask: int32 [64, 64], replicated, may hold values from 0 to 1, as said below
Outputs:
- grad_image: float32 [16384, 512], P('row', 'col')
- grad_text: float32 [16384, 512], P('col', 'row')
Inputs may be any that keep to these rules, and one draw needn't show every extreme that they name: `image_embeddings`: embedding entries lie within -4 to 4. `text_embeddings`: embedding entries lie within -4 to 4. `negatives_mask`: 0 or 1; the diagonal blocks are allowed whatever it holds there.
All inputs are finite; a program needn't handle non-finite values.
Results may differ from a plain program's by a relative error of at most 0.0003.
Values sent between devices are 32-bit elements; how exact they have to be, the bound alone decides.
No kernel may reach another device: no remote copies, remote signals or barrier semaphores. Data moves between devices by JAX's collectives and lax.ppermute only.
A program may use at most 64 MiB of HBM per device.

v0:
```python
import jax
import jax.numpy as jnp
from jax import lax
from jax.sharding import PartitionSpec as P

BLK = 256


NEG = -1e30


def body(image_embeddings, text_embeddings, negatives_mask):
    images = lax.all_gather(image_embeddings, "col", axis=1, tiled=True)
    texts = lax.all_gather(text_embeddings, "row", axis=1, tiled=True)
    rows = images.shape[0]
    cols = texts.shape[0]
    width = images.shape[1]
    inv = width ** (-0.5)
    row_start = lax.axis_index("row") * rows
    col_start = lax.axis_index("col") * cols
    logits = (
        jnp.dot(
            images, texts.T, precision=lax.Precision.HIGHEST, preferred_element_type=jnp.float32
        )
        * inv
    )
    row_blocks = rows // BLK
    col_blocks = cols // BLK
    first_row = row_start // BLK
    first_col = col_start // BLK
    window = lax.dynamic_slice(negatives_mask, (first_row, first_col), (row_blocks, col_blocks))
    row_ids = first_row + jnp.arange(row_blocks, dtype=jnp.int32)
    col_ids = first_col + jnp.arange(col_blocks, dtype=jnp.int32)
    block_allow = (window > 0) | (row_ids[:, None] == col_ids[None, :])
    allowed = jnp.broadcast_to(
        block_allow[:, None, :, None], (row_blocks, BLK, col_blocks, BLK)
    ).reshape(rows, cols)
    masked = jnp.where(allowed, logits, NEG)
    row_max = lax.pmax(jnp.max(masked, axis=1), "col")
    row_sum = lax.psum(
        jnp.sum(jnp.where(allowed, jnp.exp(logits - row_max[:, None]), 0.0), axis=1), "col"
    )
    col_max = lax.pmax(jnp.max(masked, axis=0), "row")
    col_sum = lax.psum(
        jnp.sum(jnp.where(allowed, jnp.exp(logits - col_max[None, :]), 0.0), axis=0), "row"
    )
    row_lse = row_max + jnp.log(row_sum)
    col_lse = col_max + jnp.log(col_sum)
    diagonal = (
        (row_start + jnp.arange(rows, dtype=jnp.int32))[:, None]
        == (col_start + jnp.arange(cols, dtype=jnp.int32))[None, :]
    ).astype(jnp.float32)
    grad_logits = (
        jnp.where(
            allowed,
            0.5 * (jnp.exp(logits - row_lse[:, None]) + jnp.exp(logits - col_lse[None, :])),
            0.0,
        )
        - diagonal
    )
    image_terms = (
        jnp.dot(
            grad_logits, texts, precision=lax.Precision.HIGHEST, preferred_element_type=jnp.float32
        )
        * inv
    )
    text_terms = (
        lax.dot_general(
            grad_logits,
            images,
            (((0,), (0,)), ((), ())),
            precision=lax.Precision.HIGHEST,
            preferred_element_type=jnp.float32,
        )
        * inv
    )
    grad_image = lax.psum_scatter(image_terms, "col", scatter_dimension=1, tiled=True)
    grad_text = lax.psum_scatter(text_terms, "row", scatter_dimension=1, tiled=True)
    return (grad_image, grad_text)


def solution(mesh):
    return jax.shard_map(
        body,
        mesh=mesh,
        in_specs=(P("row", "col"), P("col", "row"), P()),
        out_specs=(P("row", "col"), P("col", "row")),
        check_vma=False,
    )
```

profile of v0, /device:TPU:8, one launch (start us, length us, event | category | flops | bytes accessed | tf_op | source)
XLA Modules:
  0.0 633.2 jit_solution(35640983593023795)
XLA Ops:
  7.2 0.0 all-gather.5.cloned.1.call-start
  7.2 0.7 all-gather.5.cloned.1.call-update
  7.9 0.0 all-gather.3.cloned.1.call-start
  7.9 0.7 all-gather.3.cloned.1.call-update
  8.6 0.0 reduce-scatter.5.cloned.1.call-start
  8.8 0.8 fusion.2
  9.5 0.1 copy.14
  9.7 0.3 broadcast_in_dim.11
  10.0 0.3 copy.24
  10.3 0.6 copy.18
  10.9 44.3 %all-gather.5.cloned.1.call-done = f32[512,512]{0,1:T(8,128)} async-done(((f32[512,32]{0,1:T(8,128)}), f32[512,512]{0,1:T(8,128)}) %all-gather.5.cloned.1.call-update) | async-done | bytes 1048592 | tf_op jit(solution)/shard_map/all_gather | solution.py:14
  55.2 86.6 %all-gather.3.cloned.1.call-done = f32[1024,512]{0,1:T(8,128)} async-done(((f32[1024,16]{0,1:T(8,128)}), f32[1024,512]{0,1:T(8,128)}) %all-gather.3.cloned.1.call-update) | async-done | bytes 2097168 | tf_op jit(solution)/shard_map/all_gather | solution.py:13
  141.8 5.6 fusion.1
  147.4 72.1 %pmax.14 = f32[1024]{0:T(1024)S(1)} all-reduce(f32[1024]{0:T(1024)S(1)} %get-tuple-element.10), channel_id=1, replica_groups=mesh['row'=16,'col'=32] {'col'}, use_global_device_ids=true, to_apply=%region_1.2 | all-reduce | flops 1024 | bytes 8192 | tf_op jit(solution)/shard_map/pmax | solution.py:39
  219.5 1.0 select_reduce_fusion.1
  220.5 69.6 %psum.14 = f32[1024]{0:T(1024)S(1)} all-reduce(f32[1024]{0:T(1024)S(1)} %get-tuple-element.8), channel_id=1, replica_groups=mesh['row'=16,'col'=32] {'col'}, use_global_device_ids=true, to_apply=%region_3.4 | all-reduce | flops 1024 | bytes 8192 | tf_op jit(solution)/shard_map/psum | solution.py:40
  290.1 20.6 %pmax.15 = f32[512]{0:T(512)S(1)} all-reduce(f32[512]{0:T(512)S(1)} %get-tuple-element.9), channel_id=1, replica_groups=mesh['row'=16,'col'=32] {'row'}, use_global_device_ids=true, to_apply=%region_5.6 | all-reduce | flops 512 | bytes 4096 | tf_op jit(solution)/shard_map/pmax | solution.py:43
  310.7 0.6 select_reduce_fusion
  311.3 23.7 %psum.15 = f32[512]{0:T(512)S(1)} all-reduce(f32[512]{0:T(512)S(1)} %select_reduce_fusion), channel_id=1, replica_groups=mesh['row'=16,'col'=32] {'row'}, use_global_device_ids=true, to_apply=%region_7.8 | all-reduce | flops 512 | bytes 4096 | tf_op jit(solution)/shard_map/psum | solution.py:44
  335.0 7.2 %convolution_multiply_fusion.1 = f32[512,512]{0,1:T(8,128)} fusion(f32[1024,512]{0,1:T(8,128)} %all-gather.3.cloned.1.call-done, pred[1024,512]{1,0:T(32,128)(4,1)S(1)} %copy.18, f32[1024,512]{1,0:T(8,128)S(1)} %get-tuple-element.11, s32[512]{0:T(512)S(1)} %iota_add_fusion.1, f32[512]{0:T(512)S(1)} %log_add_fusion.1, f32[1024]{0:T(1024)S(1)} %log_add_fusion, ...), kind=kOutput, calls=%fused_computation.7 | convolution fusion | flops 3226206208 | bytes 5779456 | tf_op jit(solution)/shard_map/dot_general | solution.py:68
  342.2 0.0 reduce-scatter.5.cloned.1.call-update
  342.3 0.0 reduce-scatter.7.cloned.1.call-start
  342.3 7.0 %convolution_multiply_fusion = f32[1024,512]{1,0:T(8,128)} fusion(f32[512,512]{0,1:T(8,128)} %all-gather.5.cloned.1.call-done, pred[1024,512]{1,0:T(32,128)(4,1)S(1)} %copy.18, f32[1024,512]{1,0:T(8,128)S(1)} %get-tuple-element.11, s32[512]{0:T(512)S(1)} %iota_add_fusion.1, f32[512]{0:T(512)S(1)} %log_add_fusion.1, f32[1024]{0:T(1024)S(1)} %log_add_fusion, ...), kind=kOutput, calls=%fused_computation.4 | convolution fusion | flops 3226468352 | bytes 5779456 | tf_op jit(solution)/shard_map/dot_general | solution.py:62
  349.3 2.9 copy.22
  352.2 0.0 reduce-scatter.7.cloned.1.call-update
  352.2 44.7 %reduce-scatter.5.cloned.1.call-done = f32[512,32]{0,1:T(8,128)} async-done(((f32[512,512]{0,1:T(8,128)}), f32[512,32]{0,1:T(8,128)}) %reduce-scatter.5.cloned.1.call-update) | async-done | bytes 65552 | tf_op jit(solution)/shard_map/reduce_scatter | solution.py:78
  396.9 229.8 %reduce-scatter.7.cloned.1.call-done = f32[16,1024]{1,0:T(8,128)} async-done(((f32[512,1024]{1,0:T(8,128)}), f32[16,1024]{1,0:T(8,128)}) %reduce-scatter.7.cloned.1.call-update) | async-done | bytes 65552
  (6 shorter events, 0.0 us)
Async XLA Ops:
  7.2 48.1 %all-gather.5.cloned.1.call-start = ((), (), s32[]{:S(2)}) async-start(), calls=%async_computation.3 | async-start | bytes 1114112 | tf_op jit(solution)/shard_map/all_gather | solution.py:14
  7.9 133.9 %all-gather.3.cloned.1.call-start = ((), (), s32[]{:S(2)}) async-start(), calls=%async_computation.2 | async-start | bytes 2162688 | tf_op jit(solution)/shard_map/all_gather | solution.py:13
  8.6 388.3 %reduce-scatter.5.cloned.1.call-start = ((), (), s32[]{:S(2)}) async-start(), calls=%async_computation.4 | async-start | bytes 1114112 | tf_op jit(solution)/shard_map/reduce_scatter | solution.py:78
  342.3 284.4 %reduce-scatter.7.cloned.1.call-start = ((), (), s32[]{:S(2)}) async-start(), calls=%async_computation.5 | async-start | bytes 2162688
Sparse Core Ops, SparseCore 0:
  10.1 45.0 all-gather.4
  58.4 83.3 all-gather.2
  342.4 54.4 reduce-scatter.4
  402.4 224.2 reduce-scatter.6
where the time goes:
time: 634 us; the launch traced here: 633 us
  waiting for transfers between devices  407 us (64%)
  blocking collectives  186 us (29%)
  matrix products  19.8 us (3%)
  between operations  13.9 us (2%)
    unnamed x5, waiting for transfers between devices  231 us
    all_gather x1, waiting for transfers between devices, body(): images = lax.all_gather(image_embeddings, 'col', axis=1, tiled=True)  86.6 us
    pmax x1, blocking collectives, body(): row_max = lax.pmax(jnp.max(masked, axis=1), 'col')  72.1 us
    psum x1, blocking collectives, body(): lax.psum(jnp.sum(jnp.where(allowed, jnp.exp(logits - row_max[:, None]), 0...  69.6 us
    reduce_scatter x1, waiting for transfers between devices, body(): lax.psum_scatter(text_terms, 'row', scatter_dimension=1, tiled=True)  44.7 us
    all_gather x1, waiting for transfers between devices, body(): texts = lax.all_gather(text_embeddings, 'row', axis=1, tiled=True)  44.3 us
    psum x1, blocking collectives, body(): lax.psum(jnp.sum(jnp.where(allowed, jnp.exp(logits - col_max[None, :]), 0...  23.7 us
    pmax x1, blocking collectives, body(): col_max = lax.pmax(jnp.max(masked, axis=0), 'row')  20.6 us
  transfers between devices with their start and end apart: 4, of which 4 were waited for; matrix products, arithmetic and copies ran while one was open for 2% of the time, Pallas kernels for 0%

commit v1 on v0

v1 whole, which is shorter than its diff:
```python
import jax
import jax.numpy as jnp
from jax import lax
from jax.sharding import Mesh
from jax.sharding import PartitionSpec as P

BLK = 256
NEG = -1e30
ROW = ("y", "core")
COL = ("x", "z")


def gather(block, axis, n):
    copies = jnp.broadcast_to(block[None], (n,) + block.shape)
    got = lax.all_to_all(copies, axis, 0, 0)
    return got.reshape((n * block.shape[0],) + block.shape[1:])


def scatter_sum(terms, axis, n):
    parts = terms.reshape((n, terms.shape[0] // n) + terms.shape[1:])
    return jnp.sum(lax.all_to_all(parts, axis, 0, 0), axis=0)


def total_lse(local, axis, n):
    every = gather(local[None], axis, n)
    top = jnp.max(every, axis=0)
    return top + jnp.log(jnp.sum(jnp.exp(every - top[None]), axis=0))


def body(image_embeddings, text_embeddings, negatives_mask):
    ny, nc, nx, nz = (lax.axis_size(a) for a in ("y", "core", "x", "z"))
    texts = lax.all_gather(text_embeddings.T, ROW, axis=0, tiled=True)
    images = gather(gather(image_embeddings.T, "z", nz), "x", nx)
    rows = images.shape[1]
    cols = texts.shape[1]
    inv = images.shape[0] ** (-0.5)
    row_start = lax.axis_index(ROW) * rows
    col_start = lax.axis_index(COL) * cols
    logits = (
        lax.dot_general(
            images,
            texts,
            (((0,), (0,)), ((), ())),
            precision=lax.Precision.HIGHEST,
            preferred_element_type=jnp.float32,
        )
        * inv
    )
    row_blocks = rows // BLK
    col_blocks = cols // BLK
    first_row = row_start // BLK
    first_col = col_start // BLK
    window = lax.dynamic_slice(negatives_mask, (first_row, first_col), (row_blocks, col_blocks))
    row_ids = first_row + jnp.arange(row_blocks, dtype=jnp.int32)
    col_ids = first_col + jnp.arange(col_blocks, dtype=jnp.int32)
    block_allow = (window > 0) | (row_ids[:, None] == col_ids[None, :])
    allowed = jnp.broadcast_to(
        block_allow[:, None, :, None], (row_blocks, BLK, col_blocks, BLK)
    ).reshape(rows, cols)
    masked = jnp.where(allowed, logits, NEG)

    def local_lse(axis):
        top = jnp.max(masked, axis=axis, keepdims=True)
        total = jnp.sum(jnp.where(allowed, jnp.exp(logits - top), 0.0), axis=axis, keepdims=True)
        return jnp.squeeze(top + jnp.log(jnp.maximum(total, 1e-30)), axis)

    row_lse = total_lse(local_lse(1), COL, nx * nz)
    col_lse = total_lse(local_lse(0), ROW, ny * nc)
    diagonal = (
        (row_start + jnp.arange(rows, dtype=jnp.int32))[:, None]
        == (col_start + jnp.arange(cols, dtype=jnp.int32))[None, :]
    ).astype(jnp.float32)
    grad_logits = (
        jnp.where(
            allowed,
            0.5 * (jnp.exp(logits - row_lse[:, None]) + jnp.exp(logits - col_lse[None, :])),
            0.0,
        )
        - diagonal
    )
    text_terms = (
        lax.dot_general(
            images,
            grad_logits,
            (((1,), (0,)), ((), ())),
            precision=lax.Precision.HIGH,
            preferred_element_type=jnp.float32,
        )
        * inv
    )
    grad_text = lax.psum_scatter(text_terms, ROW, scatter_dimension=0, tiled=True)
    image_terms = (
        lax.dot_general(
            texts,
            grad_logits,
            (((1,), (1,)), ((), ())),
            precision=lax.Precision.HIGH,
            preferred_element_type=jnp.float32,
        )
        * inv
    )
    grad_image = scatter_sum(scatter_sum(image_terms, "x", nx), "z", nz)
    return (grad_image.T, grad_text.T)


def solution(mesh):
    rows, cols = mesh.devices.shape
    fine = Mesh(mesh.devices.reshape(rows // 2, 2, 4, cols // 4), ("y", "core", "x", "z"))
    return jax.shard_map(
        body,
        mesh=fine,
        in_specs=(P(ROW, COL), P(COL, ROW), P()),
        out_specs=(P(ROW, COL), P(COL, ROW)),
        check_vma=False,
    )
```

time: 634 us -> 188 us (0.30)
  the two profiles are of different devices: /device:TPU:8 before, /device:TPU:25 now
where the time goes in v1:
time: 188 us; the launch traced here: 187 us
  waiting for transfers between devices  90.8 us (48%)
  starting transfers between devices  31.2 us (17%)
  blocking collectives  18.5 us (10%)
  matrix products  16.2 us (9%)
  between operations  14.1 us (8%)
  local copies, waits for them, and re-layouts  11.6 us (6%)
  other arithmetic  5.01 us (3%)
    all_to_all x4, waiting for transfers between devices, gather(): got = lax.all_to_all(copies, axis, 0, 0)  34.3 us
    all_to_all x4, starting transfers between devices, gather(): got = lax.all_to_all(copies, axis, 0, 0)  26.5 us
    unnamed x3, waiting for transfers between devices  21.8 us
    all_gather x1, waiting for transfers between devices, body(): texts = lax.all_gather(text_embeddings.T, ROW, axis=0, tiled=True)  20 us
    all_to_all x1, blocking collectives, scatter_sum(): return jnp.sum(lax.all_to_all(parts, axis, 0, 0), axis=0)  18.5 us
    all_to_all x1, waiting for transfers between devices, scatter_sum(): return jnp.sum(lax.all_to_all(parts, axis, 0, 0), axis=0)  14.7 us
    dot_general x1, matrix products, body(): lax.dot_general(images, grad_logits, (((1,), (0,)), ((), ())), precision=...  6.82 us
    dot_general x1, matrix products, body(): lax.dot_general(images, texts, (((0,), (0,)), ((), ())), precision=lax.Pr...  5.59 us
  transfers between devices with their start and end apart: 7, of which 7 were waited for; matrix products, arithmetic and copies ran while one was open for 8% of the time, Pallas kernels for 0%

profile of v1, /device:TPU:25, one launch (start us, length us, event | category | flops | bytes accessed | tf_op | source)
XLA Modules:
  0.0 187.4 jit_solution(1532835417861568190)
XLA Ops:
  7.2 1.7 broadcast_in_dim.22
  8.8 10.0 %all-to-all-start = ((f32[8,16,1024]{2,1,0:T(8,128)}), f32[8,16,1024]{2,1,0:T(8,128)S(1)}, u32[]{:S(2)}, u32[]{:S(2)}) async-start(f32[8,16,1024]{2,1,0:T(8,128)} %broadcast_in_dim.22), calls=%async_computation | async-start | bytes 1048576 | tf_op jit(solution)/shard_map/all_to_all | solution.py:15
  18.9 0.7 all-gather.2.cloned.1.call-update
  19.6 17.2 %all-to-all-done = f32[8,16,1024]{2,1,0:T(8,128)S(1)} async-done(((f32[8,16,1024]{2,1,0:T(8,128)}), f32[8,16,1024]{2,1,0:T(8,128)S(1)}, u32[]{:S(2)}, u32[]{:S(2)}) %all-to-all-start) | async-done | bytes 524320 | tf_op jit(solution)/shard_map/all_to_all | solution.py:15
  36.8 1.6 broadcast_in_dim.24
  38.5 4.0 %all-to-all-start.1 = ((f32[4,128,1024]{2,1,0:T(8,128)}), f32[4,128,1024]{2,1,0:T(8,128)S(1)}, u32[]{:S(2)}, u32[]{:S(2)}) async-start(f32[4,128,1024]{2,1,0:T(8,128)} %broadcast_in_dim.24), calls=%async_computation.1 | async-start | bytes 4194304 | tf_op jit(solution)/shard_map/all_to_all | solution.py:15
  42.5 0.8 fusion.7
  43.4 0.3 broadcast_in_dim.21
  43.7 0.3 copy.65
  44.0 0.6 copy.49
  44.6 20.0 %all-gather.2.cloned.1.call-done = f32[512,512]{1,0:T(8,128)} async-done(((f32[32,512]{1,0:T(8,128)}), f32[512,512]{1,0:T(8,128)}) %all-gather.2.cloned.1.call-update) | async-done | bytes 1048592 | tf_op jit(solution)/shard_map/all_gather | solution.py:32
  64.6 3.5 %all-to-all-done.1 = f32[4,128,1024]{2,1,0:T(8,128)S(1)} async-done(((f32[4,128,1024]{2,1,0:T(8,128)}), f32[4,128,1024]{2,1,0:T(8,128)S(1)}, u32[]{:S(2)}, u32[]{:S(2)}) %all-to-all-start.1) | async-done | bytes 2097184 | tf_op jit(solution)/shard_map/all_to_all | solution.py:15
  68.1 1.3 copy-done
  69.5 5.6 %fusion.1 = (f32[1024]{0:T(1024)S(1)}, f32[1024,512]{1,0:T(8,128)S(1)}) fusion(pred[1024,512]{1,0:T(32,128)(4,1)S(1)} %copy.49, f32[512,1024]{1,0:T(8,128)} %bitcast.38, f32[512,512]{1,0:T(8,128)} %all-gather.2.cloned.1.call-done), kind=kOutput, calls=%fused_computation.7 | convolution fusion | flops 3222797312 | bytes 5771264 | tf_op jit(solution)/shard_map/dot_general | solution.py:40
  75.0 1.0 select_reduce_fusion.1
  76.0 0.6 select_reduce_fusion
  76.6 0.6 broadcast_in_dim.28
  77.2 8.6 %all-to-all-start.3 = ((f32[16,1,512]{2,1,0:T(1,128)}), f32[16,1,512]{2,1,0:T(1,128)S(1)}, u32[]{:S(2)}, u32[]{:S(2)}) async-start(f32[16,1,512]{2,1,0:T(1,128)} %broadcast_in_dim.28), calls=%async_computation.3 | async-start | bytes 65536 | tf_op jit(solution)/shard_map/all_to_all | solution.py:15
  85.9 4.6 %all-to-all-done.3 = f32[16,1,512]{2,1,0:T(1,128)S(1)} async-done(((f32[16,1,512]{2,1,0:T(1,128)}), f32[16,1,512]{2,1,0:T(1,128)S(1)}, u32[]{:S(2)}, u32[]{:S(2)}) %all-to-all-start.3) | async-done | bytes 32800 | tf_op jit(solution)/shard_map/all_to_all | solution.py:15
  90.5 0.7 broadcast_in_dim.27
  91.2 3.9 %all-to-all-start.2 = ((f32[32,1,1024]{2,1,0:T(1,128)}), f32[32,1,1024]{2,1,0:T(1,128)S(1)}, u32[]{:S(2)}, u32[]{:S(2)}) async-start(f32[32,1,1024]{2,1,0:T(1,128)} %broadcast_in_dim.27), calls=%async_computation.2 | async-start | bytes 262144 | tf_op jit(solution)/shard_map/all_to_all | solution.py:15
  95.1 9.1 %all-to-all-done.2 = f32[32,1,1024]{2,1,0:T(1,128)S(1)} async-done(((f32[32,1,1024]{2,1,0:T(1,128)}), f32[32,1,1024]{2,1,0:T(1,128)S(1)}, u32[]{:S(2)}, u32[]{:S(2)}) %all-to-all-start.2) | async-done | bytes 131104 | tf_op jit(solution)/shard_map/all_to_all | solution.py:15
  104.3 3.7 %multiply_bitcast_fusion = f32[128,4,8,128]{3,2,1,0:T(8,128)S(1)} fusion(f32[512,512]{1,0:T(8,128)} %all-gather.2.cloned.1.call-done, pred[1024,512]{1,0:T(32,128)(4,1)S(1)} %copy.49, f32[1024,512]{1,0:T(8,128)S(1)} %get-tuple-element.17, s32[512]{0:T(512)S(1)} %iota_add_fusion.1, f32[512]{0:T(512)S(1)} %log_add_fusion.2, f32[1024]{0:T(1024)S(1)} %log_add_fusion, ...), kind=kOutput, calls=%fused_computation.1 | convolution fusion | flops 1615855616 | bytes 5779456 | tf_op jit(solution)/shard_map/dot_general | solution.py:93
  108.1 1.5 copy.69
  109.6 4.4 %all-to-all-start.4 = ((f32[4,128,1024]{1,2,0:T(8,128)}), f32[4,128,1024]{1,2,0:T(8,128)}, u32[]{:S(2)}, u32[]{:S(2)}) async-start(f32[4,128,1024]{1,2,0:T(8,128)} %bitcast.40), calls=%async_computation.4 | async-start | bytes 4194304 | tf_op jit(solution)/shard_map/all_to_all | solution.py:21
  114.2 6.8 %fusion.2 = f32[512,512]{0,1:T(8,128)} fusion(f32[512,1024]{1,0:T(8,128)} %bitcast.39, pred[1024,512]{1,0:T(32,128)(4,1)S(1)} %copy.49, f32[1024,512]{1,0:T(8,128)S(1)} %get-tuple-element.17, s32[512]{0:T(512)S(1)} %iota_add_fusion.1, f32[512]{0:T(512)S(1)} %log_add_fusion.2, f32[1024]{0:T(1024)S(1)} %log_add_fusion, s32[1024]{0:T(1024)S(1)} %iota_add_fusion), kind=kOutput, calls=%fused_computation.9 | convolution fusion | flops 1615593472 | bytes 5779456 | tf_op jit(solution)/shard_map/dot_general | solution.py:82
  121.1 2.5 %copy.56 = f32[512,512]{1,0:T(8,128)} copy(f32[512,512]{0,1:T(8,128)} %fusion.2) | data formatting | bytes 2097152
  123.6 14.7 %all-to-all-done.4 = f32[4,128,1024]{1,2,0:T(8,128)} async-done(((f32[4,128,1024]{1,2,0:T(8,128)}), f32[4,128,1024]{1,2,0:T(8,128)}, u32[]{:S(2)}, u32[]{:S(2)}) %all-to-all-start.4) | async-done | bytes 2097184 | tf_op jit(solution)/shard_map/all_to_all | solution.py:21
  138.3 1.8 reduce_sum.58
  140.3 18.5 %all_to_all.30 = f32[8,16,1024]{2,1,0:T(8,128)S(1)} all-to-all(f32[8,16,1024]{2,1,0:T(8,128)S(1)} %bitcast.44), channel_id=1, replica_groups=mesh['y'=8,'core'=2,'x'=4,'z'=8] {'z'}, dimensions={0} | all-to-all | bytes 1048576 | tf_op jit(solution)/shard_map/all_to_all | solution.py:21
  158.8 0.7 reduce_sum.59
  159.5 21.1 %reduce-scatter.4.cloned.1.call-done = f32[32,512]{1,0:T(8,128)} async-done(((f32[512,512]{1,0:T(8,128)}), f32[32,512]{1,0:T(8,128)}) %reduce-scatter.4.cloned.1.call-update) | async-done | bytes 65552
  (18 shorter events, 0.8 us)
Async XLA Ops:
  8.8 28.0 %all-to-all-start = ((f32[8,16,1024]{2,1,0:T(8,128)}), f32[8,16,1024]{2,1,0:T(8,128)S(1)}, u32[]{:S(2)}, u32[]{:S(2)}) async-start(f32[8,16,1024]{2,1,0:T(8,128)} %broadcast_in_dim.22), calls=%async_computation | async-start | bytes 1048576 | tf_op jit(solution)/shard_map/all_to_all | solution.py:15
  18.9 45.7 %all-gather.2.cloned.1.call-start = ((), (), s32[]{:S(2)}) async-start(), calls=%async_computation.7 | async-start | bytes 1114112 | tf_op jit(solution)/shard_map/all_gather | solution.py:32
  38.5 29.6 %all-to-all-start.1 = ((f32[4,128,1024]{2,1,0:T(8,128)}), f32[4,128,1024]{2,1,0:T(8,128)S(1)}, u32[]{:S(2)}, u32[]{:S(2)}) async-start(f32[4,128,1024]{2,1,0:T(8,128)} %broadcast_in_dim.24), calls=%async_computation.1 | async-start | bytes 4194304 | tf_op jit(solution)/shard_map/all_to_all | solution.py:15
  68.1 1.4 copy-start
  77.2 13.2 %all-to-all-start.3 = ((f32[16,1,512]{2,1,0:T(1,128)}), f32[16,1,512]{2,1,0:T(1,128)S(1)}, u32[]{:S(2)}, u32[]{:S(2)}) async-start(f32[16,1,512]{2,1,0:T(1,128)} %broadcast_in_dim.28), calls=%async_computation.3 | async-start | bytes 65536 | tf_op jit(solution)/shard_map/all_to_all | solution.py:15
  91.2 13.0 %all-to-all-start.2 = ((f32[32,1,1024]{2,1,0:T(1,128)}), f32[32,1,1024]{2,1,0:T(1,128)S(1)}, u32[]{:S(2)}, u32[]{:S(2)}) async-start(f32[32,1,1024]{2,1,0:T(1,128)} %broadcast_in_dim.27), calls=%async_computation.2 | async-start | bytes 262144 | tf_op jit(solution)/shard_map/all_to_all | solution.py:15
  109.6 28.8 %all-to-all-start.4 = ((f32[4,128,1024]{1,2,0:T(8,128)}), f32[4,128,1024]{1,2,0:T(8,128)}, u32[]{:S(2)}, u32[]{:S(2)}) async-start(f32[4,128,1024]{1,2,0:T(8,128)} %bitcast.40), calls=%async_computation.4 | async-start | bytes 4194304 | tf_op jit(solution)/shard_map/all_to_all | solution.py:21
  114.0 66.6 %reduce-scatter.4.cloned.1.call-start = ((), (), s32[]{:S(2)}) async-start(), calls=%async_computation.8 | async-start | bytes 1114112
Sparse Core Ops, SparseCore 0:
  21.8 42.7 all-gather.1
  123.8 56.8 reduce-scatter.3

commit v2 on v1

--- a/solution.py
+++ b/solution.py
@@ -21,6 +21,23 @@
     return jnp.sum(lax.all_to_all(parts, axis, 0, 0), axis=0)
 
 
+def flip(axis, n, bit):
+    return [(i, i ^ bit) for i in range(n)]
+
+
+def pair_gather(block, axis, n, bit, dim):
+    other = lax.ppermute(block, axis, flip(axis, n, bit))
+    low = (lax.axis_index(axis) & bit) == 0
+    return jnp.stack([jnp.where(low, block, other), jnp.where(low, other, block)], axis=dim)
+
+
+def pair_sum(terms, axis, n, bit, dim):
+    mine = jnp.where((lax.axis_index(axis) & bit) == 0, 0, 1)
+    send = lax.dynamic_index_in_dim(terms, 1 - mine, dim, keepdims=False)
+    keep = lax.dynamic_index_in_dim(terms, mine, dim, keepdims=False)
+    return keep + lax.ppermute(send, axis, flip(axis, n, bit))
+
+
 def total_lse(local, axis, n):
     every = gather(local[None], axis, n)
     top = jnp.max(every, axis=0)
@@ -29,7 +46,12 @@
 
 def body(image_embeddings, text_embeddings, negatives_mask):
     ny, nc, nx, nz = (lax.axis_size(a) for a in ("y", "core", "x", "z"))
-    texts = lax.all_gather(text_embeddings.T, ROW, axis=0, tiled=True)
+    texts = text_embeddings.T
+    bits = [1 << b for b in reversed(range(ny.bit_length() - 1))]
+    for dim, bit in enumerate(bits):
+        texts = pair_gather(texts, "y", ny, bit, dim)
+    texts = pair_gather(texts, "core", nc, 1, len(bits))
+    texts = texts.reshape(-1, texts.shape[-1])
     images = gather(gather(image_embeddings.T, "z", nz), "x", nx)
     rows = images.shape[1]
     cols = texts.shape[1]
@@ -88,7 +110,10 @@
         )
         * inv
     )
-    grad_text = lax.psum_scatter(text_terms, ROW, scatter_dimension=0, tiled=True)
+    grad_text = text_terms.reshape((2,) * (len(bits) + 1) + (-1, cols))
+    grad_text = pair_sum(grad_text, "core", nc, 1, len(bits))
+    for dim, bit in reversed(list(enumerate(bits))):
+        grad_text = pair_sum(grad_text, "y", ny, bit, dim)
     image_terms = (
         lax.dot_general(
             texts,

time: 188 us -> 167 us (0.89)
  the two profiles are of different devices: /device:TPU:25 before, /device:TPU:64 now
where the time goes in v2:
time: 167 us; the launch traced here: 166 us
  waiting for transfers between devices  74.1 us (44%)
  starting transfers between devices  58.4 us (35%)
  matrix products  15.3 us (9%)
  other arithmetic  10.7 us (6%)
  local copies, waits for them, and re-layouts  6.92 us (4%)
    all_to_all x4, waiting for transfers between devices, gather(): got = lax.all_to_all(copies, axis, 0, 0)  36.2 us
    all_to_all x4, starting transfers between devices, gather(): got = lax.all_to_all(copies, axis, 0, 0)  25.7 us
    ppermute x4, waiting for transfers between devices, pair_sum(): return keep + lax.ppermute(send, axis, flip(axis, n, bit))  15.9 us
    ppermute x4, starting transfers between devices, pair_gather(): other = lax.ppermute(block, axis, flip(axis, n, bit))  14.3 us
    all_to_all x2, waiting for transfers between devices, scatter_sum(): return jnp.sum(lax.all_to_all(parts, axis, 0, 0), axis=0)  14.1 us
    ppermute x4, starting transfers between devices, pair_sum(): return keep + lax.ppermute(send, axis, flip(axis, n, bit))  9.5 us
    all_to_all x2, starting transfers between devices, scatter_sum(): return jnp.sum(lax.all_to_all(parts, axis, 0, 0), axis=0)  8.89 us
    ppermute x4, waiting for transfers between devices, pair_gather(): other = lax.ppermute(block, axis, flip(axis, n, bit))  7.96 us
  transfers between devices with their start and end apart: 14, of which 10 were waited for; matrix products, arithmetic and copies ran while one was open for 10% of the time, Pallas kernels for 0%

profile of v2, /device:TPU:64, one launch (start us, length us, event | category | flops | bytes accessed | tf_op | source)
XLA Modules:
  0.0 166.4 jit_solution(3947738316093689794)
XLA Ops:
  0.6 7.7 %collective-permute-start = (f32[32,512]{1,0:T(8,128)}, f32[32,512]{1,0:T(8,128)S(1)}, u32[]{:S(2)}, u32[]{:S(2)}) collective-permute-start(f32[32,512]{1,0:T(8,128)} %bitcast.130), channel_id=1, source_target_pairs={{0,256},{64,320},{128,384},{192,448},{256,0},{320,64},{384,128},{4... | collective-permute-start | bytes 196616 | tf_op jit(solution)/shard_map/ppermute | solution.py:29
  8.4 1.7 %broadcast_in_dim.22 = f32[8,16,1024]{2,1,0:T(8,128)} broadcast(f32[16,1024]{1,0:T(8,128)} %bitcast.129), dimensions={1,2} | broadcast | bytes 589824 | tf_op jit(solution)/shard_map/broadcast_in_dim | solution.py:14
  10.1 10.0 %all-to-all-start = ((f32[8,16,1024]{2,1,0:T(8,128)}), f32[8,16,1024]{2,1,0:T(8,128)S(1)}, u32[]{:S(2)}, u32[]{:S(2)}) async-start(f32[8,16,1024]{2,1,0:T(8,128)} %broadcast_in_dim.22), calls=%async_computation | async-start | bytes 1048576 | tf_op jit(solution)/shard_map/all_to_all | solution.py:15
  20.9 2.7 %collective-permute-start.1 = (f32[2,32,512]{2,1,0:T(8,128)S(1)}, f32[2,32,512]{2,1,0:T(8,128)S(1)}, u32[]{:S(2)}, u32[]{:S(2)}) collective-permute-start(f32[2,32,512]{2,1,0:T(8,128)S(1)} %pad_maximum_fusion.3), channel_id=1, source_target_pairs={{0,128},{64,192},{128,0},{192,64},{256,384},{320,448},{384,256},{4... | collective-permute-start | bytes 393224 | tf_op jit(solution)/shard_map/ppermute | solution.py:29
  23.6 7.3 %collective-permute-done.1 = f32[2,32,512]{2,1,0:T(8,128)S(1)} collective-permute-done((f32[2,32,512]{2,1,0:T(8,128)S(1)}, f32[2,32,512]{2,1,0:T(8,128)S(1)}, u32[]{:S(2)}, u32[]{:S(2)}) %collective-permute-start.1) | collective-permute-done | bytes 131104 | tf_op jit(solution)/shard_map/ppermute | solution.py:29
  30.9 1.9 %collective-permute-start.2 = (f32[2,2,32,512]{3,2,1,0:T(8,128)S(1)}, f32[2,2,32,512]{3,2,1,0:T(8,128)S(1)}, u32[]{:S(2)}, u32[]{:S(2)}) collective-permute-start(f32[2,2,32,512]{3,2,1,0:T(8,128)S(1)} %pad_maximum_fusion.2), channel_id=1, source_target_pairs={{0,64},{64,0},{128,192},{192,128},{256,320},{320,256},{384,448},{4... | collective-permute-start | bytes 786440 | tf_op jit(solution)/shard_map/ppermute | solution.py:29
  32.9 2.9 %all-to-all-done = f32[8,16,1024]{2,1,0:T(8,128)S(1)} async-done(((f32[8,16,1024]{2,1,0:T(8,128)}), f32[8,16,1024]{2,1,0:T(8,128)S(1)}, u32[]{:S(2)}, u32[]{:S(2)}) %all-to-all-start) | async-done | bytes 524320 | tf_op jit(solution)/shard_map/all_to_all | solution.py:15
  35.8 1.6 broadcast_in_dim.24
  37.4 4.3 %all-to-all-start.1 = ((f32[4,128,1024]{2,1,0:T(8,128)}), f32[4,128,1024]{2,1,0:T(8,128)S(1)}, u32[]{:S(2)}, u32[]{:S(2)}) async-start(f32[4,128,1024]{2,1,0:T(8,128)} %broadcast_in_dim.24), calls=%async_computation.1 | async-start | bytes 4194304 | tf_op jit(solution)/shard_map/all_to_all | solution.py:15
  42.6 1.9 %collective-permute-start.3 = (f32[2,2,2,32,512]{4,3,2,1,0:T(8,128)}, f32[2,2,2,32,512]{4,3,2,1,0:T(8,128)}, u32[]{:S(2)}, u32[]{:S(2)}) collective-permute-start(f32[2,2,2,32,512]{4,3,2,1,0:T(8,128)} %pad_maximum_fusion.1), channel_id=1, source_target_pairs={{0,32},{32,0},{1,33},{33,1},{2,34},{34,2},{3,35},{35,3},{4,36},{36... | collective-permute-start | bytes 1572872 | tf_op jit(solution)/shard_map/ppermute | solution.py:29
  46.8 1.2 select_bitcast_fusion.1
  47.9 1.1 pad_maximum_fusion
  49.0 15.7 %all-to-all-done.1 = f32[4,128,1024]{2,1,0:T(8,128)S(1)} async-done(((f32[4,128,1024]{2,1,0:T(8,128)}), f32[4,128,1024]{2,1,0:T(8,128)S(1)}, u32[]{:S(2)}, u32[]{:S(2)}) %all-to-all-start.1) | async-done | bytes 2097184 | tf_op jit(solution)/shard_map/all_to_all | solution.py:15
  64.8 1.3 copy-done
  66.1 5.6 %fusion.13 = (f32[1024]{0:T(1024)S(1)}, f32[512,1024]{1,0:T(8,128)S(1)}) fusion(pred[1024,512]{0,1:T(8,128)(4,1)S(1)} %bitcast.115, f32[512,512]{1,0:T(8,128)} %bitcast.122, f32[512,1024]{1,0:T(8,128)} %bitcast.120), kind=kOutput, calls=%fused_computation.19 | convolution fusion | flops 3222797312 | bytes 5771264 | tf_op jit(solution)/shard_map/dot_general | solution.py:62
  74.0 3.5 %all-to-all-start.3 = ((f32[16,1,512]{2,1,0:T(1,128)}), f32[16,1,512]{2,1,0:T(1,128)S(1)}, u32[]{:S(2)}, u32[]{:S(2)}) async-start(f32[16,1,512]{2,1,0:T(1,128)} %broadcast_in_dim.28), calls=%async_computation.3 | async-start | bytes 65536 | tf_op jit(solution)/shard_map/all_to_all | solution.py:15
  77.5 7.6 %all-to-all-done.3 = f32[16,1,512]{2,1,0:T(1,128)S(1)} async-done(((f32[16,1,512]{2,1,0:T(1,128)}), f32[16,1,512]{2,1,0:T(1,128)S(1)}, u32[]{:S(2)}, u32[]{:S(2)}) %all-to-all-start.3) | async-done | bytes 32800 | tf_op jit(solution)/shard_map/all_to_all | solution.py:15
  85.9 8.0 %all-to-all-start.2 = ((f32[32,1,1024]{2,1,0:T(1,128)}), f32[32,1,1024]{2,1,0:T(1,128)S(1)}, u32[]{:S(2)}, u32[]{:S(2)}) async-start(f32[32,1,1024]{2,1,0:T(1,128)} %broadcast_in_dim.27), calls=%async_computation.2 | async-start | bytes 262144 | tf_op jit(solution)/shard_map/all_to_all | solution.py:15
  93.9 9.9 %all-to-all-done.2 = f32[32,1,1024]{2,1,0:T(1,128)S(1)} async-done(((f32[32,1,1024]{2,1,0:T(1,128)}), f32[32,1,1024]{2,1,0:T(1,128)S(1)}, u32[]{:S(2)}, u32[]{:S(2)}) %all-to-all-start.2) | async-done | bytes 131104 | tf_op jit(solution)/shard_map/all_to_all | solution.py:15
  104.0 5.3 %convolution_multiply_fusion = f32[512,1024]{1,0:T(8,128)} fusion(f32[512,512]{1,0:T(8,128)} %bitcast.123, pred[1024,512]{0,1:T(8,128)(4,1)S(1)} %bitcast.118, f32[512,1024]{1,0:T(8,128)S(1)} %get-tuple-element.15, s32[1024]{0:T(1024)S(1)} %iota_add_fusion, f32[512]{0:T(512)S(1)} %log_add_fusion.2, f32[1024]{0:T(1024)S(1)} %log_add_fusion, ...), kind=kOutput, calls=%fused_computation.17 | convolution fusion | flops 1615855616 | bytes 5779456 | tf_op jit(solution)/shard_map/dot_general | solution.py:118
  109.3 4.6 %all-to-all-start.4 = ((f32[4,128,1024]{2,1,0:T(8,128)}), f32[4,128,1024]{2,1,0:T(8,128)}, u32[]{:S(2)}, u32[]{:S(2)}) async-start(f32[4,128,1024]{2,1,0:T(8,128)} %bitcast.125), calls=%async_computation.4 | async-start | bytes 4194304 | tf_op jit(solution)/shard_map/all_to_all | solution.py:21
  113.9 4.4 %convolution_multiply_fusion.1 = f32[512,512]{0,1:T(8,128)S(1)} fusion(f32[512,1024]{1,0:T(8,128)} %bitcast.121, pred[1024,512]{0,1:T(8,128)(4,1)S(1)} %bitcast.119, f32[512,1024]{1,0:T(8,128)S(1)} %get-tuple-element.15, s32[1024]{0:T(1024)S(1)} %iota_add_fusion, f32[512]{0:T(512)S(1)} %log_add_fusion.2, f32[1024]{0:T(1024)S(1)} %log_add_fusion, ...), kind=kOutput, calls=%fused_computation.20 | convolution fusion | flops 1615593472 | bytes 5779456 | tf_op jit(solution)/shard_map/dot_general | solution.py:104
  118.5 1.9 %collective-permute-start.4 = (f32[2,2,2,32,512]{4,3,1,0,2:T(8,128)S(1)}, f32[2,2,2,32,512]{4,3,1,0,2:T(8,128)S(1)}, u32[]{:S(2)}, u32[]{:S(2)}) collective-permute-start(f32[2,2,2,32,512]{4,3,1,0,2:T(8,128)S(1)} %bitcast.128), channel_id=1, source_target_pairs={{0,32},{32,0},{1,33},{33,1},{2,34},{34,2},{3,35},{35,3},{4,36},{36... | collective-permute-start | bytes 1572872 | tf_op jit(solution)/shard_map/ppermute | solution.py:38
  120.4 1.9 %collective-permute-done.4 = f32[2,2,2,32,512]{4,3,1,0,2:T(8,128)S(1)} collective-permute-done((f32[2,2,2,32,512]{4,3,1,0,2:T(8,128)S(1)}, f32[2,2,2,32,512]{4,3,1,0,2:T(8,128)S(1)}, u32[]{:S(2)}, u32[]{:S(2)}) %collective-permute-start.4) | collective-permute-done | bytes 524320 | tf_op jit(solution)/shard_map/ppermute | solution.py:38
  122.4 2.4 %collective-permute-start.5 = (f32[2,2,32,512]{3,2,1,0:T(8,128)S(1)}, f32[2,2,32,512]{3,2,1,0:T(8,128)S(1)}, u32[]{:S(2)}, u32[]{:S(2)}) collective-permute-start(f32[2,2,32,512]{3,2,1,0:T(8,128)S(1)} %dynamic-slice_bitcast_fusion), channel_id=1, source_target_pairs={{0,64},{64,0},{128,192},{192,128},{256,320},{320,256},{384,448},{4... | collective-permute-start | bytes 786440 | tf_op jit(solution)/shard_map/ppermute | solution.py:38
  124.8 14.1 %all-to-all-done.4 = f32[4,128,1024]{2,1,0:T(8,128)} async-done(((f32[4,128,1024]{2,1,0:T(8,128)}), f32[4,128,1024]{2,1,0:T(8,128)}, u32[]{:S(2)}, u32[]{:S(2)}) %all-to-all-start.4) | async-done | bytes 2097184 | tf_op jit(solution)/shard_map/all_to_all | solution.py:21
  139.0 2.6 %reduce_sum.58 = f32[128,1024]{1,0:T(8,128)} reduce(f32[4,128,1024]{2,1,0:T(8,128)} %all-to-all-done.4, f32[]{:T(128)} %constant.99.clone.1), dimensions={0}, to_apply=%region_8.9 | reduce | flops 393216 | bytes 2621444 | tf_op jit(solution)/shard_map/reduce_sum | solution.py:21
  141.5 4.3 %all-to-all-start.5 = ((f32[8,16,1024]{2,1,0:T(8,128)}), f32[8,16,1024]{2,1,0:T(8,128)S(1)}, u32[]{:S(2)}, u32[]{:S(2)}) async-start(f32[8,16,1024]{2,1,0:T(8,128)} %bitcast.18), calls=%async_computation.5 | async-start | bytes 1048576 | tf_op jit(solution)/shard_map/all_to_all | solution.py:21
  145.9 2.5 %collective-permute-start.6 = (f32[2,32,512]{2,1,0:T(8,128)S(1)}, f32[2,32,512]{2,1,0:T(8,128)S(1)}, u32[]{:S(2)}, u32[]{:S(2)}) collective-permute-start(f32[2,32,512]{2,1,0:T(8,128)S(1)} %dynamic-slice_bitcast_fusion.1), channel_id=1, source_target_pairs={{0,128},{64,192},{128,0},{192,64},{256,384},{320,448},{384,256},{4... | collective-permute-start | bytes 393224 | tf_op jit(solution)/shard_map/ppermute | solution.py:38
  148.4 6.6 %collective-permute-done.6 = f32[2,32,512]{2,1,0:T(8,128)S(1)} collective-permute-done((f32[2,32,512]{2,1,0:T(8,128)S(1)}, f32[2,32,512]{2,1,0:T(8,128)S(1)}, u32[]{:S(2)}, u32[]{:S(2)}) %collective-permute-start.6) | collective-permute-done | bytes 131104 | tf_op jit(solution)/shard_map/ppermute | solution.py:38
  155.0 2.7 %collective-permute-start.7 = (f32[32,512]{1,0:T(8,128)S(1)}, f32[32,512]{1,0:T(8,128)S(1)}, u32[]{:S(2)}, u32[]{:S(2)}) collective-permute-start(f32[32,512]{1,0:T(8,128)S(1)} %dynamic-slice_bitcast_fusion.2), channel_id=1, source_target_pairs={{0,256},{64,320},{128,384},{192,448},{256,0},{320,64},{384,128},{4... | collective-permute-start | bytes 196616 | tf_op jit(solution)/shard_map/ppermute | solution.py:38
  157.7 7.4 %collective-permute-done.7 = f32[32,512]{1,0:T(8,128)S(1)} collective-permute-done((f32[32,512]{1,0:T(8,128)S(1)}, f32[32,512]{1,0:T(8,128)S(1)}, u32[]{:S(2)}, u32[]{:S(2)}) %collective-permute-start.7) | collective-permute-done | bytes 65568 | tf_op jit(solution)/shard_map/ppermute | solution.py:38
  (42 shorter events, 8.8 us)
Async XLA Ops:
  0.6 19.4 %collective-permute-start = (f32[32,512]{1,0:T(8,128)}, f32[32,512]{1,0:T(8,128)S(1)}, u32[]{:S(2)}, u32[]{:S(2)}) collective-permute-start(f32[32,512]{1,0:T(8,128)} %bitcast.130), channel_id=1, source_target_pairs={{0,256},{64,320},{128,384},{192,448},{256,0},{320,64},{384,128},{4... | collective-permute-start | bytes 196616 | tf_op jit(solution)/shard_map/ppermute | solution.py:29
  10.1 25.7 %all-to-all-start = ((f32[8,16,1024]{2,1,0:T(8,128)}), f32[8,16,1024]{2,1,0:T(8,128)S(1)}, u32[]{:S(2)}, u32[]{:S(2)}) async-start(f32[8,16,1024]{2,1,0:T(8,128)} %broadcast_in_dim.22), calls=%async_computation | async-start | bytes 1048576 | tf_op jit(solution)/shard_map/all_to_all | solution.py:15
  20.9 10.0 %collective-permute-start.1 = (f32[2,32,512]{2,1,0:T(8,128)S(1)}, f32[2,32,512]{2,1,0:T(8,128)S(1)}, u32[]{:S(2)}, u32[]{:S(2)}) collective-permute-start(f32[2,32,512]{2,1,0:T(8,128)S(1)} %pad_maximum_fusion.3), channel_id=1, source_target_pairs={{0,128},{64,192},{128,0},{192,64},{256,384},{320,448},{384,256},{4... | collective-permute-start | bytes 393224 | tf_op jit(solution)/shard_map/ppermute | solution.py:29
  30.9 10.8 %collective-permute-start.2 = (f32[2,2,32,512]{3,2,1,0:T(8,128)S(1)}, f32[2,2,32,512]{3,2,1,0:T(8,128)S(1)}, u32[]{:S(2)}, u32[]{:S(2)}) collective-permute-start(f32[2,2,32,512]{3,2,1,0:T(8,128)S(1)} %pad_maximum_fusion.2), channel_id=1, source_target_pairs={{0,64},{64,0},{128,192},{192,128},{256,320},{320,256},{384,448},{4... | collective-permute-start | bytes 786440 | tf_op jit(solution)/shard_map/ppermute | solution.py:29
  37.4 27.4 %all-to-all-start.1 = ((f32[4,128,1024]{2,1,0:T(8,128)}), f32[4,128,1024]{2,1,0:T(8,128)S(1)}, u32[]{:S(2)}, u32[]{:S(2)}) async-start(f32[4,128,1024]{2,1,0:T(8,128)} %broadcast_in_dim.24), calls=%async_computation.1 | async-start | bytes 4194304 | tf_op jit(solution)/shard_map/all_to_all | solution.py:15
  42.6 4.1 %collective-permute-start.3 = (f32[2,2,2,32,512]{4,3,2,1,0:T(8,128)}, f32[2,2,2,32,512]{4,3,2,1,0:T(8,128)}, u32[]{:S(2)}, u32[]{:S(2)}) collective-permute-start(f32[2,2,2,32,512]{4,3,2,1,0:T(8,128)} %pad_maximum_fusion.1), channel_id=1, source_target_pairs={{0,32},{32,0},{1,33},{33,1},{2,34},{34,2},{3,35},{35,3},{4,36},{36... | collective-permute-start | bytes 1572872 | tf_op jit(solution)/shard_map/ppermute | solution.py:29
  64.8 1.4 copy-start
  74.0 11.2 %all-to-all-start.3 = ((f32[16,1,512]{2,1,0:T(1,128)}), f32[16,1,512]{2,1,0:T(1,128)S(1)}, u32[]{:S(2)}, u32[]{:S(2)}) async-start(f32[16,1,512]{2,1,0:T(1,128)} %broadcast_in_dim.28), calls=%async_computation.3 | async-start | bytes 65536 | tf_op jit(solution)/shard_map/all_to_all | solution.py:15
  85.9 18.0 %all-to-all-start.2 = ((f32[32,1,1024]{2,1,0:T(1,128)}), f32[32,1,1024]{2,1,0:T(1,128)S(1)}, u32[]{:S(2)}, u32[]{:S(2)}) async-start(f32[32,1,1024]{2,1,0:T(1,128)} %broadcast_in_dim.27), calls=%async_computation.2 | async-start | bytes 262144 | tf_op jit(solution)/shard_map/all_to_all | solution.py:15
  109.3 29.7 %all-to-all-start.4 = ((f32[4,128,1024]{2,1,0:T(8,128)}), f32[4,128,1024]{2,1,0:T(8,128)}, u32[]{:S(2)}, u32[]{:S(2)}) async-start(f32[4,128,1024]{2,1,0:T(8,128)} %bitcast.125), calls=%async_computation.4 | async-start | bytes 4194304 | tf_op jit(solution)/shard_map/all_to_all | solution.py:21
  118.5 3.8 %collective-permute-start.4 = (f32[2,2,2,32,512]{4,3,1,0,2:T(8,128)S(1)}, f32[2,2,2,32,512]{4,3,1,0,2:T(8,128)S(1)}, u32[]{:S(2)}, u32[]{:S(2)}) collective-permute-start(f32[2,2,2,32,512]{4,3,1,0,2:T(8,128)S(1)} %bitcast.128), channel_id=1, source_target_pairs={{0,32},{32,0},{1,33},{33,1},{2,34},{34,2},{3,35},{35,3},{4,36},{36... | collective-permute-start | bytes 1572872 | tf_op jit(solution)/shard_map/ppermute | solution.py:38
  122.4 23.4 %collective-permute-start.5 = (f32[2,2,32,512]{3,2,1,0:T(8,128)S(1)}, f32[2,2,32,512]{3,2,1,0:T(8,128)S(1)}, u32[]{:S(2)}, u32[]{:S(2)}) collective-permute-start(f32[2,2,32,512]{3,2,1,0:T(8,128)S(1)} %dynamic-slice_bitcast_fusion), channel_id=1, source_target_pairs={{0,64},{64,0},{128,192},{192,128},{256,320},{320,256},{384,448},{4... | collective-permute-start | bytes 786440 | tf_op jit(solution)/shard_map/ppermute | solution.py:38
  141.5 24.2 %all-to-all-start.5 = ((f32[8,16,1024]{2,1,0:T(8,128)}), f32[8,16,1024]{2,1,0:T(8,128)S(1)}, u32[]{:S(2)}, u32[]{:S(2)}) async-start(f32[8,16,1024]{2,1,0:T(8,128)} %bitcast.18), calls=%async_computation.5 | async-start | bytes 1048576 | tf_op jit(solution)/shard_map/all_to_all | solution.py:21
  145.9 9.1 %collective-permute-start.6 = (f32[2,32,512]{2,1,0:T(8,128)S(1)}, f32[2,32,512]{2,1,0:T(8,128)S(1)}, u32[]{:S(2)}, u32[]{:S(2)}) collective-permute-start(f32[2,32,512]{2,1,0:T(8,128)S(1)} %dynamic-slice_bitcast_fusion.1), channel_id=1, source_target_pairs={{0,128},{64,192},{128,0},{192,64},{256,384},{320,448},{384,256},{4... | collective-permute-start | bytes 393224 | tf_op jit(solution)/shard_map/ppermute | solution.py:38
  155.0 10.1 %collective-permute-start.7 = (f32[32,512]{1,0:T(8,128)S(1)}, f32[32,512]{1,0:T(8,128)S(1)}, u32[]{:S(2)}, u32[]{:S(2)}) collective-permute-start(f32[32,512]{1,0:T(8,128)S(1)} %dynamic-slice_bitcast_fusion.2), channel_id=1, source_target_pairs={{0,256},{64,320},{128,384},{192,448},{256,0},{320,64},{384,128},{4... | collective-permute-start | bytes 196616 | tf_op jit(solution)/shard_map/ppermute | solution.py:38

commit v3 on v1

v3 whole, which is shorter than its diff:
```python
import functools

import jax
import jax.numpy as jnp
from jax import lax
from jax.experimental import pallas as pl
from jax.experimental.pallas import tpu as pltpu
from jax.sharding import Mesh
from jax.sharding import PartitionSpec as P

BLK = 256
LANES = 128
NEG = -1e30
ROW = ("y", "core")
COL = ("x", "z")
VMEM = pl.BlockSpec(memory_space=pltpu.VMEM)
HBM = pl.BlockSpec(memory_space=pltpu.HBM)
SMEM = pl.BlockSpec(memory_space=pltpu.SMEM)
ANY = pl.BlockSpec(memory_space=pl.ANY)
PARAMS = pltpu.CompilerParams(vmem_limit_bytes=40 * 2**20)
NN = (((1,), (0,)), ((), ()))
NT = (((1,), (1,)), ((), ()))


def split(x, terms):
    out = []
    for _ in range(terms):
        out.append(x.astype(jnp.bfloat16))
        x = x - out[-1].astype(jnp.float32)
    return out


def product(a, b, dims, order):
    total = None
    for both in range(order, -1, -1):
        for i in range(both + 1):
            if i < len(a) and both - i < len(b):
                p = lax.dot_general(a[i], b[both - i], dims, preferred_element_type=jnp.float32)
                total = p if total is None else total + p
    return total


def natural(me_ref, near_ref, far_ref, texts_ref):
    n, step, _ = near_ref.shape
    core, y = me_ref[0], me_ref[1]
    for k in range(n):
        for other, ref in enumerate((near_ref, far_ref)):
            at = ((y ^ place_of(k)) * 2 + (core ^ other)) * step
            texts_ref[pl.ds(pl.multiple_of(at, step), step), :] = ref[k]


def place_of(k):
    return (k % 2) * 4 + k // 2


def logits_kernel(
    me_ref, allow_ref, images_ref, near_ref, far_ref, logits_ref, row_ref, col_ref, texts_ref
):
    width, rows = images_ref.shape
    cols = texts_ref.shape[1]
    inv = width ** (-0.5)
    natural(me_ref, near_ref, far_ref, texts_ref)
    texts = split(texts_ref[...].T, 3)
    for i in range(rows // BLK):
        at = pl.ds(i * BLK, BLK)
        part = product(texts, split(images_ref[:, at], 3), NN, 2) * inv
        for j in range(cols // BLK):
            block = jnp.where(allow_ref[i, j] > 0, part[j * BLK : (j + 1) * BLK], NEG)
            logits_ref[pl.ds(j * BLK, BLK), at] = block
        part = logits_ref[:, at]
        top = jnp.max(part, axis=0, keepdims=True)
        lse = top + jnp.log(jnp.sum(jnp.exp(part - top), axis=0, keepdims=True))
        put(row_ref, lse, i * BLK // LANES)
    for j in range(cols // BLK):
        part = logits_ref[pl.ds(j * BLK, BLK), :]
        top = jnp.max(part, axis=1, keepdims=True)
        lse = top + jnp.log(jnp.sum(jnp.exp(part - top), axis=1, keepdims=True))
        lse = jnp.broadcast_to(lse, (BLK, LANES)).T[:1]
        for first in range(j * BLK // LANES, col_ref.shape[1], cols // LANES):
            put(col_ref, lse, first)


def put(ref, values, first):
    for k in range(values.shape[1] // LANES):
        row = values[:, k * LANES : (k + 1) * LANES]
        ref[:, pl.ds(first + k, 1), :] = jnp.broadcast_to(row[None], (ref.shape[0], 1, LANES))


def lse_of(parts):
    top = jnp.max(parts, axis=0)
    return top + jnp.log(jnp.sum(jnp.exp(parts - top[None]), axis=0))


def gradient(me_ref, logits_ref, row_ref, col_ref):
    cols, rows = logits_ref.shape
    row_lse = lse_of(row_ref[...])
    col_lse = lse_of(col_ref[...])
    col_lse = jnp.concatenate(
        [jnp.broadcast_to(col_lse[k : k + 1], (LANES, LANES)).T[:, :1] for k in range(cols // LANES)]
    )
    ahead = me_ref[2] - me_ref[3]
    for i in range(rows // BLK):
        part = logits_ref[:, pl.ds(i * BLK, BLK)]
        first = i * BLK // LANES
        row = jnp.concatenate([row_lse[first + k : first + k + 1] for k in range(BLK // LANES)], axis=1)
        grad = 0.5 * (jnp.exp(part - row) + jnp.exp(part - col_lse))
        text_at = lax.broadcasted_iota(jnp.int32, grad.shape, 0)
        image_at = lax.broadcasted_iota(jnp.int32, grad.shape, 1) + (i * BLK + ahead)
        yield pl.ds(i * BLK, BLK), jnp.where(text_at == image_at, grad - 1.0, grad)


def image_kernel(me_ref, logits_ref, row_ref, col_ref, near_ref, far_ref, terms_ref, texts_ref):
    inv = texts_ref.shape[0] ** (-0.5)
    natural(me_ref, near_ref, far_ref, texts_ref)
    texts = split(texts_ref[...], 2)
    for at, grad in gradient(me_ref, logits_ref, row_ref, col_ref):
        terms_ref[:, at] = product(texts, split(grad, 2), NN, 1) * inv


def text_kernel(me_ref, logits_ref, row_ref, col_ref, images_ref, keep_ref, send_ref, all_ref):
    inv = images_ref.shape[0] ** (-0.5)
    total = None
    for at, grad in gradient(me_ref, logits_ref, row_ref, col_ref):
        p = product(split(images_ref[:, at], 2), split(grad, 2), NT, 1)
        total = p if total is None else total + p
    all_ref[...] = total * inv
    n, step, _ = keep_ref.shape
    core, y = me_ref[0], me_ref[1]
    for k in range(n):
        for other, ref in enumerate((keep_ref, send_ref)):
            at = ((y ^ place_of(k)) * 2 + (core ^ other)) * step
            ref[k] = all_ref[pl.ds(pl.multiple_of(at, step), step), :]


def sum_kernel(parts_in, after_ref, out_ref, parts_ref, sems):
    del after_ref
    loads = [
        pltpu.make_async_copy(parts_in.at[k], parts_ref.at[k], sems.at[k]) for k in range(parts_in.shape[0])
    ]
    for load in loads:
        load.start()
    for load in loads:
        load.wait()
    out_ref[...] = jnp.sum(parts_ref[...], axis=0)


def gather(block, axis, n):
    return lax.all_to_all(jnp.broadcast_to(block[None], (n,) + block.shape), axis, 0, 0)


def after(x, y):
    return x + 0.0 * y.reshape(-1)[0]


def sum_of(parts, after):
    return pl.pallas_call(
        sum_kernel,
        out_shape=jax.ShapeDtypeStruct(parts.shape[1:], parts.dtype),
        in_specs=[ANY, ANY],
        scratch_shapes=[pltpu.VMEM(parts.shape, parts.dtype), pltpu.SemaphoreType.DMA((parts.shape[0],))],
        compiler_params=PARAMS,
        name="sum",
    )(parts, after)


def flip(axis, n, bit):
    return [(i, i ^ bit) for i in range(n)]


def body(image_embeddings, text_embeddings, negatives_mask):
    ny, nc, nx, nz = (lax.axis_size(a) for a in ("y", "core", "x", "z"))
    rows, own = image_embeddings.shape
    cols, own_text = text_embeddings.shape
    texts = text_embeddings.T
    far_half = lax.ppermute(texts, "y", flip("y", ny, 4))
    images = gather(image_embeddings.T, "z", nz).reshape(nz * own, rows)
    texts = after(jnp.stack([texts, far_half]), images)
    images = gather(after(images, far_half), "x", nx).reshape(nx * nz * own, rows)
    near = jnp.concatenate([texts] + [lax.ppermute(texts, "y", flip("y", ny, k)) for k in (1, 2, 3)])
    far = lax.ppermute(near, "core", flip("core", nc, 1))
    width = images.shape[0]
    row_start = lax.axis_index(ROW) * rows
    col_start = lax.axis_index(COL) * cols
    row_blocks, col_blocks = rows // BLK, cols // BLK
    first_row, first_col = row_start // BLK, col_start // BLK
    window = lax.dynamic_slice(negatives_mask, (first_row, first_col), (row_blocks, col_blocks))
    row_ids = first_row + jnp.arange(row_blocks, dtype=jnp.int32)
    col_ids = first_col + jnp.arange(col_blocks, dtype=jnp.int32)
    allow = ((window > 0) | (row_ids[:, None] == col_ids[None, :])).astype(jnp.int32)
    f32 = jnp.float32
    passes = 2 * rows * cols * width
    me = [lax.axis_index("core"), lax.axis_index("y"), row_start, col_start]
    me = jnp.stack(me).astype(jnp.int32)
    logits, row_parts, col_parts = pl.pallas_call(
        logits_kernel,
        out_shape=(
            jax.ShapeDtypeStruct((cols, rows), f32),
            jax.ShapeDtypeStruct((nx * nz, rows // LANES, LANES), f32),
            jax.ShapeDtypeStruct((ny * nc, rows // LANES, LANES), f32),
        ),
        in_specs=[SMEM, SMEM, VMEM, VMEM, VMEM],
        out_specs=(VMEM, VMEM, VMEM),
        scratch_shapes=[pltpu.VMEM((width, cols), f32)],
        compiler_params=PARAMS,
        cost_estimate=pl.CostEstimate(flops=6 * passes, bytes_accessed=5 << 20, transcendentals=0),
        name="logits",
    )(me, allow, images, near, far)
    col_parts = lax.all_to_all(col_parts, ROW, 0, 0)
    row_parts = lax.all_to_all(row_parts, COL, 0, 0)
    image_terms = pl.pallas_call(
        image_kernel,
        out_shape=jax.ShapeDtypeStruct((width, rows), f32),
        in_specs=[SMEM, VMEM, VMEM, VMEM, VMEM, VMEM],
        out_specs=VMEM,
        scratch_shapes=[pltpu.VMEM((width, cols), f32)],
        compiler_params=PARAMS,
        cost_estimate=pl.CostEstimate(flops=3 * passes, bytes_accessed=5 << 20, transcendentals=0),
        name="image_terms",
    )(me, logits, row_parts, col_parts, near, far)
    half = jax.ShapeDtypeStruct((ny, own_text, cols), f32)
    keep, send = pl.pallas_call(
        text_kernel,
        out_shape=(half, half),
        in_specs=[SMEM, VMEM, VMEM, VMEM, VMEM],
        out_specs=(VMEM, VMEM),
        scratch_shapes=[pltpu.VMEM((width, cols), f32)],
        compiler_params=PARAMS,
        cost_estimate=pl.CostEstimate(flops=3 * passes, bytes_accessed=5 << 20, transcendentals=0),
        name="text_terms",
    )(me, logits, row_parts, col_parts, images)
    parts = lax.all_to_all(image_terms.reshape(nx, nz * own, rows), "x", 0, 0)
    grad_text = keep + lax.ppermute(send, "core", flip("core", nc, 1))
    grad_text = grad_text.reshape(4, 2, own_text, cols)
    grad_text = sum([lax.ppermute(grad_text[k], "y", flip("y", ny, k)) for k in (1, 2, 3)], grad_text[0])
    parts = sum_of(parts, grad_text)
    grad_text = grad_text[0] + lax.ppermute(grad_text[1], "y", flip("y", ny, 4))
    grad_image = jnp.sum(lax.all_to_all(parts.reshape(nz, own, rows), "z", 0, 0), axis=0)
    return (grad_image.T, grad_text.T)


def solution(mesh):
    rows, cols = mesh.devices.shape
    fine = Mesh(mesh.devices.reshape(rows // 2, 2, 4, cols // 4), ("y", "core", "x", "z"))
    return jax.shard_map(
        body,
        mesh=fine,
        in_specs=(P(ROW, COL), P(COL, ROW), P()),
        out_specs=(P(ROW, COL), P(COL, ROW)),
        check_vma=False,
    )
```

time: 188 us -> 157 us (0.84)
  the two profiles are of different devices: /device:TPU:25 before, /device:TPU:2 now
where the time goes in v3:
time: 157 us; the launch traced here: 156 us
  starting transfers between devices  57.7 us (37%)
  waiting for transfers between devices  44 us (28%)
  blocking collectives  28.9 us (18%)
  Pallas kernels  12.1 us (8%)
  local copies, waits for them, and re-layouts  8.99 us (6%)
  other arithmetic  2.36 us (2%)
  between operations  2.24 us (1%)
    all_to_all x2, starting transfers between devices, gather(): lax.all_to_all(jnp.broadcast_to(block[None], (n,) + block.shape), axis, 0...  15.3 us
    all_to_all x1, blocking collectives, body(): col_parts = lax.all_to_all(col_parts, ROW, 0, 0)  14.9 us
    all_to_all x1, blocking collectives, body(): row_parts = lax.all_to_all(row_parts, COL, 0, 0)  14 us
    ppermute x3, starting transfers between devices, body(): lax.ppermute(texts, 'y', flip('y', ny, k))  10.1 us
    ppermute x3, waiting for transfers between devices, body(): lax.ppermute(grad_text[k], 'y', flip('y', ny, k))  9.71 us
    ppermute x3, starting transfers between devices, body(): lax.ppermute(grad_text[k], 'y', flip('y', ny, k))  9.21 us
    all_to_all x2, waiting for transfers between devices, gather(): lax.all_to_all(jnp.broadcast_to(block[None], (n,) + block.shape), axis, 0...  8.76 us
    ppermute x1, starting transfers between devices, body(): far_half = lax.ppermute(texts, 'y', flip('y', ny, 4))  7.72 us
  transfers between devices with their start and end apart: 14, of which 11 were waited for; matrix products, arithmetic and copies ran while one was open for 2% of the time, Pallas kernels for 2%

profile of v3, /device:TPU:2, one launch (start us, length us, event | category | flops | bytes accessed | tf_op | source)
XLA Modules:
  0.0 156.3 jit_solution(1277216920475448838)
XLA Ops:
  0.6 1.7 %broadcast_in_dim.4 = f32[8,16,1024]{2,1,0:T(8,128)} broadcast(f32[16,1024]{1,0:T(8,128)} %bitcast.38), dimensions={1,2} | broadcast | bytes 589824 | tf_op jit(solution)/shard_map/broadcast_in_dim | solution.py:148
  2.3 10.3 %all-to-all-start = ((f32[8,16,1024]{2,1,0:T(8,128)}), f32[8,16,1024]{2,1,0:T(8,128)S(1)}, u32[]{:S(2)}, u32[]{:S(2)}) async-start(f32[8,16,1024]{2,1,0:T(8,128)} %broadcast_in_dim.4), calls=%async_computation | async-start | bytes 1048576 | tf_op jit(solution)/shard_map/all_to_all | solution.py:148
  12.6 7.7 %collective-permute-start = (f32[32,512]{1,0:T(8,128)}, f32[32,512]{1,0:T(8,128)S(1)}, u32[]{:S(2)}, u32[]{:S(2)}) collective-permute-start(f32[32,512]{1,0:T(8,128)} %bitcast.40), channel_id=1, source_target_pairs={{0,256},{64,320},{128,384},{192,448},{256,0},{320,64},{384,128},{4... | collective-permute-start | bytes 196616 | tf_op jit(solution)/shard_map/ppermute | solution.py:175
  20.4 2.9 %collective-permute-done = f32[32,512]{1,0:T(8,128)S(1)} collective-permute-done((f32[32,512]{1,0:T(8,128)}, f32[32,512]{1,0:T(8,128)S(1)}, u32[]{:S(2)}, u32[]{:S(2)}) %collective-permute-start) | collective-permute-done | bytes 65568 | tf_op jit(solution)/shard_map/ppermute | solution.py:175
  24.4 5.7 %all-to-all-done = f32[8,16,1024]{2,1,0:T(8,128)S(1)} async-done(((f32[8,16,1024]{2,1,0:T(8,128)}), f32[8,16,1024]{2,1,0:T(8,128)S(1)}, u32[]{:S(2)}, u32[]{:S(2)}) %all-to-all-start) | async-done | bytes 524320 | tf_op jit(solution)/shard_map/all_to_all | solution.py:148
  30.2 1.6 %broadcast_in_dim.5 = f32[4,128,1024]{2,1,0:T(8,128)} broadcast(f32[128,1024]{1,0:T(8,128)S(1)} %bitcast.34), dimensions={1,2} | broadcast | bytes 2621440 | tf_op jit(solution)/shard_map/broadcast_in_dim | solution.py:148
  31.8 5.0 %all-to-all-start.1 = ((f32[4,128,1024]{2,1,0:T(8,128)}), f32[4,128,1024]{2,1,0:T(8,128)S(1)}, u32[]{:S(2)}, u32[]{:S(2)}) async-start(f32[4,128,1024]{2,1,0:T(8,128)} %broadcast_in_dim.5), calls=%async_computation.1 | async-start | bytes 4194304 | tf_op jit(solution)/shard_map/all_to_all | solution.py:148
  38.0 5.5 %collective-permute-start.3 = (f32[2,32,512]{2,1,0:T(8,128)S(1)}, f32[2,32,512]{2,1,0:T(8,128)S(1)}, u32[]{:S(2)}, u32[]{:S(2)}) collective-permute-start(f32[2,32,512]{2,1,0:T(8,128)S(1)} %maximum_add_fusion), channel_id=1, source_target_pairs={{0,192},{64,128},{128,64},{192,0},{256,448},{320,384},{384,320},{4... | collective-permute-start | bytes 393224 | tf_op jit(solution)/shard_map/ppermute | solution.py:179
  43.6 1.9 %collective-permute-start.2 = (f32[2,32,512]{2,1,0:T(8,128)S(1)}, f32[2,32,512]{2,1,0:T(8,128)S(1)}, u32[]{:S(2)}, u32[]{:S(2)}) collective-permute-start(f32[2,32,512]{2,1,0:T(8,128)S(1)} %maximum_add_fusion), channel_id=1, source_target_pairs={{0,128},{64,192},{128,0},{192,64},{256,384},{320,448},{384,256},{4... | collective-permute-start | bytes 393224 | tf_op jit(solution)/shard_map/ppermute | solution.py:179
  45.5 2.7 %collective-permute-start.1 = (f32[2,32,512]{2,1,0:T(8,128)S(1)}, f32[2,32,512]{2,1,0:T(8,128)S(1)}, u32[]{:S(2)}, u32[]{:S(2)}) collective-permute-start(f32[2,32,512]{2,1,0:T(8,128)S(1)} %maximum_add_fusion), channel_id=1, source_target_pairs={{0,64},{64,0},{128,192},{192,128},{256,320},{320,256},{384,448},{4... | collective-permute-start | bytes 393224 | tf_op jit(solution)/shard_map/ppermute | solution.py:179
  48.2 6.1 %collective-permute-done.2 = f32[2,32,512]{2,1,0:T(8,128)S(1)} collective-permute-done((f32[2,32,512]{2,1,0:T(8,128)S(1)}, f32[2,32,512]{2,1,0:T(8,128)S(1)}, u32[]{:S(2)}, u32[]{:S(2)}) %collective-permute-start.2) | collective-permute-done | bytes 131104 | tf_op jit(solution)/shard_map/ppermute | solution.py:179
  54.9 1.9 %collective-permute-start.4 = (f32[8,32,512]{2,1,0:T(8,128)S(1)}, f32[8,32,512]{2,1,0:T(8,128)S(1)}, u32[]{:S(2)}, u32[]{:S(2)}) collective-permute-start(f32[8,32,512]{2,1,0:T(8,128)S(1)} %pad_maximum_fusion.near_ref), channel_id=1, source_target_pairs={{0,32},{32,0},{1,33},{33,1},{2,34},{34,2},{3,35},{35,3},{4,36},{36... | collective-permute-start | bytes 1572872 | tf_op jit(solution)/shard_map/ppermute | solution.py:180
  58.7 3.1 %all-to-all-done.1 = f32[4,128,1024]{2,1,0:T(8,128)S(1)} async-done(((f32[4,128,1024]{2,1,0:T(8,128)}), f32[4,128,1024]{2,1,0:T(8,128)S(1)}, u32[]{:S(2)}, u32[]{:S(2)}) %all-to-all-start.1) | async-done | bytes 2097184 | tf_op jit(solution)/shard_map/all_to_all | solution.py:148
  61.8 5.1 %logits.1 = (f32[512,1024]{1,0:T(8,128)S(1)}, f32[32,8,128]{2,1,0:T(8,128)S(1)}, f32[16,8,128]{2,1,0:T(8,128)S(1)}) custom-call(s32[4]{0:T(128)S(1)} %pad_add_fusion.me_ref, s32[4,2]{1,0:T(4,128)S(1)} %fusion.5.allow_ref, f32[512,1024]{1,0:T(8,128)S(1)} %bitcast.30, f32[8,32,512]{2,1,0:T(8,128)S(1)} %pad_maximum_fusion.near_ref, ...), custom_call_target="tpu_custom_call" | custom-call | flops 3221225472 | bytes 5242880 | tf_op jit(solution)/shard_map/logits/pallas_call | solution.py:194
  66.9 14.9 %all_to_all.30.col_ref = f32[16,8,128]{2,1,0:T(8,128)S(1)} all-to-all(f32[16,8,128]{2,1,0:T(8,128)S(1)} %get-tuple-element.9), channel_id=1, replica_groups=mesh['y'=8,'core'=2,'x'=4,'z'=8] {'y','core'}, dimensions={0} | all-to-all | bytes 131072 | tf_op jit(solution)/shard_map/all_to_all | solution.py:208
  81.8 14.0 %all_to_all.31.row_ref = f32[32,8,128]{2,1,0:T(8,128)S(1)} all-to-all(f32[32,8,128]{2,1,0:T(8,128)S(1)} %get-tuple-element.8), channel_id=1, replica_groups=mesh['y'=8,'core'=2,'x'=4,'z'=8] {'x','z'}, dimensions={0} | all-to-all | bytes 262144 | tf_op jit(solution)/shard_map/all_to_all | solution.py:209
  95.8 3.0 %image_terms.1 = f32[512,1024]{1,0:T(8,128)S(1)} custom-call(s32[4]{0:T(128)S(1)} %pad_add_fusion.me_ref, f32[512,1024]{1,0:T(8,128)S(1)} %get-tuple-element.7.logits_ref, f32[32,8,128]{2,1,0:T(8,128)S(1)} %all_to_all.31.row_ref, f32[16,8,128]{2,1,0:T(8,128)S(1)} %all_to_all.30.col_ref, f32[8,32,512]{2,1,0:T(8,128)S(1)} %pad_maximum_fusion.near_ref, ...), custom_call_target="tpu_custom_call" | custom-call | flops 1610612736 | bytes 5242880 | tf_op jit(solution)/shard_map/image_terms/pallas_call | solution.py:210
  100.2 5.0 %all-to-all-start.4 = ((f32[4,128,1024]{2,1,0:T(8,128)}), f32[4,128,1024]{2,1,0:T(8,128)S(1)}, u32[]{:S(2)}, u32[]{:S(2)}) async-start(f32[4,128,1024]{2,1,0:T(8,128)} %bitcast.32), calls=%async_computation.4 | async-start | bytes 4194304 | tf_op jit(solution)/shard_map/all_to_all | solution.py:231
  105.2 1.6 %copy-done.1 = f32[4,128,1024]{2,1,0:T(8,128)S(1)} copy-done((f32[4,128,1024]{2,1,0:T(8,128)S(1)}, f32[4,128,1024]{2,1,0:T(8,128)}, u32[]{:S(2)}) %copy-start.1) | copy-done | bytes 2097176
  106.8 1.6 %copy-done.4 = f32[512,1024]{1,0:T(8,128)S(1)} copy-done((f32[512,1024]{1,0:T(8,128)S(1)}, f32[512,1024]{1,0:T(8,128)}, u32[]{:S(2)}) %copy-start.4) | copy-done | bytes 2097176
  108.3 2.9 %text_terms.1 = (f32[8,32,512]{2,1,0:T(8,128)S(1)}, f32[8,32,512]{2,1,0:T(8,128)S(1)}) custom-call(s32[4]{0:T(128)S(1)} %pad_add_fusion.me_ref, f32[512,1024]{1,0:T(8,128)S(1)} %copy-done.4, f32[32,8,128]{2,1,0:T(8,128)S(1)} %all_to_all.31.row_ref, f32[16,8,128]{2,1,0:T(8,128)S(1)} %all_to_all.30.col_ref, f32[512,1024]{1,0:T(8,128)S(1)} %bitcast.31), custom_call_target="tpu_custom_call" | custom-call | flops 1610612736 | bytes 5242880 | tf_op jit(solution)/shard_map/text_terms/pallas_call | solution.py:221
  111.3 1.9 %collective-permute-start.5 = (f32[8,32,512]{2,1,0:T(8,128)S(1)}, f32[8,32,512]{2,1,0:T(8,128)S(1)}, u32[]{:S(2)}, u32[]{:S(2)}) collective-permute-start(f32[8,32,512]{2,1,0:T(8,128)S(1)} %get-tuple-element.11), channel_id=1, source_target_pairs={{0,32},{32,0},{1,33},{33,1},{2,34},{34,2},{3,35},{35,3},{4,36},{36... | collective-permute-start | bytes 1572872 | tf_op jit(solution)/shard_map/ppermute | solution.py:232
  113.2 1.9 %collective-permute-done.5 = f32[8,32,512]{2,1,0:T(8,128)S(1)} collective-permute-done((f32[8,32,512]{2,1,0:T(8,128)S(1)}, f32[8,32,512]{2,1,0:T(8,128)S(1)}, u32[]{:S(2)}, u32[]{:S(2)}) %collective-permute-start.5) | collective-permute-done | bytes 524320 | tf_op jit(solution)/shard_map/ppermute | solution.py:232
  115.2 2.6 %collective-permute-start.6 = (f32[2,32,512]{2,1,0:T(8,128)S(1)}, f32[2,32,512]{2,1,0:T(8,128)S(1)}, u32[]{:S(2)}, u32[]{:S(2)}) collective-permute-start(f32[2,32,512]{2,1,0:T(8,128)S(1)} %get-tuple-element.12), channel_id=1, source_target_pairs={{0,64},{64,0},{128,192},{192,128},{256,320},{320,256},{384,448},{4... | collective-permute-start | bytes 393224 | tf_op jit(solution)/shard_map/ppermute | solution.py:234
  117.7 3.3 %collective-permute-start.8 = (f32[2,32,512]{2,1,0:T(8,128)S(1)}, f32[2,32,512]{2,1,0:T(8,128)S(1)}, u32[]{:S(2)}, u32[]{:S(2)}) collective-permute-start(f32[2,32,512]{2,1,0:T(8,128)S(1)} %get-tuple-element.13), channel_id=1, source_target_pairs={{0,192},{64,128},{128,64},{192,0},{256,448},{320,384},{384,320},{4... | collective-permute-start | bytes 393224 | tf_op jit(solution)/shard_map/ppermute | solution.py:234
  121.1 3.3 %collective-permute-start.7 = (f32[2,32,512]{2,1,0:T(8,128)S(1)}, f32[2,32,512]{2,1,0:T(8,128)S(1)}, u32[]{:S(2)}, u32[]{:S(2)}) collective-permute-start(f32[2,32,512]{2,1,0:T(8,128)S(1)} %get-tuple-element.14), channel_id=1, source_target_pairs={{0,128},{64,192},{128,0},{192,64},{256,384},{320,448},{384,256},{4... | collective-permute-start | bytes 393224 | tf_op jit(solution)/shard_map/ppermute | solution.py:234
  124.4 3.3 %collective-permute-done.8 = f32[2,32,512]{2,1,0:T(8,128)S(1)} collective-permute-done((f32[2,32,512]{2,1,0:T(8,128)S(1)}, f32[2,32,512]{2,1,0:T(8,128)S(1)}, u32[]{:S(2)}, u32[]{:S(2)}) %collective-permute-start.8) | collective-permute-done | bytes 131104 | tf_op jit(solution)/shard_map/ppermute | solution.py:234
  127.8 6.4 %collective-permute-done.7 = f32[2,32,512]{2,1,0:T(8,128)S(1)} collective-permute-done((f32[2,32,512]{2,1,0:T(8,128)S(1)}, f32[2,32,512]{2,1,0:T(8,128)S(1)}, u32[]{:S(2)}, u32[]{:S(2)}) %collective-permute-start.7) | collective-permute-done | bytes 131104 | tf_op jit(solution)/shard_map/ppermute | solution.py:234
  135.3 3.5 %all-to-all-start.5 = ((f32[8,16,1024]{2,1,0:T(8,128)}), f32[8,16,1024]{2,1,0:T(8,128)S(1)}, u32[]{:S(2)}, u32[]{:S(2)}) async-start(f32[8,16,1024]{2,1,0:T(8,128)} %bitcast.13), calls=%async_computation.5 | async-start | bytes 1048576 | tf_op jit(solution)/shard_map/all_to_all | solution.py:237
  138.8 3.1 %collective-permute-start.9 = (f32[32,512]{1,0:T(8,128)S(1)}, f32[32,512]{1,0:T(8,128)S(1)}, u32[]{:S(2)}, u32[]{:S(2)}) collective-permute-start(f32[32,512]{1,0:T(8,128)S(1)} %slice_bitcast_fusion), channel_id=1, source_target_pairs={{0,256},{64,320},{128,384},{192,448},{256,0},{320,64},{384,128},{4... | collective-permute-start | bytes 196616 | tf_op jit(solution)/shard_map/ppermute | solution.py:236
  141.9 7.0 %collective-permute-done.9 = f32[32,512]{1,0:T(8,128)S(1)} collective-permute-done((f32[32,512]{1,0:T(8,128)S(1)}, f32[32,512]{1,0:T(8,128)S(1)}, u32[]{:S(2)}, u32[]{:S(2)}) %collective-permute-start.9) | collective-permute-done | bytes 65568 | tf_op jit(solution)/shard_map/ppermute | solution.py:236
  149.5 6.2 %all-to-all-done.5 = f32[8,16,1024]{2,1,0:T(8,128)S(1)} async-done(((f32[8,16,1024]{2,1,0:T(8,128)}), f32[8,16,1024]{2,1,0:T(8,128)S(1)}, u32[]{:S(2)}, u32[]{:S(2)}) %all-to-all-start.5) | async-done | bytes 524320 | tf_op jit(solution)/shard_map/all_to_all | solution.py:237
  (33 shorter events, 7.5 us)
Async XLA Ops:
  2.3 27.8 %all-to-all-start = ((f32[8,16,1024]{2,1,0:T(8,128)}), f32[8,16,1024]{2,1,0:T(8,128)S(1)}, u32[]{:S(2)}, u32[]{:S(2)}) async-start(f32[8,16,1024]{2,1,0:T(8,128)} %broadcast_in_dim.4), calls=%async_computation | async-start | bytes 1048576 | tf_op jit(solution)/shard_map/all_to_all | solution.py:148
  12.6 10.6 %collective-permute-start = (f32[32,512]{1,0:T(8,128)}, f32[32,512]{1,0:T(8,128)S(1)}, u32[]{:S(2)}, u32[]{:S(2)}) collective-permute-start(f32[32,512]{1,0:T(8,128)} %bitcast.40), channel_id=1, source_target_pairs={{0,256},{64,320},{128,384},{192,448},{256,0},{320,64},{384,128},{4... | collective-permute-start | bytes 196616 | tf_op jit(solution)/shard_map/ppermute | solution.py:175
  31.8 6.2 %copy-start.5 = (f32[512,32]{0,1:T(8,128)S(1)}, f32[512,32]{0,1:T(8,128)}, u32[]{:S(2)}) copy-start(f32[512,32]{0,1:T(8,128)} %param.4) | copy-start | bytes 196612
  31.8 30.0 %all-to-all-start.1 = ((f32[4,128,1024]{2,1,0:T(8,128)}), f32[4,128,1024]{2,1,0:T(8,128)S(1)}, u32[]{:S(2)}, u32[]{:S(2)}) async-start(f32[4,128,1024]{2,1,0:T(8,128)} %broadcast_in_dim.5), calls=%async_computation.1 | async-start | bytes 4194304 | tf_op jit(solution)/shard_map/all_to_all | solution.py:148
  38.0 10.2 %collective-permute-start.3 = (f32[2,32,512]{2,1,0:T(8,128)S(1)}, f32[2,32,512]{2,1,0:T(8,128)S(1)}, u32[]{:S(2)}, u32[]{:S(2)}) collective-permute-start(f32[2,32,512]{2,1,0:T(8,128)S(1)} %maximum_add_fusion), channel_id=1, source_target_pairs={{0,192},{64,128},{128,64},{192,0},{256,448},{320,384},{384,320},{4... | collective-permute-start | bytes 393224 | tf_op jit(solution)/shard_map/ppermute | solution.py:179
  43.6 10.8 %collective-permute-start.2 = (f32[2,32,512]{2,1,0:T(8,128)S(1)}, f32[2,32,512]{2,1,0:T(8,128)S(1)}, u32[]{:S(2)}, u32[]{:S(2)}) collective-permute-start(f32[2,32,512]{2,1,0:T(8,128)S(1)} %maximum_add_fusion), channel_id=1, source_target_pairs={{0,128},{64,192},{128,0},{192,64},{256,384},{320,448},{384,256},{4... | collective-permute-start | bytes 393224 | tf_op jit(solution)/shard_map/ppermute | solution.py:179
  45.5 9.4 %collective-permute-start.1 = (f32[2,32,512]{2,1,0:T(8,128)S(1)}, f32[2,32,512]{2,1,0:T(8,128)S(1)}, u32[]{:S(2)}, u32[]{:S(2)}) collective-permute-start(f32[2,32,512]{2,1,0:T(8,128)S(1)} %maximum_add_fusion), channel_id=1, source_target_pairs={{0,64},{64,0},{128,192},{192,128},{256,320},{320,256},{384,448},{4... | collective-permute-start | bytes 393224 | tf_op jit(solution)/shard_map/ppermute | solution.py:179
  54.9 3.8 %collective-permute-start.4 = (f32[8,32,512]{2,1,0:T(8,128)S(1)}, f32[8,32,512]{2,1,0:T(8,128)S(1)}, u32[]{:S(2)}, u32[]{:S(2)}) collective-permute-start(f32[8,32,512]{2,1,0:T(8,128)S(1)} %pad_maximum_fusion.near_ref), channel_id=1, source_target_pairs={{0,32},{32,0},{1,33},{33,1},{2,34},{34,2},{3,35},{35,3},{4,36},{36... | collective-permute-start | bytes 1572872 | tf_op jit(solution)/shard_map/ppermute | solution.py:180
  61.8 5.1 %copy-start = (f32[4,128,1024]{2,1,0:T(8,128)}, f32[4,128,1024]{2,1,0:T(8,128)S(1)}, u32[]{:S(2)}) copy-start(f32[4,128,1024]{2,1,0:T(8,128)S(1)} %all-to-all-done.1) | copy-start | bytes 6291460
  66.9 31.9 %copy-start.3 = (f32[512,1024]{1,0:T(8,128)}, f32[512,1024]{1,0:T(8,128)S(1)}, u32[]{:S(2)}) copy-start(f32[512,1024]{1,0:T(8,128)S(1)} %get-tuple-element.7.logits_ref) | copy-start | bytes 6291460
  98.8 1.3 copy-start.2
  100.2 34.0 %all-to-all-start.4 = ((f32[4,128,1024]{2,1,0:T(8,128)}), f32[4,128,1024]{2,1,0:T(8,128)S(1)}, u32[]{:S(2)}, u32[]{:S(2)}) async-start(f32[4,128,1024]{2,1,0:T(8,128)} %bitcast.32), calls=%async_computation.4 | async-start | bytes 4194304 | tf_op jit(solution)/shard_map/all_to_all | solution.py:231
  105.2 1.6 %copy-start.1 = (f32[4,128,1024]{2,1,0:T(8,128)S(1)}, f32[4,128,1024]{2,1,0:T(8,128)}, u32[]{:S(2)}) copy-start(f32[4,128,1024]{2,1,0:T(8,128)} %copy-done) | copy-start | bytes 6291460
  106.8 1.6 %copy-start.4 = (f32[512,1024]{1,0:T(8,128)S(1)}, f32[512,1024]{1,0:T(8,128)}, u32[]{:S(2)}) copy-start(f32[512,1024]{1,0:T(8,128)} %copy-done.3) | copy-start | bytes 6291460
  111.3 3.8 %collective-permute-start.5 = (f32[8,32,512]{2,1,0:T(8,128)S(1)}, f32[8,32,512]{2,1,0:T(8,128)S(1)}, u32[]{:S(2)}, u32[]{:S(2)}) collective-permute-start(f32[8,32,512]{2,1,0:T(8,128)S(1)} %get-tuple-element.11), channel_id=1, source_target_pairs={{0,32},{32,0},{1,33},{33,1},{2,34},{34,2},{3,35},{35,3},{4,36},{36... | collective-permute-start | bytes 1572872 | tf_op jit(solution)/shard_map/ppermute | solution.py:232
  115.2 9.2 %collective-permute-start.6 = (f32[2,32,512]{2,1,0:T(8,128)S(1)}, f32[2,32,512]{2,1,0:T(8,128)S(1)}, u32[]{:S(2)}, u32[]{:S(2)}) collective-permute-start(f32[2,32,512]{2,1,0:T(8,128)S(1)} %get-tuple-element.12), channel_id=1, source_target_pairs={{0,64},{64,0},{128,192},{192,128},{256,320},{320,256},{384,448},{4... | collective-permute-start | bytes 393224 | tf_op jit(solution)/shard_map/ppermute | solution.py:234
  117.7 10.0 %collective-permute-start.8 = (f32[2,32,512]{2,1,0:T(8,128)S(1)}, f32[2,32,512]{2,1,0:T(8,128)S(1)}, u32[]{:S(2)}, u32[]{:S(2)}) collective-permute-start(f32[2,32,512]{2,1,0:T(8,128)S(1)} %get-tuple-element.13), channel_id=1, source_target_pairs={{0,192},{64,128},{128,64},{192,0},{256,448},{320,384},{384,320},{4... | collective-permute-start | bytes 393224 | tf_op jit(solution)/shard_map/ppermute | solution.py:234
  121.1 13.1 %collective-permute-start.7 = (f32[2,32,512]{2,1,0:T(8,128)S(1)}, f32[2,32,512]{2,1,0:T(8,128)S(1)}, u32[]{:S(2)}, u32[]{:S(2)}) collective-permute-start(f32[2,32,512]{2,1,0:T(8,128)S(1)} %get-tuple-element.14), channel_id=1, source_target_pairs={{0,128},{64,192},{128,0},{192,64},{256,384},{320,448},{384,256},{4... | collective-permute-start | bytes 393224 | tf_op jit(solution)/shard_map/ppermute | solution.py:234
  135.3 20.4 %all-to-all-start.5 = ((f32[8,16,1024]{2,1,0:T(8,128)}), f32[8,16,1024]{2,1,0:T(8,128)S(1)}, u32[]{:S(2)}, u32[]{:S(2)}) async-start(f32[8,16,1024]{2,1,0:T(8,128)} %bitcast.13), calls=%async_computation.5 | async-start | bytes 1048576 | tf_op jit(solution)/shard_map/all_to_all | solution.py:237
  138.8 10.1 %collective-permute-start.9 = (f32[32,512]{1,0:T(8,128)S(1)}, f32[32,512]{1,0:T(8,128)S(1)}, u32[]{:S(2)}, u32[]{:S(2)}) collective-permute-start(f32[32,512]{1,0:T(8,128)S(1)} %slice_bitcast_fusion), channel_id=1, source_target_pairs={{0,256},{64,320},{128,384},{192,448},{256,0},{320,64},{384,128},{4... | collective-permute-start | bytes 196616 | tf_op jit(solution)/shard_map/ppermute | solution.py:236

commit v4 on v3

--- a/solution.py
+++ b/solution.py
@@ -43,14 +43,15 @@
 def natural(me_ref, near_ref, far_ref, texts_ref):
     n, step, _ = near_ref.shape
     core, y = me_ref[0], me_ref[1]
-    for k in range(n):
+    for k, there in enumerate(pairs(y, -1, n)):
         for other, ref in enumerate((near_ref, far_ref)):
-            at = ((y ^ place_of(k)) * 2 + (core ^ other)) * step
+            at = (there * 2 + (core ^ other)) * step
             texts_ref[pl.ds(pl.multiple_of(at, step), step), :] = ref[k]
 
 
-def place_of(k):
-    return (k % 2) * 4 + k // 2
+def pairs(y, way, n):
+    two = y + way * (2 - 4 * (y & 1))
+    return [(at + half) & (n - 1) for at in (y, y + way, y - way, two) for half in (0, n // 2)]
 
 
 def logits_kernel(
@@ -126,9 +127,9 @@
     all_ref[...] = total * inv
     n, step, _ = keep_ref.shape
     core, y = me_ref[0], me_ref[1]
-    for k in range(n):
+    for k, there in enumerate(pairs(y, 1, n)):
         for other, ref in enumerate((keep_ref, send_ref)):
-            at = ((y ^ place_of(k)) * 2 + (core ^ other)) * step
+            at = (there * 2 + (core ^ other)) * step
             ref[k] = all_ref[pl.ds(pl.multiple_of(at, step), step), :]
 
 
@@ -163,8 +164,16 @@
     )(parts, after)
 
 
-def flip(axis, n, bit):
+def flip(n, bit):
     return [(i, i ^ bit) for i in range(n)]
+
+
+def shifts(n):
+    return [
+        [(i, (i + 1) % n) for i in range(n)],
+        [(i, (i - 1) % n) for i in range(n)],
+        [(i, (i + 2 - 4 * (i % 2)) % n) for i in range(n)],
+    ]
 
 
 def body(image_embeddings, text_embeddings, negatives_mask):
@@ -172,12 +181,12 @@
     rows, own = image_embeddings.shape
     cols, own_text = text_embeddings.shape
     texts = text_embeddings.T
-    far_half = lax.ppermute(texts, "y", flip("y", ny, 4))
+    far_half = lax.ppermute(texts, "y", flip(ny, ny // 2))
     images = gather(image_embeddings.T, "z", nz).reshape(nz * own, rows)
     texts = after(jnp.stack([texts, far_half]), images)
     images = gather(after(images, far_half), "x", nx).reshape(nx * nz * own, rows)
-    near = jnp.concatenate([texts] + [lax.ppermute(texts, "y", flip("y", ny, k)) for k in (1, 2, 3)])
-    far = lax.ppermute(near, "core", flip("core", nc, 1))
+    near = jnp.concatenate([texts] + [lax.ppermute(texts, "y", perm) for perm in shifts(ny)])
+    far = lax.ppermute(near, "core", flip(nc, 1))
     width = images.shape[0]
     row_start = lax.axis_index(ROW) * rows
     col_start = lax.axis_index(COL) * cols
@@ -229,11 +238,12 @@
         name="text_terms",
     )(me, logits, row_parts, col_parts, images)
     parts = lax.all_to_all(image_terms.reshape(nx, nz * own, rows), "x", 0, 0)
-    grad_text = keep + lax.ppermute(send, "core", flip("core", nc, 1))
+    grad_text = keep + lax.ppermute(send, "core", flip(nc, 1))
     grad_text = grad_text.reshape(4, 2, own_text, cols)
-    grad_text = sum([lax.ppermute(grad_text[k], "y", flip("y", ny, k)) for k in (1, 2, 3)], grad_text[0])
-    parts = sum_of(parts, grad_text)
-    grad_text = grad_text[0] + lax.ppermute(grad_text[1], "y", flip("y", ny, 4))
+    moved = [lax.ppermute(grad_text[k + 1], "y", perm) for k, perm in enumerate(shifts(ny))]
+    parts = sum_of(parts, moved[0] + moved[1])
+    grad_text = sum(moved, grad_text[0])
+    grad_text = grad_text[0] + lax.ppermute(grad_text[1], "y", flip(ny, ny // 2))
     grad_image = jnp.sum(lax.all_to_all(parts.reshape(nz, own, rows), "z", 0, 0), axis=0)
     return (grad_image.T, grad_text.T)
 

time: 157 us -> 152 us (0.968)
  waiting for transfers between devices: 44 us -> 35.6 us
  starting transfers between devices: 57.7 us -> 60.8 us
    ppermute x10, waiting for transfers between devices: 29.1 us -> 21.7 us  [the longest x3 6.09 us: body(): lax.ppermute(texts, 'y', perm)]
    ppermute x10, starting transfers between devices: 34 us -> 36.8 us  [the longest x3 11.3 us: body(): lax.ppermute(texts, 'y', perm)]
  transfers between devices with their start and end apart: 14 -> 14, of which waited for: 11 -> 13; matrix products, arithmetic and copies ran while one was open for 2% -> 2% of each run, Pallas kernels for 2% -> 2%
where the time goes in v4:
time: 152 us; the launch traced here: 151 us
  starting transfers between devices  60.8 us (40%)
  waiting for transfers between devices  35.6 us (23%)
  blocking collectives  28.9 us (19%)
  Pallas kernels  12.1 us (8%)
  local copies, waits for them, and re-layouts  8.98 us (6%)
  other arithmetic  2.36 us (2%)
  between operations  2.21 us (1%)
    all_to_all x2, starting transfers between devices, gather(): lax.all_to_all(jnp.broadcast_to(block[None], (n,) + block.shape), axis, 0...  15.3 us
    all_to_all x1, blocking collectives, body(): col_parts = lax.all_to_all(col_parts, ROW, 0, 0)  14.9 us
    all_to_all x1, blocking collectives, body(): row_parts = lax.all_to_all(row_parts, COL, 0, 0)  14 us
    ppermute x3, starting transfers between devices, body(): lax.ppermute(texts, 'y', perm)  11.3 us
    ppermute x3, starting transfers between devices, body(): lax.ppermute(grad_text[k + 1], 'y', perm)  8.35 us
    all_to_all x2, waiting for transfers between devices, gather(): lax.all_to_all(jnp.broadcast_to(block[None], (n,) + block.shape), axis, 0...  8.1 us
    ppermute x1, starting transfers between devices, body(): far_half = lax.ppermute(texts, 'y', flip(ny, ny // 2))  7.72 us
    ppermute x3, waiting for transfers between devices, body(): lax.ppermute(texts, 'y', perm)  6.09 us
  transfers between devices with their start and end apart: 14, of which 13 were waited for; matrix products, arithmetic and copies ran while one was open for 2% of the time, Pallas kernels for 2%

profile of v4, /device:TPU:2, one launch (start us, length us, event | category | flops | bytes accessed | tf_op | source)
XLA Modules:
  0.0 151.0 jit_solution(4391246449570990808)
XLA Ops:
  0.6 1.7 %broadcast_in_dim.4 = f32[8,16,1024]{2,1,0:T(8,128)} broadcast(f32[16,1024]{1,0:T(8,128)} %bitcast.38), dimensions={1,2} | broadcast | bytes 589824 | tf_op jit(solution)/shard_map/broadcast_in_dim | solution.py:149
  2.3 10.3 %all-to-all-start = ((f32[8,16,1024]{2,1,0:T(8,128)}), f32[8,16,1024]{2,1,0:T(8,128)S(1)}, u32[]{:S(2)}, u32[]{:S(2)}) async-start(f32[8,16,1024]{2,1,0:T(8,128)} %broadcast_in_dim.4), calls=%async_computation | async-start | bytes 1048576 | tf_op jit(solution)/shard_map/all_to_all | solution.py:149
  12.6 7.7 %collective-permute-start = (f32[32,512]{1,0:T(8,128)}, f32[32,512]{1,0:T(8,128)S(1)}, u32[]{:S(2)}, u32[]{:S(2)}) collective-permute-start(f32[32,512]{1,0:T(8,128)} %bitcast.40), channel_id=1, source_target_pairs={{0,256},{64,320},{128,384},{192,448},{256,0},{320,64},{384,128},{4... | collective-permute-start | bytes 196616 | tf_op jit(solution)/shard_map/ppermute | solution.py:184
  20.4 2.9 %collective-permute-done = f32[32,512]{1,0:T(8,128)S(1)} collective-permute-done((f32[32,512]{1,0:T(8,128)}, f32[32,512]{1,0:T(8,128)S(1)}, u32[]{:S(2)}, u32[]{:S(2)}) %collective-permute-start) | collective-permute-done | bytes 65568 | tf_op jit(solution)/shard_map/ppermute | solution.py:184
  24.4 5.7 %all-to-all-done = f32[8,16,1024]{2,1,0:T(8,128)S(1)} async-done(((f32[8,16,1024]{2,1,0:T(8,128)}), f32[8,16,1024]{2,1,0:T(8,128)S(1)}, u32[]{:S(2)}, u32[]{:S(2)}) %all-to-all-start) | async-done | bytes 524320 | tf_op jit(solution)/shard_map/all_to_all | solution.py:149
  30.2 1.6 %broadcast_in_dim.5 = f32[4,128,1024]{2,1,0:T(8,128)} broadcast(f32[128,1024]{1,0:T(8,128)S(1)} %bitcast.34), dimensions={1,2} | broadcast | bytes 2621440 | tf_op jit(solution)/shard_map/broadcast_in_dim | solution.py:149
  31.8 5.0 %all-to-all-start.1 = ((f32[4,128,1024]{2,1,0:T(8,128)}), f32[4,128,1024]{2,1,0:T(8,128)S(1)}, u32[]{:S(2)}, u32[]{:S(2)}) async-start(f32[4,128,1024]{2,1,0:T(8,128)} %broadcast_in_dim.5), calls=%async_computation.1 | async-start | bytes 4194304 | tf_op jit(solution)/shard_map/all_to_all | solution.py:149
  38.0 4.5 %collective-permute-start.3 = (f32[2,32,512]{2,1,0:T(8,128)S(1)}, f32[2,32,512]{2,1,0:T(8,128)S(1)}, u32[]{:S(2)}, u32[]{:S(2)}) collective-permute-start(f32[2,32,512]{2,1,0:T(8,128)S(1)} %maximum_add_fusion), channel_id=1, source_target_pairs={{0,128},{64,448},{128,256},{192,64},{256,384},{320,192},{384,0},{4... | collective-permute-start | bytes 393224 | tf_op jit(solution)/shard_map/ppermute | solution.py:188
  42.5 4.9 %collective-permute-start.2 = (f32[2,32,512]{2,1,0:T(8,128)S(1)}, f32[2,32,512]{2,1,0:T(8,128)S(1)}, u32[]{:S(2)}, u32[]{:S(2)}) collective-permute-start(f32[2,32,512]{2,1,0:T(8,128)S(1)} %maximum_add_fusion), channel_id=1, source_target_pairs={{0,448},{64,0},{128,64},{192,128},{256,192},{320,256},{384,320},{4... | collective-permute-start | bytes 393224 | tf_op jit(solution)/shard_map/ppermute | solution.py:188
  47.5 1.9 %collective-permute-start.1 = (f32[2,32,512]{2,1,0:T(8,128)S(1)}, f32[2,32,512]{2,1,0:T(8,128)S(1)}, u32[]{:S(2)}, u32[]{:S(2)}) collective-permute-start(f32[2,32,512]{2,1,0:T(8,128)S(1)} %maximum_add_fusion), channel_id=1, source_target_pairs={{0,64},{64,128},{128,192},{192,256},{256,320},{320,384},{384,448},... | collective-permute-start | bytes 393224 | tf_op jit(solution)/shard_map/ppermute | solution.py:188
  50.6 4.9 %collective-permute-done.1 = f32[2,32,512]{2,1,0:T(8,128)S(1)} collective-permute-done((f32[2,32,512]{2,1,0:T(8,128)S(1)}, f32[2,32,512]{2,1,0:T(8,128)S(1)}, u32[]{:S(2)}, u32[]{:S(2)}) %collective-permute-start.1) | collective-permute-done | bytes 131104 | tf_op jit(solution)/shard_map/ppermute | solution.py:188
  55.6 1.9 %collective-permute-start.4 = (f32[8,32,512]{2,1,0:T(8,128)S(1)}, f32[8,32,512]{2,1,0:T(8,128)S(1)}, u32[]{:S(2)}, u32[]{:S(2)}) collective-permute-start(f32[8,32,512]{2,1,0:T(8,128)S(1)} %pad_maximum_fusion.near_ref), channel_id=1, source_target_pairs={{0,32},{32,0},{1,33},{33,1},{2,34},{34,2},{3,35},{35,3},{4,36},{36... | collective-permute-start | bytes 1572872 | tf_op jit(solution)/shard_map/ppermute | solution.py:189
  59.4 2.4 %all-to-all-done.1 = f32[4,128,1024]{2,1,0:T(8,128)S(1)} async-done(((f32[4,128,1024]{2,1,0:T(8,128)}), f32[4,128,1024]{2,1,0:T(8,128)S(1)}, u32[]{:S(2)}, u32[]{:S(2)}) %all-to-all-start.1) | async-done | bytes 2097184 | tf_op jit(solution)/shard_map/all_to_all | solution.py:149
  61.8 5.1 %logits.1 = (f32[512,1024]{1,0:T(8,128)S(1)}, f32[32,8,128]{2,1,0:T(8,128)S(1)}, f32[16,8,128]{2,1,0:T(8,128)S(1)}) custom-call(s32[4]{0:T(128)S(1)} %pad_add_fusion.me_ref, s32[4,2]{1,0:T(4,128)S(1)} %fusion.5.allow_ref, f32[512,1024]{1,0:T(8,128)S(1)} %bitcast.30, f32[8,32,512]{2,1,0:T(8,128)S(1)} %pad_maximum_fusion.near_ref, ...), custom_call_target="tpu_custom_call" | custom-call | flops 3221225472 | bytes 5242880 | tf_op jit(solution)/shard_map/logits/pallas_call | solution.py:203
  66.9 14.9 %all_to_all.30.col_ref = f32[16,8,128]{2,1,0:T(8,128)S(1)} all-to-all(f32[16,8,128]{2,1,0:T(8,128)S(1)} %get-tuple-element.9), channel_id=1, replica_groups=mesh['y'=8,'core'=2,'x'=4,'z'=8] {'y','core'}, dimensions={0} | all-to-all | bytes 131072 | tf_op jit(solution)/shard_map/all_to_all | solution.py:217
  81.8 14.0 %all_to_all.31.row_ref = f32[32,8,128]{2,1,0:T(8,128)S(1)} all-to-all(f32[32,8,128]{2,1,0:T(8,128)S(1)} %get-tuple-element.8), channel_id=1, replica_groups=mesh['y'=8,'core'=2,'x'=4,'z'=8] {'x','z'}, dimensions={0} | all-to-all | bytes 262144 | tf_op jit(solution)/shard_map/all_to_all | solution.py:218
  95.8 3.0 %image_terms.1 = f32[512,1024]{1,0:T(8,128)S(1)} custom-call(s32[4]{0:T(128)S(1)} %pad_add_fusion.me_ref, f32[512,1024]{1,0:T(8,128)S(1)} %get-tuple-element.7.logits_ref, f32[32,8,128]{2,1,0:T(8,128)S(1)} %all_to_all.31.row_ref, f32[16,8,128]{2,1,0:T(8,128)S(1)} %all_to_all.30.col_ref, f32[8,32,512]{2,1,0:T(8,128)S(1)} %pad_maximum_fusion.near_ref, ...), custom_call_target="tpu_custom_call" | custom-call | flops 1610612736 | bytes 5242880 | tf_op jit(solution)/shard_map/image_terms/pallas_call | solution.py:219
  98.8 1.3 copy-done.2
  100.2 5.0 %all-to-all-start.4 = ((f32[4,128,1024]{2,1,0:T(8,128)}), f32[4,128,1024]{2,1,0:T(8,128)S(1)}, u32[]{:S(2)}, u32[]{:S(2)}) async-start(f32[4,128,1024]{2,1,0:T(8,128)} %bitcast.32), calls=%async_computation.4 | async-start | bytes 4194304 | tf_op jit(solution)/shard_map/all_to_all | solution.py:240
  105.1 1.6 %copy-done.1 = f32[4,128,1024]{2,1,0:T(8,128)S(1)} copy-done((f32[4,128,1024]{2,1,0:T(8,128)S(1)}, f32[4,128,1024]{2,1,0:T(8,128)}, u32[]{:S(2)}) %copy-start.1) | copy-done | bytes 2097176
  106.7 1.6 %copy-done.4 = f32[512,1024]{1,0:T(8,128)S(1)} copy-done((f32[512,1024]{1,0:T(8,128)S(1)}, f32[512,1024]{1,0:T(8,128)}, u32[]{:S(2)}) %copy-start.4) | copy-done | bytes 2097176
  108.3 2.9 %text_terms.1 = (f32[8,32,512]{2,1,0:T(8,128)S(1)}, f32[8,32,512]{2,1,0:T(8,128)S(1)}) custom-call(s32[4]{0:T(128)S(1)} %pad_add_fusion.me_ref, f32[512,1024]{1,0:T(8,128)S(1)} %copy-done.4, f32[32,8,128]{2,1,0:T(8,128)S(1)} %all_to_all.31.row_ref, f32[16,8,128]{2,1,0:T(8,128)S(1)} %all_to_all.30.col_ref, f32[512,1024]{1,0:T(8,128)S(1)} %bitcast.31), custom_call_target="tpu_custom_call" | custom-call | flops 1610612736 | bytes 5242880 | tf_op jit(solution)/shard_map/text_terms/pallas_call | solution.py:230
  111.2 1.9 %collective-permute-start.5 = (f32[8,32,512]{2,1,0:T(8,128)S(1)}, f32[8,32,512]{2,1,0:T(8,128)S(1)}, u32[]{:S(2)}, u32[]{:S(2)}) collective-permute-start(f32[8,32,512]{2,1,0:T(8,128)S(1)} %get-tuple-element.11), channel_id=1, source_target_pairs={{0,32},{32,0},{1,33},{33,1},{2,34},{34,2},{3,35},{35,3},{4,36},{36... | collective-permute-start | bytes 1572872 | tf_op jit(solution)/shard_map/ppermute | solution.py:241
  113.2 1.9 %collective-permute-done.5 = f32[8,32,512]{2,1,0:T(8,128)S(1)} collective-permute-done((f32[8,32,512]{2,1,0:T(8,128)S(1)}, f32[8,32,512]{2,1,0:T(8,128)S(1)}, u32[]{:S(2)}, u32[]{:S(2)}) %collective-permute-start.5) | collective-permute-done | bytes 524320 | tf_op jit(solution)/shard_map/ppermute | solution.py:241
  115.2 2.5 %collective-permute-start.8 = (f32[2,32,512]{2,1,0:T(8,128)S(1)}, f32[2,32,512]{2,1,0:T(8,128)S(1)}, u32[]{:S(2)}, u32[]{:S(2)}) collective-permute-start(f32[2,32,512]{2,1,0:T(8,128)S(1)} %get-tuple-element.12), channel_id=1, source_target_pairs={{0,128},{64,448},{128,256},{192,64},{256,384},{320,192},{384,0},{4... | collective-permute-start | bytes 393224 | tf_op jit(solution)/shard_map/ppermute | solution.py:243
  117.7 2.3 %collective-permute-start.7 = (f32[2,32,512]{2,1,0:T(8,128)S(1)}, f32[2,32,512]{2,1,0:T(8,128)S(1)}, u32[]{:S(2)}, u32[]{:S(2)}) collective-permute-start(f32[2,32,512]{2,1,0:T(8,128)S(1)} %get-tuple-element.13), channel_id=1, source_target_pairs={{0,448},{64,0},{128,64},{192,128},{256,192},{320,256},{384,320},{4... | collective-permute-start | bytes 393224 | tf_op jit(solution)/shard_map/ppermute | solution.py:243
  120.0 3.6 %collective-permute-start.6 = (f32[2,32,512]{2,1,0:T(8,128)S(1)}, f32[2,32,512]{2,1,0:T(8,128)S(1)}, u32[]{:S(2)}, u32[]{:S(2)}) collective-permute-start(f32[2,32,512]{2,1,0:T(8,128)S(1)} %get-tuple-element.14), channel_id=1, source_target_pairs={{0,64},{64,128},{128,192},{192,256},{256,320},{320,384},{384,448},... | collective-permute-start | bytes 393224 | tf_op jit(solution)/shard_map/ppermute | solution.py:243
  125.4 3.4 %collective-permute-done.6 = f32[2,32,512]{2,1,0:T(8,128)S(1)} collective-permute-done((f32[2,32,512]{2,1,0:T(8,128)S(1)}, f32[2,32,512]{2,1,0:T(8,128)S(1)}, u32[]{:S(2)}, u32[]{:S(2)}) %collective-permute-start.6) | collective-permute-done | bytes 131104 | tf_op jit(solution)/shard_map/ppermute | solution.py:243
  130.0 3.8 %all-to-all-start.5 = ((f32[8,16,1024]{2,1,0:T(8,128)}), f32[8,16,1024]{2,1,0:T(8,128)S(1)}, u32[]{:S(2)}, u32[]{:S(2)}) async-start(f32[8,16,1024]{2,1,0:T(8,128)} %bitcast.13), calls=%async_computation.5 | async-start | bytes 1048576 | tf_op jit(solution)/shard_map/all_to_all | solution.py:247
  133.8 5.6 %collective-permute-start.9 = (f32[32,512]{1,0:T(8,128)S(1)}, f32[32,512]{1,0:T(8,128)S(1)}, u32[]{:S(2)}, u32[]{:S(2)}) collective-permute-start(f32[32,512]{1,0:T(8,128)S(1)} %slice_bitcast_fusion), channel_id=1, source_target_pairs={{0,256},{64,320},{128,384},{192,448},{256,0},{320,64},{384,128},{4... | collective-permute-start | bytes 196616 | tf_op jit(solution)/shard_map/ppermute | solution.py:246
  139.4 4.5 %collective-permute-done.9 = f32[32,512]{1,0:T(8,128)S(1)} collective-permute-done((f32[32,512]{1,0:T(8,128)S(1)}, f32[32,512]{1,0:T(8,128)S(1)}, u32[]{:S(2)}, u32[]{:S(2)}) %collective-permute-start.9) | collective-permute-done | bytes 65568 | tf_op jit(solution)/shard_map/ppermute | solution.py:246
  144.5 5.8 %all-to-all-done.5 = f32[8,16,1024]{2,1,0:T(8,128)S(1)} async-done(((f32[8,16,1024]{2,1,0:T(8,128)}), f32[8,16,1024]{2,1,0:T(8,128)S(1)}, u32[]{:S(2)}, u32[]{:S(2)}) %all-to-all-start.5) | async-done | bytes 524320 | tf_op jit(solution)/shard_map/all_to_all | solution.py:247
  (33 shorter events, 8.7 us)
Async XLA Ops:
  2.3 27.8 %all-to-all-start = ((f32[8,16,1024]{2,1,0:T(8,128)}), f32[8,16,1024]{2,1,0:T(8,128)S(1)}, u32[]{:S(2)}, u32[]{:S(2)}) async-start(f32[8,16,1024]{2,1,0:T(8,128)} %broadcast_in_dim.4), calls=%async_computation | async-start | bytes 1048576 | tf_op jit(solution)/shard_map/all_to_all | solution.py:149
  12.6 10.6 %collective-permute-start = (f32[32,512]{1,0:T(8,128)}, f32[32,512]{1,0:T(8,128)S(1)}, u32[]{:S(2)}, u32[]{:S(2)}) collective-permute-start(f32[32,512]{1,0:T(8,128)} %bitcast.40), channel_id=1, source_target_pairs={{0,256},{64,320},{128,384},{192,448},{256,0},{320,64},{384,128},{4... | collective-permute-start | bytes 196616 | tf_op jit(solution)/shard_map/ppermute | solution.py:184
  31.8 6.2 %copy-start.5 = (f32[512,32]{0,1:T(8,128)S(1)}, f32[512,32]{0,1:T(8,128)}, u32[]{:S(2)}) copy-start(f32[512,32]{0,1:T(8,128)} %param.4) | copy-start | bytes 196612
  31.8 30.0 %all-to-all-start.1 = ((f32[4,128,1024]{2,1,0:T(8,128)}), f32[4,128,1024]{2,1,0:T(8,128)S(1)}, u32[]{:S(2)}, u32[]{:S(2)}) async-start(f32[4,128,1024]{2,1,0:T(8,128)} %broadcast_in_dim.5), calls=%async_computation.1 | async-start | bytes 4194304 | tf_op jit(solution)/shard_map/all_to_all | solution.py:149
  38.0 11.4 %collective-permute-start.3 = (f32[2,32,512]{2,1,0:T(8,128)S(1)}, f32[2,32,512]{2,1,0:T(8,128)S(1)}, u32[]{:S(2)}, u32[]{:S(2)}) collective-permute-start(f32[2,32,512]{2,1,0:T(8,128)S(1)} %maximum_add_fusion), channel_id=1, source_target_pairs={{0,128},{64,448},{128,256},{192,64},{256,384},{320,192},{384,0},{4... | collective-permute-start | bytes 393224 | tf_op jit(solution)/shard_map/ppermute | solution.py:188
  42.5 8.1 %collective-permute-start.2 = (f32[2,32,512]{2,1,0:T(8,128)S(1)}, f32[2,32,512]{2,1,0:T(8,128)S(1)}, u32[]{:S(2)}, u32[]{:S(2)}) collective-permute-start(f32[2,32,512]{2,1,0:T(8,128)S(1)} %maximum_add_fusion), channel_id=1, source_target_pairs={{0,448},{64,0},{128,64},{192,128},{256,192},{320,256},{384,320},{4... | collective-permute-start | bytes 393224 | tf_op jit(solution)/shard_map/ppermute | solution.py:188
  47.5 8.1 %collective-permute-start.1 = (f32[2,32,512]{2,1,0:T(8,128)S(1)}, f32[2,32,512]{2,1,0:T(8,128)S(1)}, u32[]{:S(2)}, u32[]{:S(2)}) collective-permute-start(f32[2,32,512]{2,1,0:T(8,128)S(1)} %maximum_add_fusion), channel_id=1, source_target_pairs={{0,64},{64,128},{128,192},{192,256},{256,320},{320,384},{384,448},... | collective-permute-start | bytes 393224 | tf_op jit(solution)/shard_map/ppermute | solution.py:188
  55.6 3.8 %collective-permute-start.4 = (f32[8,32,512]{2,1,0:T(8,128)S(1)}, f32[8,32,512]{2,1,0:T(8,128)S(1)}, u32[]{:S(2)}, u32[]{:S(2)}) collective-permute-start(f32[8,32,512]{2,1,0:T(8,128)S(1)} %pad_maximum_fusion.near_ref), channel_id=1, source_target_pairs={{0,32},{32,0},{1,33},{33,1},{2,34},{34,2},{3,35},{35,3},{4,36},{36... | collective-permute-start | bytes 1572872 | tf_op jit(solution)/shard_map/ppermute | solution.py:189
  61.8 5.1 %copy-start = (f32[4,128,1024]{2,1,0:T(8,128)}, f32[4,128,1024]{2,1,0:T(8,128)S(1)}, u32[]{:S(2)}) copy-start(f32[4,128,1024]{2,1,0:T(8,128)S(1)} %all-to-all-done.1) | copy-start | bytes 6291460
  66.9 31.9 %copy-start.3 = (f32[512,1024]{1,0:T(8,128)}, f32[512,1024]{1,0:T(8,128)S(1)}, u32[]{:S(2)}) copy-start(f32[512,1024]{1,0:T(8,128)S(1)} %get-tuple-element.7.logits_ref) | copy-start | bytes 6291460
  98.8 1.3 copy-start.2
  100.2 28.8 %all-to-all-start.4 = ((f32[4,128,1024]{2,1,0:T(8,128)}), f32[4,128,1024]{2,1,0:T(8,128)S(1)}, u32[]{:S(2)}, u32[]{:S(2)}) async-start(f32[4,128,1024]{2,1,0:T(8,128)} %bitcast.32), calls=%async_computation.4 | async-start | bytes 4194304 | tf_op jit(solution)/shard_map/all_to_all | solution.py:240
  105.1 1.6 %copy-start.1 = (f32[4,128,1024]{2,1,0:T(8,128)S(1)}, f32[4,128,1024]{2,1,0:T(8,128)}, u32[]{:S(2)}) copy-start(f32[4,128,1024]{2,1,0:T(8,128)} %copy-done) | copy-start | bytes 6291460
  106.7 1.6 %copy-start.4 = (f32[512,1024]{1,0:T(8,128)S(1)}, f32[512,1024]{1,0:T(8,128)}, u32[]{:S(2)}) copy-start(f32[512,1024]{1,0:T(8,128)} %copy-done.3) | copy-start | bytes 6291460
  111.2 3.8 %collective-permute-start.5 = (f32[8,32,512]{2,1,0:T(8,128)S(1)}, f32[8,32,512]{2,1,0:T(8,128)S(1)}, u32[]{:S(2)}, u32[]{:S(2)}) collective-permute-start(f32[8,32,512]{2,1,0:T(8,128)S(1)} %get-tuple-element.11), channel_id=1, source_target_pairs={{0,32},{32,0},{1,33},{33,1},{2,34},{34,2},{3,35},{35,3},{4,36},{36... | collective-permute-start | bytes 1572872 | tf_op jit(solution)/shard_map/ppermute | solution.py:241
  115.2 9.5 %collective-permute-start.8 = (f32[2,32,512]{2,1,0:T(8,128)S(1)}, f32[2,32,512]{2,1,0:T(8,128)S(1)}, u32[]{:S(2)}, u32[]{:S(2)}) collective-permute-start(f32[2,32,512]{2,1,0:T(8,128)S(1)} %get-tuple-element.12), channel_id=1, source_target_pairs={{0,128},{64,448},{128,256},{192,64},{256,384},{320,192},{384,0},{4... | collective-permute-start | bytes 393224 | tf_op jit(solution)/shard_map/ppermute | solution.py:243
  117.7 7.7 %collective-permute-start.7 = (f32[2,32,512]{2,1,0:T(8,128)S(1)}, f32[2,32,512]{2,1,0:T(8,128)S(1)}, u32[]{:S(2)}, u32[]{:S(2)}) collective-permute-start(f32[2,32,512]{2,1,0:T(8,128)S(1)} %get-tuple-element.13), channel_id=1, source_target_pairs={{0,448},{64,0},{128,64},{192,128},{256,192},{320,256},{384,320},{4... | collective-permute-start | bytes 393224 | tf_op jit(solution)/shard_map/ppermute | solution.py:243
  120.0 8.9 %collective-permute-start.6 = (f32[2,32,512]{2,1,0:T(8,128)S(1)}, f32[2,32,512]{2,1,0:T(8,128)S(1)}, u32[]{:S(2)}, u32[]{:S(2)}) collective-permute-start(f32[2,32,512]{2,1,0:T(8,128)S(1)} %get-tuple-element.14), channel_id=1, source_target_pairs={{0,64},{64,128},{128,192},{192,256},{256,320},{320,384},{384,448},... | collective-permute-start | bytes 393224 | tf_op jit(solution)/shard_map/ppermute | solution.py:243
  130.0 20.3 %all-to-all-start.5 = ((f32[8,16,1024]{2,1,0:T(8,128)}), f32[8,16,1024]{2,1,0:T(8,128)S(1)}, u32[]{:S(2)}, u32[]{:S(2)}) async-start(f32[8,16,1024]{2,1,0:T(8,128)} %bitcast.13), calls=%async_computation.5 | async-start | bytes 1048576 | tf_op jit(solution)/shard_map/all_to_all | solution.py:247
  133.8 10.1 %collective-permute-start.9 = (f32[32,512]{1,0:T(8,128)S(1)}, f32[32,512]{1,0:T(8,128)S(1)}, u32[]{:S(2)}, u32[]{:S(2)}) collective-permute-start(f32[32,512]{1,0:T(8,128)S(1)} %slice_bitcast_fusion), channel_id=1, source_target_pairs={{0,256},{64,320},{128,384},{192,448},{256,0},{320,64},{384,128},{4... | collective-permute-start | bytes 196616 | tf_op jit(solution)/shard_map/ppermute | solution.py:246

commit v5 on v4

--- a/solution.py
+++ b/solution.py
@@ -11,7 +11,8 @@
 BLK = 256
 LANES = 128
 NEG = -1e30
-ROW = ("y", "core")
+Y = ("y_far", "y_near")
+ROW = Y + ("core",)
 COL = ("x", "z")
 VMEM = pl.BlockSpec(memory_space=pltpu.VMEM)
 HBM = pl.BlockSpec(memory_space=pltpu.HBM)
@@ -40,13 +41,22 @@
     return total
 
 
-def natural(me_ref, near_ref, far_ref, texts_ref):
+def place(me_ref, there, core, step, chunk):
+    shard = there * 2 + core
+    per = chunk // step
+    apart = (shard // per) ^ me_ref[4]
+    first = 1 + me_ref[0]
+    order = jnp.where(apart == 0, 0, jnp.where(apart == 1, first, jnp.where(apart == 3, 3 - first, 3)))
+    return pl.ds(pl.multiple_of(order * chunk + (shard & (per - 1)) * step, step), step)
+
+
+def arrange(me_ref, near_ref, far_ref, texts_ref):
     n, step, _ = near_ref.shape
     core, y = me_ref[0], me_ref[1]
-    for k, there in enumerate(pairs(y, -1, n)):
+    for k in range(n):
+        there = (((y // (n // 2)) ^ (k % 2)) * (n // 2)) + k // 2
         for other, ref in enumerate((near_ref, far_ref)):
-            at = (there * 2 + (core ^ other)) * step
-            texts_ref[pl.ds(pl.multiple_of(at, step), step), :] = ref[k]
+            texts_ref[place(me_ref, there, core ^ other, step, texts_ref.shape[0] // 4), :] = ref[k]
 
 
 def pairs(y, way, n):
@@ -55,16 +65,18 @@
 
 
 def logits_kernel(
-    me_ref, allow_ref, images_ref, near_ref, far_ref, logits_ref, row_ref, col_ref, texts_ref
+    me_ref, allow_ref, own_ref, first_ref, second_ref, across_ref, near_ref, far_ref, logits_ref, row_ref, col_ref, texts_ref
 ):
-    width, rows = images_ref.shape
-    cols = texts_ref.shape[1]
+    rows = own_ref.shape[1]
+    width, cols = texts_ref.shape
     inv = width ** (-0.5)
-    natural(me_ref, near_ref, far_ref, texts_ref)
+    refs = (own_ref, first_ref, second_ref, across_ref)
+    arrange(me_ref, near_ref, far_ref, texts_ref)
     texts = split(texts_ref[...].T, 3)
     for i in range(rows // BLK):
         at = pl.ds(i * BLK, BLK)
-        part = product(texts, split(images_ref[:, at], 3), NN, 2) * inv
+        images = jnp.concatenate([ref[:, at] for ref in refs])
+        part = product(texts, split(images, 3), NN, 2) * inv
         for j in range(cols // BLK):
             block = jnp.where(allow_ref[i, j] > 0, part[j * BLK : (j + 1) * BLK], NEG)
             logits_ref[pl.ds(j * BLK, BLK), at] = block
@@ -110,39 +122,40 @@
         yield pl.ds(i * BLK, BLK), jnp.where(text_at == image_at, grad - 1.0, grad)
 
 
-def image_kernel(me_ref, logits_ref, row_ref, col_ref, near_ref, far_ref, terms_ref, texts_ref):
+def image_kernel(
+    me_ref, logits_ref, row_ref, col_ref, near_ref, far_ref, own_ref, first_ref, second_ref, across_ref, texts_ref
+):
     inv = texts_ref.shape[0] ** (-0.5)
-    natural(me_ref, near_ref, far_ref, texts_ref)
+    arrange(me_ref, near_ref, far_ref, texts_ref)
     texts = split(texts_ref[...], 2)
+    chunk = own_ref.shape[0]
     for at, grad in gradient(me_ref, logits_ref, row_ref, col_ref):
-        terms_ref[:, at] = product(texts, split(grad, 2), NN, 1) * inv
-
-
-def text_kernel(me_ref, logits_ref, row_ref, col_ref, images_ref, keep_ref, send_ref, all_ref):
-    inv = images_ref.shape[0] ** (-0.5)
+        terms = product(texts, split(grad, 2), NN, 1) * inv
+        for k, ref in enumerate((own_ref, first_ref, second_ref, across_ref)):
+            ref[:, at] = terms[k * chunk : (k + 1) * chunk]
+
+
+def text_kernel(
+    me_ref, logits_ref, row_ref, col_ref, own_ref, first_ref, second_ref, across_ref, keep_ref, send_ref, all_ref
+):
+    inv = all_ref.shape[0] ** (-0.5)
+    refs = (own_ref, first_ref, second_ref, across_ref)
     total = None
     for at, grad in gradient(me_ref, logits_ref, row_ref, col_ref):
-        p = product(split(images_ref[:, at], 2), split(grad, 2), NT, 1)
+        images = jnp.concatenate([ref[:, at] for ref in refs])
+        p = product(split(images, 2), split(grad, 2), NT, 1)
         total = p if total is None else total + p
     all_ref[...] = total * inv
     n, step, _ = keep_ref.shape
     core, y = me_ref[0], me_ref[1]
     for k, there in enumerate(pairs(y, 1, n)):
         for other, ref in enumerate((keep_ref, send_ref)):
-            at = (there * 2 + (core ^ other)) * step
-            ref[k] = all_ref[pl.ds(pl.multiple_of(at, step), step), :]
-
-
-def sum_kernel(parts_in, after_ref, out_ref, parts_ref, sems):
+            ref[k] = all_ref[place(me_ref, there, core ^ other, step, own_ref.shape[0]), :]
+
+
+def sum_kernel(a_ref, b_ref, c_ref, after_ref, out_ref):
     del after_ref
-    loads = [
-        pltpu.make_async_copy(parts_in.at[k], parts_ref.at[k], sems.at[k]) for k in range(parts_in.shape[0])
-    ]
-    for load in loads:
-        load.start()
-    for load in loads:
-        load.wait()
-    out_ref[...] = jnp.sum(parts_ref[...], axis=0)
+    out_ref[...] = a_ref[...] + b_ref[...] + c_ref[...]
 
 
 def gather(block, axis, n):
@@ -150,18 +163,17 @@
 
 
 def after(x, y):
-    return x + 0.0 * y.reshape(-1)[0]
-
-
-def sum_of(parts, after):
+    return x + 0.0 * y[(0,) * y.ndim]
+
+
+def sum_of(a, b, c, then):
     return pl.pallas_call(
         sum_kernel,
-        out_shape=jax.ShapeDtypeStruct(parts.shape[1:], parts.dtype),
-        in_specs=[ANY, ANY],
-        scratch_shapes=[pltpu.VMEM(parts.shape, parts.dtype), pltpu.SemaphoreType.DMA((parts.shape[0],))],
+        out_shape=jax.ShapeDtypeStruct(a.shape, a.dtype),
+        in_specs=[VMEM, VMEM, VMEM, ANY],
         compiler_params=PARAMS,
         name="sum",
-    )(parts, after)
+    )(a, b, c, then)
 
 
 def flip(n, bit):
@@ -176,18 +188,31 @@
     ]
 
 
+def neighbours(nx, nc):
+    first, second = (1, 3), (3, 1)
+    return [
+        [(c * nx + x, c * nx + (x ^ apart[c])) for c in range(nc) for x in range(nx)]
+        for apart in (first, second)
+    ]
+
+
 def body(image_embeddings, text_embeddings, negatives_mask):
-    ny, nc, nx, nz = (lax.axis_size(a) for a in ("y", "core", "x", "z"))
+    ny, nc, nx, nz = (lax.axis_size(a) for a in (Y, "core", "x", "z"))
     rows, own = image_embeddings.shape
     cols, own_text = text_embeddings.shape
     texts = text_embeddings.T
-    far_half = lax.ppermute(texts, "y", flip(ny, ny // 2))
+    far_half = lax.ppermute(texts, Y, flip(ny, ny // 2))
     images = gather(image_embeddings.T, "z", nz).reshape(nz * own, rows)
     texts = after(jnp.stack([texts, far_half]), images)
-    images = gather(after(images, far_half), "x", nx).reshape(nx * nz * own, rows)
-    near = jnp.concatenate([texts] + [lax.ppermute(texts, "y", perm) for perm in shifts(ny)])
-    far = lax.ppermute(near, "core", flip(nc, 1))
-    width = images.shape[0]
+    images = after(images, far_half)
+    to_first, to_second = neighbours(nx, nc)
+    first = lax.ppermute(images, ("core", "x"), to_first)
+    second = lax.ppermute(images, ("core", "x"), to_second)
+    across = lax.ppermute(first, ("core", "x"), to_second)
+    images = (images, first, second, across)
+    near = gather(texts, "y_near", ny // 2).reshape(ny, own_text, cols)
+    far = lax.ppermute(after(near, across), "core", flip(nc, 1))
+    width = nx * nz * own
     row_start = lax.axis_index(ROW) * rows
     col_start = lax.axis_index(COL) * cols
     row_blocks, col_blocks = rows // BLK, cols // BLK
@@ -198,7 +223,7 @@
     allow = ((window > 0) | (row_ids[:, None] == col_ids[None, :])).astype(jnp.int32)
     f32 = jnp.float32
     passes = 2 * rows * cols * width
-    me = [lax.axis_index("core"), lax.axis_index("y"), row_start, col_start]
+    me = [lax.axis_index("core"), lax.axis_index(Y), row_start, col_start, lax.axis_index("x")]
     me = jnp.stack(me).astype(jnp.int32)
     logits, row_parts, col_parts = pl.pallas_call(
         logits_kernel,
@@ -207,20 +232,20 @@
             jax.ShapeDtypeStruct((nx * nz, rows // LANES, LANES), f32),
             jax.ShapeDtypeStruct((ny * nc, rows // LANES, LANES), f32),
         ),
-        in_specs=[SMEM, SMEM, VMEM, VMEM, VMEM],
+        in_specs=[SMEM, SMEM] + [VMEM] * 6,
         out_specs=(VMEM, VMEM, VMEM),
         scratch_shapes=[pltpu.VMEM((width, cols), f32)],
         compiler_params=PARAMS,
         cost_estimate=pl.CostEstimate(flops=6 * passes, bytes_accessed=5 << 20, transcendentals=0),
         name="logits",
-    )(me, allow, images, near, far)
+    )(me, allow, *images, near, far)
     col_parts = lax.all_to_all(col_parts, ROW, 0, 0)
     row_parts = lax.all_to_all(row_parts, COL, 0, 0)
-    image_terms = pl.pallas_call(
+    own_terms, first, second, across = pl.pallas_call(
         image_kernel,
-        out_shape=jax.ShapeDtypeStruct((width, rows), f32),
-        in_specs=[SMEM, VMEM, VMEM, VMEM, VMEM, VMEM],
-        out_specs=VMEM,
+        out_shape=(jax.ShapeDtypeStruct((nz * own, rows), f32),) * 4,
+        in_specs=[SMEM] + [VMEM] * 5,
+        out_specs=(VMEM,) * 4,
         scratch_shapes=[pltpu.VMEM((width, cols), f32)],
         compiler_params=PARAMS,
         cost_estimate=pl.CostEstimate(flops=3 * passes, bytes_accessed=5 << 20, transcendentals=0),
@@ -230,27 +255,29 @@
     keep, send = pl.pallas_call(
         text_kernel,
         out_shape=(half, half),
-        in_specs=[SMEM, VMEM, VMEM, VMEM, VMEM],
+        in_specs=[SMEM] + [VMEM] * 7,
         out_specs=(VMEM, VMEM),
         scratch_shapes=[pltpu.VMEM((width, cols), f32)],
         compiler_params=PARAMS,
         cost_estimate=pl.CostEstimate(flops=3 * passes, bytes_accessed=5 << 20, transcendentals=0),
         name="text_terms",
-    )(me, logits, row_parts, col_parts, images)
-    parts = lax.all_to_all(image_terms.reshape(nx, nz * own, rows), "x", 0, 0)
+    )(me, logits, row_parts, col_parts, *images)
+    across = lax.ppermute(across, ("core", "x"), to_second)
+    second = lax.ppermute(second, ("core", "x"), to_second)
+    first = lax.ppermute(first + across, ("core", "x"), to_first)
     grad_text = keep + lax.ppermute(send, "core", flip(nc, 1))
     grad_text = grad_text.reshape(4, 2, own_text, cols)
-    moved = [lax.ppermute(grad_text[k + 1], "y", perm) for k, perm in enumerate(shifts(ny))]
-    parts = sum_of(parts, moved[0] + moved[1])
+    moved = [lax.ppermute(grad_text[k + 1], Y, perm) for k, perm in enumerate(shifts(ny))]
+    parts = sum_of(own_terms, first, second, moved[0] + moved[1])
     grad_text = sum(moved, grad_text[0])
-    grad_text = grad_text[0] + lax.ppermute(grad_text[1], "y", flip(ny, ny // 2))
+    grad_text = grad_text[0] + lax.ppermute(grad_text[1], Y, flip(ny, ny // 2))
     grad_image = jnp.sum(lax.all_to_all(parts.reshape(nz, own, rows), "z", 0, 0), axis=0)
     return (grad_image.T, grad_text.T)
 
 
 def solution(mesh):
     rows, cols = mesh.devices.shape
-    fine = Mesh(mesh.devices.reshape(rows // 2, 2, 4, cols // 4), ("y", "core", "x", "z"))
+    fine = Mesh(mesh.devices.reshape(2, rows // 4, 2, 4, cols // 4), ROW + COL)
     return jax.shard_map(
         body,
         mesh=fine,

time: 152 us -> 150 us (0.987)
  local copies, waits for them, and re-layouts: 8.98 us -> 4.26 us
    ppermute x9 -> x12, starting transfers between devices: 34.9 us -> 40.7 us  [the longest x3 8.3 us: body(): lax.ppermute(grad_text[k + 1], Y, perm)]
    all_to_all x1 -> x0, starting transfers between devices: 4.98 us -> none  [body(): parts = lax.all_to_all(image_terms.reshape(nx, nz * own, rows), 'x', 0, 0)]
    unnamed x14 -> x2, local copies, waits for them, and re-layouts: 4.63 us -> 0.01 us
    ppermute x9 -> x12, waiting for transfers between devices: 19.8 us -> 23.7 us  [the longest x1 6.64 us: body(): grad_text = grad_text[0] + lax.ppermute(grad_text[1], Y, flip(ny, ny // 2))]
    ppermute x1, waiting for transfers between devices: 1.88 us -> 0.01 us  [body(): grad_text = keep + lax.ppermute(send, 'core', flip(nc, 1))]
  transfers between devices with their start and end apart: 14 -> 16, of which waited for: 13 -> 11; matrix products, arithmetic and copies ran while one was open for 2% -> 3% of each run, Pallas kernels for 2% -> 2%
where the time goes in v5:
time: 150 us; the launch traced here: 149 us
  starting transfers between devices  61.3 us (41%)
  waiting for transfers between devices  36.2 us (24%)
  blocking collectives  28.8 us (19%)
  Pallas kernels  12.2 us (8%)
  local copies, waits for them, and re-layouts  4.26 us (3%)
  other arithmetic  3.17 us (2%)
  between operations  2.87 us (2%)
    all_to_all x2, starting transfers between devices, gather(): lax.all_to_all(jnp.broadcast_to(block[None], (n,) + block.shape), axis, 0...  15.2 us
    all_to_all x1, blocking collectives, body(): row_parts = lax.all_to_all(row_parts, COL, 0, 0)  15.1 us
    all_to_all x1, blocking collectives, body(): col_parts = lax.all_to_all(col_parts, ROW, 0, 0)  13.7 us
    ppermute x3, starting transfers between devices, body(): lax.ppermute(grad_text[k + 1], Y, perm)  8.3 us
    ppermute x1, starting transfers between devices, body(): far_half = lax.ppermute(texts, Y, flip(ny, ny // 2))  7.72 us
    all_to_all x2, waiting for transfers between devices, gather(): lax.all_to_all(jnp.broadcast_to(block[None], (n,) + block.shape), axis, 0...  7.17 us
    ppermute x1, waiting for transfers between devices, body(): grad_text = grad_text[0] + lax.ppermute(grad_text[1], Y, flip(ny, ny // 2))  6.64 us
    ppermute x3, waiting for transfers between devices, body(): lax.ppermute(grad_text[k + 1], Y, perm)  5.82 us
  transfers between devices with their start and end apart: 16, of which 11 were waited for; matrix products, arithmetic and copies ran while one was open for 3% of the time, Pallas kernels for 2%

profile of v5, /device:TPU:2, one launch (start us, length us, event | category | flops | bytes accessed | tf_op | source)
XLA Modules:
  0.0 148.7 jit_solution(9896279121905306460)
XLA Ops:
  0.6 1.7 %broadcast_in_dim.4 = f32[8,16,1024]{2,1,0:T(8,128)} broadcast(f32[16,1024]{1,0:T(8,128)} %bitcast.32), dimensions={1,2} | broadcast | bytes 589824 | tf_op jit(solution)/shard_map/broadcast_in_dim | solution.py:162
  2.4 10.3 %all-to-all-start = ((f32[8,16,1024]{2,1,0:T(8,128)}), f32[8,16,1024]{2,1,0:T(8,128)S(1)}, u32[]{:S(2)}, u32[]{:S(2)}) async-start(f32[8,16,1024]{2,1,0:T(8,128)} %broadcast_in_dim.4), calls=%async_computation | async-start | bytes 1048576 | tf_op jit(solution)/shard_map/all_to_all | solution.py:162
  12.7 7.7 %collective-permute-start = (f32[32,512]{1,0:T(8,128)}, f32[32,512]{1,0:T(8,128)S(1)}, u32[]{:S(2)}, u32[]{:S(2)}) collective-permute-start(f32[32,512]{1,0:T(8,128)} %bitcast.33), channel_id=1, source_target_pairs={{0,256},{64,320},{128,384},{192,448},{256,0},{320,64},{384,128},{4... | collective-permute-start | bytes 196616 | tf_op jit(solution)/shard_map/ppermute | solution.py:204
  20.4 2.9 %collective-permute-done = f32[32,512]{1,0:T(8,128)S(1)} collective-permute-done((f32[32,512]{1,0:T(8,128)}, f32[32,512]{1,0:T(8,128)S(1)}, u32[]{:S(2)}, u32[]{:S(2)}) %collective-permute-start) | collective-permute-done | bytes 65568 | tf_op jit(solution)/shard_map/ppermute | solution.py:204
  24.5 5.7 %all-to-all-done = f32[8,16,1024]{2,1,0:T(8,128)S(1)} async-done(((f32[8,16,1024]{2,1,0:T(8,128)}), f32[8,16,1024]{2,1,0:T(8,128)S(1)}, u32[]{:S(2)}, u32[]{:S(2)}) %all-to-all-start) | async-done | bytes 524320 | tf_op jit(solution)/shard_map/all_to_all | solution.py:162
  30.2 2.4 %collective-permute-start.1 = (f32[128,1024]{1,0:T(8,128)S(1)}, f32[128,1024]{1,0:T(8,128)S(1)}, u32[]{:S(2)}, u32[]{:S(2)}) collective-permute-start(f32[128,1024]{1,0:T(8,128)S(1)} %broadcast_add_fusion.1.own_ref), channel_id=1, source_target_pairs={{0,8},{8,0},{16,24},{24,16},{32,56},{40,48},{48,40},{56,32},{1,9},... | collective-permute-start | bytes 1572872 | tf_op jit(solution)/shard_map/ppermute | solution.py:209
  34.7 4.9 %all-to-all-start.1 = ((f32[4,2,32,512]{3,2,1,0:T(8,128)}), f32[4,2,32,512]{3,2,1,0:T(8,128)S(1)}, u32[]{:S(2)}, u32[]{:S(2)}) async-start(f32[4,2,32,512]{3,2,1,0:T(8,128)} %broadcast_in_dim.5), calls=%async_computation.1 | async-start | bytes 1048576 | tf_op jit(solution)/shard_map/all_to_all | solution.py:162
  39.6 1.7 %collective-permute-done.1.first_ref = f32[128,1024]{1,0:T(8,128)S(1)} collective-permute-done((f32[128,1024]{1,0:T(8,128)S(1)}, f32[128,1024]{1,0:T(8,128)S(1)}, u32[]{:S(2)}, u32[]{:S(2)}) %collective-permute-start.1) | collective-permute-done | bytes 524320 | tf_op jit(solution)/shard_map/ppermute | solution.py:209
  41.3 3.4 %collective-permute-start.3 = (f32[128,1024]{1,0:T(8,128)S(1)}, f32[128,1024]{1,0:T(8,128)S(1)}, u32[]{:S(2)}, u32[]{:S(2)}) collective-permute-start(f32[128,1024]{1,0:T(8,128)S(1)} %collective-permute-done.1.first_ref), channel_id=1, source_target_pairs={{0,24},{8,16},{16,8},{24,0},{32,40},{40,32},{48,56},{56,48},{1,25}... | collective-permute-start | bytes 1572872 | tf_op jit(solution)/shard_map/ppermute | solution.py:211
  44.7 2.4 %collective-permute-start.2 = (f32[128,1024]{1,0:T(8,128)S(1)}, f32[128,1024]{1,0:T(8,128)S(1)}, u32[]{:S(2)}, u32[]{:S(2)}) collective-permute-start(f32[128,1024]{1,0:T(8,128)S(1)} %broadcast_add_fusion.1.own_ref), channel_id=1, source_target_pairs={{0,24},{8,16},{16,8},{24,0},{32,40},{40,32},{48,56},{56,48},{1,25}... | collective-permute-start | bytes 1572872 | tf_op jit(solution)/shard_map/ppermute | solution.py:210
  47.1 5.2 %collective-permute-done.3.across_ref = f32[128,1024]{1,0:T(8,128)S(1)} collective-permute-done((f32[128,1024]{1,0:T(8,128)S(1)}, f32[128,1024]{1,0:T(8,128)S(1)}, u32[]{:S(2)}, u32[]{:S(2)}) %collective-permute-start.3) | collective-permute-done | bytes 524320 | tf_op jit(solution)/shard_map/ppermute | solution.py:211
  53.5 1.4 all-to-all-done.1
  55.8 1.9 %collective-permute-start.4 = (f32[8,32,512]{2,1,0:T(8,128)}, f32[8,32,512]{2,1,0:T(8,128)S(1)}, u32[]{:S(2)}, u32[]{:S(2)}) collective-permute-start(f32[8,32,512]{2,1,0:T(8,128)} %broadcast_add_fusion), channel_id=1, source_target_pairs={{0,32},{32,0},{1,33},{33,1},{2,34},{34,2},{3,35},{35,3},{4,36},{36... | collective-permute-start | bytes 1572872 | tf_op jit(solution)/shard_map/ppermute | solution.py:214
  58.7 1.2 collective-permute-done.4.far_ref
  59.8 5.2 %logits.1 = (f32[512,1024]{1,0:T(8,128)S(1)}, f32[32,8,128]{2,1,0:T(8,128)S(1)}, f32[16,8,128]{2,1,0:T(8,128)S(1)}) custom-call(s32[5]{0:T(128)S(1)} %stack.32.me_ref, s32[4,2]{1,0:T(4,128)S(1)} %fusion.5.allow_ref, f32[128,1024]{1,0:T(8,128)S(1)} %broadcast_add_fusion.1.own_ref, f32[128,1024]{1,0:T(8,128)S(1)} %collective-permute-done.1.first_ref, ...), custom_call_target="tpu_custom_call" | custom-call | flops 3221225472 | bytes 5242880 | tf_op jit(solution)/shard_map/logits/pallas_call | solution.py:228
  65.1 13.7 %all_to_all.25.col_ref = f32[16,8,128]{2,1,0:T(8,128)S(1)} all-to-all(f32[16,8,128]{2,1,0:T(8,128)S(1)} %get-tuple-element.13), channel_id=1, replica_groups=mesh['y_far'=2,'y_near'=4,'core'=2,'x'=4,'z'=8] {'y_far','y_near','core'}, dimensions={0} | all-to-all | bytes 131072 | tf_op jit(solution)/shard_map/all_to_all | solution.py:242
  78.8 15.1 %all_to_all.26.row_ref = f32[32,8,128]{2,1,0:T(8,128)S(1)} all-to-all(f32[32,8,128]{2,1,0:T(8,128)S(1)} %get-tuple-element.12), channel_id=1, replica_groups=mesh['y_far'=2,'y_near'=4,'core'=2,'x'=4,'z'=8] {'x','z'}, dimensions={0} | all-to-all | bytes 262144 | tf_op jit(solution)/shard_map/all_to_all | solution.py:243
  93.9 3.1 %image_terms.1 = (f32[128,1024]{1,0:T(8,128)S(1)}, f32[128,1024]{1,0:T(8,128)S(1)}, f32[128,1024]{1,0:T(8,128)S(1)}, f32[128,1024]{1,0:T(8,128)S(1)}) custom-call(s32[5]{0:T(128)S(1)} %stack.32.me_ref, f32[512,1024]{1,0:T(8,128)S(1)} %get-tuple-element.11.logits_ref, f32[32,8,128]{2,1,0:T(8,128)S(1)} %all_to_all.26.row_ref, ...), custom_call_target="tpu_custom_call" | custom-call | flops 1610612736 | bytes 5242880 | tf_op jit(solution)/shard_map/image_terms/pallas_call | solution.py:244
  96.9 2.7 %collective-permute-start.5 = (f32[128,1024]{1,0:T(8,128)S(1)}, f32[128,1024]{1,0:T(8,128)S(1)}, u32[]{:S(2)}, u32[]{:S(2)}) collective-permute-start(f32[128,1024]{1,0:T(8,128)S(1)} %get-tuple-element.16), channel_id=1, source_target_pairs={{0,24},{8,16},{16,8},{24,0},{32,40},{40,32},{48,56},{56,48},{1,25}... | collective-permute-start | bytes 1572872 | tf_op jit(solution)/shard_map/ppermute | solution.py:265
  99.7 3.0 %text_terms.1 = (f32[8,32,512]{2,1,0:T(8,128)S(1)}, f32[8,32,512]{2,1,0:T(8,128)S(1)}) custom-call(s32[5]{0:T(128)S(1)} %stack.32.me_ref, f32[512,1024]{1,0:T(8,128)S(1)} %get-tuple-element.11.logits_ref, f32[32,8,128]{2,1,0:T(8,128)S(1)} %all_to_all.26.row_ref, f32[16,8,128]{2,1,0:T(8,128)S(1)} %all_to_all.25.col_ref, ...), custom_call_target="tpu_custom_call" | custom-call | flops 1610612736 | bytes 5242880 | tf_op jit(solution)/shard_map/text_terms/pallas_call | solution.py:255
  102.7 1.9 %collective-permute-start.8 = (f32[8,32,512]{2,1,0:T(8,128)S(1)}, f32[8,32,512]{2,1,0:T(8,128)S(1)}, u32[]{:S(2)}, u32[]{:S(2)}) collective-permute-start(f32[8,32,512]{2,1,0:T(8,128)S(1)} %get-tuple-element.19), channel_id=1, source_target_pairs={{0,32},{32,0},{1,33},{33,1},{2,34},{34,2},{3,35},{35,3},{4,36},{36... | collective-permute-start | bytes 1572872 | tf_op jit(solution)/shard_map/ppermute | solution.py:268
  104.6 3.1 %collective-permute-start.7 = (f32[128,1024]{1,0:T(8,128)S(1)}, f32[128,1024]{1,0:T(8,128)S(1)}, u32[]{:S(2)}, u32[]{:S(2)}) collective-permute-start(f32[128,1024]{1,0:T(8,128)S(1)} %get-tuple-element.17), channel_id=1, source_target_pairs={{0,24},{8,16},{16,8},{24,0},{32,40},{40,32},{48,56},{56,48},{1,25}... | collective-permute-start | bytes 1572872 | tf_op jit(solution)/shard_map/ppermute | solution.py:266
  108.1 4.5 %collective-permute-start.6 = (f32[128,1024]{1,0:T(8,128)S(1)}, f32[128,1024]{1,0:T(8,128)S(1)}, u32[]{:S(2)}, u32[]{:S(2)}) collective-permute-start(f32[128,1024]{1,0:T(8,128)S(1)} %add.99), channel_id=1, source_target_pairs={{0,8},{8,0},{16,24},{24,16},{32,56},{40,48},{48,40},{56,32},{1,9},... | collective-permute-start | bytes 1572872 | tf_op jit(solution)/shard_map/ppermute | solution.py:267
  112.8 2.3 %collective-permute-start.10 = (f32[2,32,512]{2,1,0:T(8,128)S(1)}, f32[2,32,512]{2,1,0:T(8,128)S(1)}, u32[]{:S(2)}, u32[]{:S(2)}) collective-permute-start(f32[2,32,512]{2,1,0:T(8,128)S(1)} %get-tuple-element.21), channel_id=1, source_target_pairs={{0,448},{64,0},{128,64},{192,128},{256,192},{320,256},{384,320},{4... | collective-permute-start | bytes 393224 | tf_op jit(solution)/shard_map/ppermute | solution.py:270
  115.1 3.5 %collective-permute-start.11 = (f32[2,32,512]{2,1,0:T(8,128)S(1)}, f32[2,32,512]{2,1,0:T(8,128)S(1)}, u32[]{:S(2)}, u32[]{:S(2)}) collective-permute-start(f32[2,32,512]{2,1,0:T(8,128)S(1)} %get-tuple-element.20), channel_id=1, source_target_pairs={{0,128},{64,448},{128,256},{192,64},{256,384},{320,192},{384,0},{4... | collective-permute-start | bytes 393224 | tf_op jit(solution)/shard_map/ppermute | solution.py:270
  118.6 2.5 %collective-permute-start.9 = (f32[2,32,512]{2,1,0:T(8,128)S(1)}, f32[2,32,512]{2,1,0:T(8,128)S(1)}, u32[]{:S(2)}, u32[]{:S(2)}) collective-permute-start(f32[2,32,512]{2,1,0:T(8,128)S(1)} %get-tuple-element.22), channel_id=1, source_target_pairs={{0,64},{64,128},{128,192},{192,256},{256,320},{320,384},{384,448},... | collective-permute-start | bytes 393224 | tf_op jit(solution)/shard_map/ppermute | solution.py:270
  121.1 4.2 %collective-permute-done.11 = f32[2,32,512]{2,1,0:T(8,128)S(1)} collective-permute-done((f32[2,32,512]{2,1,0:T(8,128)S(1)}, f32[2,32,512]{2,1,0:T(8,128)S(1)}, u32[]{:S(2)}, u32[]{:S(2)}) %collective-permute-start.11) | collective-permute-done | bytes 131104 | tf_op jit(solution)/shard_map/ppermute | solution.py:270
  125.3 1.6 %collective-permute-done.9 = f32[2,32,512]{2,1,0:T(8,128)S(1)} collective-permute-done((f32[2,32,512]{2,1,0:T(8,128)S(1)}, f32[2,32,512]{2,1,0:T(8,128)S(1)}, u32[]{:S(2)}, u32[]{:S(2)}) %collective-permute-start.9) | collective-permute-done | bytes 131104 | tf_op jit(solution)/shard_map/ppermute | solution.py:270
  127.9 3.5 %all-to-all-start.4 = ((f32[8,16,1024]{2,1,0:T(8,128)}), f32[8,16,1024]{2,1,0:T(8,128)S(1)}, u32[]{:S(2)}, u32[]{:S(2)}) async-start(f32[8,16,1024]{2,1,0:T(8,128)} %bitcast.14), calls=%async_computation.4 | async-start | bytes 1048576 | tf_op jit(solution)/shard_map/all_to_all | solution.py:274
  131.4 4.1 %collective-permute-start.12 = (f32[32,512]{1,0:T(8,128)S(1)}, f32[32,512]{1,0:T(8,128)S(1)}, u32[]{:S(2)}, u32[]{:S(2)}) collective-permute-start(f32[32,512]{1,0:T(8,128)S(1)} %slice_bitcast_fusion), channel_id=1, source_target_pairs={{0,256},{64,320},{128,384},{192,448},{256,0},{320,64},{384,128},{4... | collective-permute-start | bytes 196616 | tf_op jit(solution)/shard_map/ppermute | solution.py:273
  135.5 6.6 %collective-permute-done.12 = f32[32,512]{1,0:T(8,128)S(1)} collective-permute-done((f32[32,512]{1,0:T(8,128)S(1)}, f32[32,512]{1,0:T(8,128)S(1)}, u32[]{:S(2)}, u32[]{:S(2)}) %collective-permute-start.12) | collective-permute-done | bytes 65568 | tf_op jit(solution)/shard_map/ppermute | solution.py:273
  142.8 5.3 %all-to-all-done.4 = f32[8,16,1024]{2,1,0:T(8,128)S(1)} async-done(((f32[8,16,1024]{2,1,0:T(8,128)}), f32[8,16,1024]{2,1,0:T(8,128)S(1)}, u32[]{:S(2)}, u32[]{:S(2)}) %all-to-all-start.4) | async-done | bytes 524320 | tf_op jit(solution)/shard_map/all_to_all | solution.py:274
  (27 shorter events, 6.9 us)
Async XLA Ops:
  0.6 33.2 %copy-start = (f32[512,32]{0,1:T(8,128)S(1)}, f32[512,32]{0,1:T(8,128)}, u32[]{:S(2)}) copy-start(f32[512,32]{0,1:T(8,128)} %param.4) | copy-start | bytes 196612
  2.4 27.8 %all-to-all-start = ((f32[8,16,1024]{2,1,0:T(8,128)}), f32[8,16,1024]{2,1,0:T(8,128)S(1)}, u32[]{:S(2)}, u32[]{:S(2)}) async-start(f32[8,16,1024]{2,1,0:T(8,128)} %broadcast_in_dim.4), calls=%async_computation | async-start | bytes 1048576 | tf_op jit(solution)/shard_map/all_to_all | solution.py:162
  12.7 10.6 %collective-permute-start = (f32[32,512]{1,0:T(8,128)}, f32[32,512]{1,0:T(8,128)S(1)}, u32[]{:S(2)}, u32[]{:S(2)}) collective-permute-start(f32[32,512]{1,0:T(8,128)} %bitcast.33), channel_id=1, source_target_pairs={{0,256},{64,320},{128,384},{192,448},{256,0},{320,64},{384,128},{4... | collective-permute-start | bytes 196616 | tf_op jit(solution)/shard_map/ppermute | solution.py:204
  30.2 11.1 %collective-permute-start.1 = (f32[128,1024]{1,0:T(8,128)S(1)}, f32[128,1024]{1,0:T(8,128)S(1)}, u32[]{:S(2)}, u32[]{:S(2)}) collective-permute-start(f32[128,1024]{1,0:T(8,128)S(1)} %broadcast_add_fusion.1.own_ref), channel_id=1, source_target_pairs={{0,8},{8,0},{16,24},{24,16},{32,56},{40,48},{48,40},{56,32},{1,9},... | collective-permute-start | bytes 1572872 | tf_op jit(solution)/shard_map/ppermute | solution.py:209
  34.7 20.2 %all-to-all-start.1 = ((f32[4,2,32,512]{3,2,1,0:T(8,128)}), f32[4,2,32,512]{3,2,1,0:T(8,128)S(1)}, u32[]{:S(2)}, u32[]{:S(2)}) async-start(f32[4,2,32,512]{3,2,1,0:T(8,128)} %broadcast_in_dim.5), calls=%async_computation.1 | async-start | bytes 1048576 | tf_op jit(solution)/shard_map/all_to_all | solution.py:162
  41.3 11.1 %collective-permute-start.3 = (f32[128,1024]{1,0:T(8,128)S(1)}, f32[128,1024]{1,0:T(8,128)S(1)}, u32[]{:S(2)}, u32[]{:S(2)}) collective-permute-start(f32[128,1024]{1,0:T(8,128)S(1)} %collective-permute-done.1.first_ref), channel_id=1, source_target_pairs={{0,24},{8,16},{16,8},{24,0},{32,40},{40,32},{48,56},{56,48},{1,25}... | collective-permute-start | bytes 1572872 | tf_op jit(solution)/shard_map/ppermute | solution.py:211
  44.7 14.0 %collective-permute-start.2 = (f32[128,1024]{1,0:T(8,128)S(1)}, f32[128,1024]{1,0:T(8,128)S(1)}, u32[]{:S(2)}, u32[]{:S(2)}) collective-permute-start(f32[128,1024]{1,0:T(8,128)S(1)} %broadcast_add_fusion.1.own_ref), channel_id=1, source_target_pairs={{0,24},{8,16},{16,8},{24,0},{32,40},{40,32},{48,56},{56,48},{1,25}... | collective-permute-start | bytes 1572872 | tf_op jit(solution)/shard_map/ppermute | solution.py:210
  55.8 4.0 %collective-permute-start.4 = (f32[8,32,512]{2,1,0:T(8,128)}, f32[8,32,512]{2,1,0:T(8,128)S(1)}, u32[]{:S(2)}, u32[]{:S(2)}) collective-permute-start(f32[8,32,512]{2,1,0:T(8,128)} %broadcast_add_fusion), channel_id=1, source_target_pairs={{0,32},{32,0},{1,33},{33,1},{2,34},{34,2},{3,35},{35,3},{4,36},{36... | collective-permute-start | bytes 1572872 | tf_op jit(solution)/shard_map/ppermute | solution.py:214
  96.9 11.1 %collective-permute-start.5 = (f32[128,1024]{1,0:T(8,128)S(1)}, f32[128,1024]{1,0:T(8,128)S(1)}, u32[]{:S(2)}, u32[]{:S(2)}) collective-permute-start(f32[128,1024]{1,0:T(8,128)S(1)} %get-tuple-element.16), channel_id=1, source_target_pairs={{0,24},{8,16},{16,8},{24,0},{32,40},{40,32},{48,56},{56,48},{1,25}... | collective-permute-start | bytes 1572872 | tf_op jit(solution)/shard_map/ppermute | solution.py:265
  102.7 10.0 %collective-permute-start.8 = (f32[8,32,512]{2,1,0:T(8,128)S(1)}, f32[8,32,512]{2,1,0:T(8,128)S(1)}, u32[]{:S(2)}, u32[]{:S(2)}) collective-permute-start(f32[8,32,512]{2,1,0:T(8,128)S(1)} %get-tuple-element.19), channel_id=1, source_target_pairs={{0,32},{32,0},{1,33},{33,1},{2,34},{34,2},{3,35},{35,3},{4,36},{36... | collective-permute-start | bytes 1572872 | tf_op jit(solution)/shard_map/ppermute | solution.py:268
  104.6 22.4 %collective-permute-start.7 = (f32[128,1024]{1,0:T(8,128)S(1)}, f32[128,1024]{1,0:T(8,128)S(1)}, u32[]{:S(2)}, u32[]{:S(2)}) collective-permute-start(f32[128,1024]{1,0:T(8,128)S(1)} %get-tuple-element.17), channel_id=1, source_target_pairs={{0,24},{8,16},{16,8},{24,0},{32,40},{40,32},{48,56},{56,48},{1,25}... | collective-permute-start | bytes 1572872 | tf_op jit(solution)/shard_map/ppermute | solution.py:266
  108.1 18.9 %collective-permute-start.6 = (f32[128,1024]{1,0:T(8,128)S(1)}, f32[128,1024]{1,0:T(8,128)S(1)}, u32[]{:S(2)}, u32[]{:S(2)}) collective-permute-start(f32[128,1024]{1,0:T(8,128)S(1)} %add.99), channel_id=1, source_target_pairs={{0,8},{8,0},{16,24},{24,16},{32,56},{40,48},{48,40},{56,32},{1,9},... | collective-permute-start | bytes 1572872 | tf_op jit(solution)/shard_map/ppermute | solution.py:267
  112.8 8.3 %collective-permute-start.10 = (f32[2,32,512]{2,1,0:T(8,128)S(1)}, f32[2,32,512]{2,1,0:T(8,128)S(1)}, u32[]{:S(2)}, u32[]{:S(2)}) collective-permute-start(f32[2,32,512]{2,1,0:T(8,128)S(1)} %get-tuple-element.21), channel_id=1, source_target_pairs={{0,448},{64,0},{128,64},{192,128},{256,192},{320,256},{384,320},{4... | collective-permute-start | bytes 393224 | tf_op jit(solution)/shard_map/ppermute | solution.py:270
  115.1 10.2 %collective-permute-start.11 = (f32[2,32,512]{2,1,0:T(8,128)S(1)}, f32[2,32,512]{2,1,0:T(8,128)S(1)}, u32[]{:S(2)}, u32[]{:S(2)}) collective-permute-start(f32[2,32,512]{2,1,0:T(8,128)S(1)} %get-tuple-element.20), channel_id=1, source_target_pairs={{0,128},{64,448},{128,256},{192,64},{256,384},{320,192},{384,0},{4... | collective-permute-start | bytes 393224 | tf_op jit(solution)/shard_map/ppermute | solution.py:270
  118.6 8.4 %collective-permute-start.9 = (f32[2,32,512]{2,1,0:T(8,128)S(1)}, f32[2,32,512]{2,1,0:T(8,128)S(1)}, u32[]{:S(2)}, u32[]{:S(2)}) collective-permute-start(f32[2,32,512]{2,1,0:T(8,128)S(1)} %get-tuple-element.22), channel_id=1, source_target_pairs={{0,64},{64,128},{128,192},{192,256},{256,320},{320,384},{384,448},... | collective-permute-start | bytes 393224 | tf_op jit(solution)/shard_map/ppermute | solution.py:270
  127.9 20.2 %all-to-all-start.4 = ((f32[8,16,1024]{2,1,0:T(8,128)}), f32[8,16,1024]{2,1,0:T(8,128)S(1)}, u32[]{:S(2)}, u32[]{:S(2)}) async-start(f32[8,16,1024]{2,1,0:T(8,128)} %bitcast.14), calls=%async_computation.4 | async-start | bytes 1048576 | tf_op jit(solution)/shard_map/all_to_all | solution.py:274
  131.4 10.8 %collective-permute-start.12 = (f32[32,512]{1,0:T(8,128)S(1)}, f32[32,512]{1,0:T(8,128)S(1)}, u32[]{:S(2)}, u32[]{:S(2)}) collective-permute-start(f32[32,512]{1,0:T(8,128)S(1)} %slice_bitcast_fusion), channel_id=1, source_target_pairs={{0,256},{64,320},{128,384},{192,448},{256,0},{320,64},{384,128},{4... | collective-permute-start | bytes 196616 | tf_op jit(solution)/shard_map/ppermute | solution.py:273

commit v6 on v5

--- a/solution.py
+++ b/solution.py
@@ -18,7 +18,7 @@
 HBM = pl.BlockSpec(memory_space=pltpu.HBM)
 SMEM = pl.BlockSpec(memory_space=pltpu.SMEM)
 ANY = pl.BlockSpec(memory_space=pl.ANY)
-PARAMS = pltpu.CompilerParams(vmem_limit_bytes=40 * 2**20)
+PARAMS = pltpu.CompilerParams(vmem_limit_bytes=24 * 2**20)
 NN = (((1,), (0,)), ((), ()))
 NT = (((1,), (1,)), ((), ()))
 
@@ -123,28 +123,28 @@
 
 
 def image_kernel(
-    me_ref, logits_ref, row_ref, col_ref, near_ref, far_ref, own_ref, first_ref, second_ref, across_ref, texts_ref
+    me_ref, logits_ref, row_ref, col_ref, near_ref, far_ref, own_ref, first_ref, second_ref, across_ref, high_ref, low_ref,
+    texts_ref,
 ):
     inv = texts_ref.shape[0] ** (-0.5)
     arrange(me_ref, near_ref, far_ref, texts_ref)
     texts = split(texts_ref[...], 2)
     chunk = own_ref.shape[0]
     for at, grad in gradient(me_ref, logits_ref, row_ref, col_ref):
-        terms = product(texts, split(grad, 2), NN, 1) * inv
+        high, low = split(grad, 2)
+        high_ref[:, at] = high
+        low_ref[:, at] = low
+        terms = product(texts, [high, low], NN, 1) * inv
         for k, ref in enumerate((own_ref, first_ref, second_ref, across_ref)):
             ref[:, at] = terms[k * chunk : (k + 1) * chunk]
 
 
 def text_kernel(
-    me_ref, logits_ref, row_ref, col_ref, own_ref, first_ref, second_ref, across_ref, keep_ref, send_ref, all_ref
+    me_ref, high_ref, low_ref, own_ref, first_ref, second_ref, across_ref, keep_ref, send_ref, all_ref
 ):
     inv = all_ref.shape[0] ** (-0.5)
-    refs = (own_ref, first_ref, second_ref, across_ref)
-    total = None
-    for at, grad in gradient(me_ref, logits_ref, row_ref, col_ref):
-        images = jnp.concatenate([ref[:, at] for ref in refs])
-        p = product(split(images, 2), split(grad, 2), NT, 1)
-        total = p if total is None else total + p
+    images = jnp.concatenate([ref[...] for ref in (own_ref, first_ref, second_ref, across_ref)])
+    total = product(split(images, 2), [high_ref[...], low_ref[...]], NT, 1)
     all_ref[...] = total * inv
     n, step, _ = keep_ref.shape
     core, y = me_ref[0], me_ref[1]
@@ -162,8 +162,16 @@
     return lax.all_to_all(jnp.broadcast_to(block[None], (n,) + block.shape), axis, 0, 0)
 
 
-def after(x, y):
-    return x + 0.0 * y[(0,) * y.ndim]
+def after(x, *others):
+    return pl.pallas_call(
+        lambda *refs: None,
+        out_shape=jax.ShapeDtypeStruct(x.shape, x.dtype),
+        in_specs=[ANY] * (1 + len(others)),
+        out_specs=ANY,
+        input_output_aliases={0: 0},
+        compiler_params=PARAMS,
+        name="after",
+    )(x, *others)
 
 
 def sum_of(a, b, c, then):
@@ -211,7 +219,7 @@
     across = lax.ppermute(first, ("core", "x"), to_second)
     images = (images, first, second, across)
     near = gather(texts, "y_near", ny // 2).reshape(ny, own_text, cols)
-    far = lax.ppermute(after(near, across), "core", flip(nc, 1))
+    far = lax.ppermute(near + 0.0 * across[0, 0], "core", flip(nc, 1))
     width = nx * nz * own
     row_start = lax.axis_index(ROW) * rows
     col_start = lax.axis_index(COL) * cols
@@ -241,11 +249,12 @@
     )(me, allow, *images, near, far)
     col_parts = lax.all_to_all(col_parts, ROW, 0, 0)
     row_parts = lax.all_to_all(row_parts, COL, 0, 0)
-    own_terms, first, second, across = pl.pallas_call(
+    own_terms, first, second, across, high, low = pl.pallas_call(
         image_kernel,
-        out_shape=(jax.ShapeDtypeStruct((nz * own, rows), f32),) * 4,
+        out_shape=(jax.ShapeDtypeStruct((nz * own, rows), f32),) * 4
+        + (jax.ShapeDtypeStruct((cols, rows), jnp.bfloat16),) * 2,
         in_specs=[SMEM] + [VMEM] * 5,
-        out_specs=(VMEM,) * 4,
+        out_specs=(VMEM,) * 6,
         scratch_shapes=[pltpu.VMEM((width, cols), f32)],
         compiler_params=PARAMS,
         cost_estimate=pl.CostEstimate(flops=3 * passes, bytes_accessed=5 << 20, transcendentals=0),
@@ -255,13 +264,13 @@
     keep, send = pl.pallas_call(
         text_kernel,
         out_shape=(half, half),
-        in_specs=[SMEM] + [VMEM] * 7,
+        in_specs=[SMEM] + [VMEM] * 6,
         out_specs=(VMEM, VMEM),
         scratch_shapes=[pltpu.VMEM((width, cols), f32)],
         compiler_params=PARAMS,
         cost_estimate=pl.CostEstimate(flops=3 * passes, bytes_accessed=5 << 20, transcendentals=0),
         name="text_terms",
-    )(me, logits, row_parts, col_parts, *images)
+    )(me, high, low, *images)
     across = lax.ppermute(across, ("core", "x"), to_second)
     second = lax.ppermute(second, ("core", "x"), to_second)
     first = lax.ppermute(first + across, ("core", "x"), to_first)

time: 150 us -> 147 us (0.980)
  waiting for transfers between devices: 36.2 us -> 32.7 us
  starting transfers between devices: 61.3 us -> 63.1 us
    ppermute x1, waiting for transfers between devices: 6.64 us -> 4.11 us  [body(): grad_text = grad_text[0] + lax.ppermute(grad_text[1], Y, flip(ny, ny // 2))]
    ppermute x1, starting transfers between devices: 4.12 us -> 5.95 us  [body(): grad_text = grad_text[0] + lax.ppermute(grad_text[1], Y, flip(ny, ny // 2))]
  transfers between devices with their start and end apart: 16 -> 16, of which waited for: 11 -> 13; matrix products, arithmetic and copies ran while one was open for 3% -> 3% of each run, Pallas kernels for 2% -> 2%
where the time goes in v6:
time: 147 us; the launch traced here: 146 us
  starting transfers between devices  63.1 us (43%)
  waiting for transfers between devices  32.7 us (22%)
  blocking collectives  30 us (20%)
  Pallas kernels  11.8 us (8%)
  other arithmetic  3.95 us (3%)
  local copies, waits for them, and re-layouts  3.19 us (2%)
  between operations  1.54 us (1%)
    all_to_all x1, blocking collectives, body(): row_parts = lax.all_to_all(row_parts, COL, 0, 0)  15.4 us
    all_to_all x2, starting transfers between devices, gather(): lax.all_to_all(jnp.broadcast_to(block[None], (n,) + block.shape), axis, 0...  15.2 us
    all_to_all x1, blocking collectives, body(): col_parts = lax.all_to_all(col_parts, ROW, 0, 0)  14.6 us
    ppermute x3, starting transfers between devices, body(): lax.ppermute(grad_text[k + 1], Y, perm)  8.28 us
    ppermute x1, starting transfers between devices, body(): far_half = lax.ppermute(texts, Y, flip(ny, ny // 2))  7.72 us
    all_to_all x2, waiting for transfers between devices, gather(): lax.all_to_all(jnp.broadcast_to(block[None], (n,) + block.shape), axis, 0...  6.28 us
    ppermute x1, starting transfers between devices, body(): grad_text = grad_text[0] + lax.ppermute(grad_text[1], Y, flip(ny, ny // 2))  5.95 us
    ppermute x1, waiting for transfers between devices, body(): across = lax.ppermute(first, ('core', 'x'), to_second)  5.22 us
  transfers between devices with their start and end apart: 16, of which 13 were waited for; matrix products, arithmetic and copies ran while one was open for 3% of the time, Pallas kernels for 2%

profile of v6, /device:TPU:2, one launch (start us, length us, event | category | flops | bytes accessed | tf_op | source)
XLA Modules:
  0.0 146.2 jit_solution(1773829603378229641)
XLA Ops:
  0.6 1.7 %broadcast_in_dim.4 = f32[8,16,1024]{2,1,0:T(8,128)} broadcast(f32[16,1024]{1,0:T(8,128)} %bitcast.31), dimensions={1,2} | broadcast | bytes 589824 | tf_op jit(solution)/shard_map/broadcast_in_dim | solution.py:162
  2.3 10.3 %all-to-all-start = ((f32[8,16,1024]{2,1,0:T(8,128)}), f32[8,16,1024]{2,1,0:T(8,128)S(1)}, u32[]{:S(2)}, u32[]{:S(2)}) async-start(f32[8,16,1024]{2,1,0:T(8,128)} %broadcast_in_dim.4), calls=%async_computation | async-start | bytes 1048576 | tf_op jit(solution)/shard_map/all_to_all | solution.py:162
  12.6 7.7 %collective-permute-start = (f32[32,512]{1,0:T(8,128)}, f32[32,512]{1,0:T(8,128)S(1)}, u32[]{:S(2)}, u32[]{:S(2)}) collective-permute-start(f32[32,512]{1,0:T(8,128)} %bitcast.32), channel_id=1, source_target_pairs={{0,256},{64,320},{128,384},{192,448},{256,0},{320,64},{384,128},{4... | collective-permute-start | bytes 196616 | tf_op jit(solution)/shard_map/ppermute | solution.py:212
  20.4 2.9 %collective-permute-done.refs_1_ = f32[32,512]{1,0:T(8,128)S(1)} collective-permute-done((f32[32,512]{1,0:T(8,128)}, f32[32,512]{1,0:T(8,128)S(1)}, u32[]{:S(2)}, u32[]{:S(2)}) %collective-permute-start) | collective-permute-done | bytes 65568 | tf_op jit(solution)/shard_map/ppermute | solution.py:212
  23.3 0.8 pad_maximum_fusion.refs_0_
  24.1 6.0 %all-to-all-done = f32[8,16,1024]{2,1,0:T(8,128)S(1)} async-done(((f32[8,16,1024]{2,1,0:T(8,128)}), f32[8,16,1024]{2,1,0:T(8,128)S(1)}, u32[]{:S(2)}, u32[]{:S(2)}) %all-to-all-start) | async-done | bytes 524320 | tf_op jit(solution)/shard_map/all_to_all | solution.py:162
  30.1 2.4 %collective-permute-start.1 = (f32[128,1024]{1,0:T(8,128)S(1)}, f32[128,1024]{1,0:T(8,128)S(1)}, u32[]{:S(2)}, u32[]{:S(2)}) collective-permute-start(f32[128,1024]{1,0:T(8,128)S(1)} %after.2.own_ref), channel_id=1, source_target_pairs={{0,8},{8,0},{16,24},{24,16},{32,56},{40,48},{48,40},{56,32},{1,9},... | collective-permute-start | bytes 1572872 | tf_op jit(solution)/shard_map/ppermute | solution.py:217
  32.6 0.9 broadcast_in_dim.5
  33.4 4.9 %all-to-all-start.1 = ((f32[4,2,32,512]{3,2,1,0:T(8,128)}), f32[4,2,32,512]{3,2,1,0:T(8,128)S(1)}, u32[]{:S(2)}, u32[]{:S(2)}) async-start(f32[4,2,32,512]{3,2,1,0:T(8,128)} %broadcast_in_dim.5), calls=%async_computation.1 | async-start | bytes 1048576 | tf_op jit(solution)/shard_map/all_to_all | solution.py:162
  38.3 2.9 %collective-permute-done.1.first_ref = f32[128,1024]{1,0:T(8,128)S(1)} collective-permute-done((f32[128,1024]{1,0:T(8,128)S(1)}, f32[128,1024]{1,0:T(8,128)S(1)}, u32[]{:S(2)}, u32[]{:S(2)}) %collective-permute-start.1) | collective-permute-done | bytes 524320 | tf_op jit(solution)/shard_map/ppermute | solution.py:217
  41.2 3.4 %collective-permute-start.3 = (f32[128,1024]{1,0:T(8,128)S(1)}, f32[128,1024]{1,0:T(8,128)S(1)}, u32[]{:S(2)}, u32[]{:S(2)}) collective-permute-start(f32[128,1024]{1,0:T(8,128)S(1)} %collective-permute-done.1.first_ref), channel_id=1, source_target_pairs={{0,24},{8,16},{16,8},{24,0},{32,40},{40,32},{48,56},{56,48},{1,25}... | collective-permute-start | bytes 1572872 | tf_op jit(solution)/shard_map/ppermute | solution.py:219
  44.6 2.4 %collective-permute-start.2 = (f32[128,1024]{1,0:T(8,128)S(1)}, f32[128,1024]{1,0:T(8,128)S(1)}, u32[]{:S(2)}, u32[]{:S(2)}) collective-permute-start(f32[128,1024]{1,0:T(8,128)S(1)} %after.2.own_ref), channel_id=1, source_target_pairs={{0,24},{8,16},{16,8},{24,0},{32,40},{40,32},{48,56},{56,48},{1,25}... | collective-permute-start | bytes 1572872 | tf_op jit(solution)/shard_map/ppermute | solution.py:218
  47.0 5.2 %collective-permute-done.3.across_ref = f32[128,1024]{1,0:T(8,128)S(1)} collective-permute-done((f32[128,1024]{1,0:T(8,128)S(1)}, f32[128,1024]{1,0:T(8,128)S(1)}, u32[]{:S(2)}, u32[]{:S(2)}) %collective-permute-start.3) | collective-permute-done | bytes 524320 | tf_op jit(solution)/shard_map/ppermute | solution.py:219
  54.5 1.9 %collective-permute-start.4 = (f32[8,32,512]{2,1,0:T(8,128)}, f32[8,32,512]{2,1,0:T(8,128)S(1)}, u32[]{:S(2)}, u32[]{:S(2)}) collective-permute-start(f32[8,32,512]{2,1,0:T(8,128)} %broadcast_add_fusion), channel_id=1, source_target_pairs={{0,32},{32,0},{1,33},{33,1},{2,34},{34,2},{3,35},{35,3},{4,36},{36... | collective-permute-start | bytes 1572872 | tf_op jit(solution)/shard_map/ppermute | solution.py:222
  58.5 5.2 %logits.1 = (f32[512,1024]{1,0:T(8,128)S(1)}, f32[32,8,128]{2,1,0:T(8,128)S(1)}, f32[16,8,128]{2,1,0:T(8,128)S(1)}) custom-call(s32[5]{0:T(128)S(1)} %stack.32.me_ref, s32[4,2]{1,0:T(4,128)S(1)} %fusion.5.allow_ref, f32[128,1024]{1,0:T(8,128)S(1)} %after.2.own_ref, f32[128,1024]{1,0:T(8,128)S(1)} %collective-permute-done.1.first_ref, ...), custom_call_target="tpu_custom_call" | custom-call | flops 3221225472 | bytes 5242880 | tf_op jit(solution)/shard_map/logits/pallas_call | solution.py:236
  63.7 14.6 %all_to_all.25.col_ref = f32[16,8,128]{2,1,0:T(8,128)S(1)} all-to-all(f32[16,8,128]{2,1,0:T(8,128)S(1)} %get-tuple-element.15), channel_id=1, replica_groups=mesh['y_far'=2,'y_near'=4,'core'=2,'x'=4,'z'=8] {'y_far','y_near','core'}, dimensions={0} | all-to-all | bytes 131072 | tf_op jit(solution)/shard_map/all_to_all | solution.py:250
  78.4 15.4 %all_to_all.26.row_ref = f32[32,8,128]{2,1,0:T(8,128)S(1)} all-to-all(f32[32,8,128]{2,1,0:T(8,128)S(1)} %get-tuple-element.14), channel_id=1, replica_groups=mesh['y_far'=2,'y_near'=4,'core'=2,'x'=4,'z'=8] {'x','z'}, dimensions={0} | all-to-all | bytes 262144 | tf_op jit(solution)/shard_map/all_to_all | solution.py:251
  93.7 3.2 %image_terms.1 = (f32[128,1024]{1,0:T(8,128)S(1)}, f32[128,1024]{1,0:T(8,128)S(1)}, f32[128,1024]{1,0:T(8,128)S(1)}, f32[128,1024]{1,0:T(8,128)S(1)}, bf16[512,1...) custom-call(s32[5]{0:T(128)S(1)} %stack.32.me_ref, f32[512,1024]{1,0:T(8,128)S(1)} %get-tuple-element.13.logits_ref, ...), custom_call_target="tpu_custom_call" | custom-call | flops 1610612736 | bytes 5242880 | tf_op jit(solution)/shard_map/image_terms/pallas_call | solution.py:252
  97.0 2.7 %collective-permute-start.5 = (f32[128,1024]{1,0:T(8,128)S(1)}, f32[128,1024]{1,0:T(8,128)S(1)}, u32[]{:S(2)}, u32[]{:S(2)}) collective-permute-start(f32[128,1024]{1,0:T(8,128)S(1)} %get-tuple-element.18), channel_id=1, source_target_pairs={{0,24},{8,16},{16,8},{24,0},{32,40},{40,32},{48,56},{56,48},{1,25}... | collective-permute-start | bytes 1572872 | tf_op jit(solution)/shard_map/ppermute | solution.py:274
  99.7 2.5 %text_terms.1 = (f32[8,32,512]{2,1,0:T(8,128)S(1)}, f32[8,32,512]{2,1,0:T(8,128)S(1)}) custom-call(s32[5]{0:T(128)S(1)} %stack.32.me_ref, bf16[512,1024]{1,0:T(8,128)(2,1)S(1)} %get-tuple-element.20.high_ref, bf16[512,1024]{1,0:T(8,128)(2,1)S(1)} %get-tuple-element.21.low_ref, f32[128,1024]{1,0:T(8,128)S(1)} %after.2.own_ref, ...), custom_call_target="tpu_custom_call" | custom-call | flops 1610612736 | bytes 5242880 | tf_op jit(solution)/shard_map/text_terms/pallas_call | solution.py:264
  102.2 1.9 %collective-permute-start.8 = (f32[8,32,512]{2,1,0:T(8,128)S(1)}, f32[8,32,512]{2,1,0:T(8,128)S(1)}, u32[]{:S(2)}, u32[]{:S(2)}) collective-permute-start(f32[8,32,512]{2,1,0:T(8,128)S(1)} %get-tuple-element.23), channel_id=1, source_target_pairs={{0,32},{32,0},{1,33},{33,1},{2,34},{34,2},{3,35},{35,3},{4,36},{36... | collective-permute-start | bytes 1572872 | tf_op jit(solution)/shard_map/ppermute | solution.py:277
  104.1 3.1 %collective-permute-start.7 = (f32[128,1024]{1,0:T(8,128)S(1)}, f32[128,1024]{1,0:T(8,128)S(1)}, u32[]{:S(2)}, u32[]{:S(2)}) collective-permute-start(f32[128,1024]{1,0:T(8,128)S(1)} %get-tuple-element.19), channel_id=1, source_target_pairs={{0,24},{8,16},{16,8},{24,0},{32,40},{40,32},{48,56},{56,48},{1,25}... | collective-permute-start | bytes 1572872 | tf_op jit(solution)/shard_map/ppermute | solution.py:275
  108.1 4.5 %collective-permute-start.6 = (f32[128,1024]{1,0:T(8,128)S(1)}, f32[128,1024]{1,0:T(8,128)S(1)}, u32[]{:S(2)}, u32[]{:S(2)}) collective-permute-start(f32[128,1024]{1,0:T(8,128)S(1)} %add.79), channel_id=1, source_target_pairs={{0,8},{8,0},{16,24},{24,16},{32,56},{40,48},{48,40},{56,32},{1,9},... | collective-permute-start | bytes 1572872 | tf_op jit(solution)/shard_map/ppermute | solution.py:276
  112.8 2.4 %collective-permute-start.11 = (f32[2,32,512]{2,1,0:T(8,128)S(1)}, f32[2,32,512]{2,1,0:T(8,128)S(1)}, u32[]{:S(2)}, u32[]{:S(2)}) collective-permute-start(f32[2,32,512]{2,1,0:T(8,128)S(1)} %get-tuple-element.24), channel_id=1, source_target_pairs={{0,128},{64,448},{128,256},{192,64},{256,384},{320,192},{384,0},{4... | collective-permute-start | bytes 393224 | tf_op jit(solution)/shard_map/ppermute | solution.py:279
  115.2 2.5 %collective-permute-start.10 = (f32[2,32,512]{2,1,0:T(8,128)S(1)}, f32[2,32,512]{2,1,0:T(8,128)S(1)}, u32[]{:S(2)}, u32[]{:S(2)}) collective-permute-start(f32[2,32,512]{2,1,0:T(8,128)S(1)} %get-tuple-element.25), channel_id=1, source_target_pairs={{0,448},{64,0},{128,64},{192,128},{256,192},{320,256},{384,320},{4... | collective-permute-start | bytes 393224 | tf_op jit(solution)/shard_map/ppermute | solution.py:279
  117.8 3.3 %collective-permute-start.9 = (f32[2,32,512]{2,1,0:T(8,128)S(1)}, f32[2,32,512]{2,1,0:T(8,128)S(1)}, u32[]{:S(2)}, u32[]{:S(2)}) collective-permute-start(f32[2,32,512]{2,1,0:T(8,128)S(1)} %get-tuple-element.26), channel_id=1, source_target_pairs={{0,64},{64,128},{128,192},{192,256},{256,320},{320,384},{384,448},... | collective-permute-start | bytes 393224 | tf_op jit(solution)/shard_map/ppermute | solution.py:279
  122.2 4.0 %collective-permute-done.9 = f32[2,32,512]{2,1,0:T(8,128)S(1)} collective-permute-done((f32[2,32,512]{2,1,0:T(8,128)S(1)}, f32[2,32,512]{2,1,0:T(8,128)S(1)}, u32[]{:S(2)}, u32[]{:S(2)}) %collective-permute-start.9) | collective-permute-done | bytes 131104 | tf_op jit(solution)/shard_map/ppermute | solution.py:279
  126.2 0.9 sum.1
  127.1 3.5 %all-to-all-start.4 = ((f32[8,16,1024]{2,1,0:T(8,128)}), f32[8,16,1024]{2,1,0:T(8,128)S(1)}, u32[]{:S(2)}, u32[]{:S(2)}) async-start(f32[8,16,1024]{2,1,0:T(8,128)} %bitcast.12), calls=%async_computation.4 | async-start | bytes 1048576 | tf_op jit(solution)/shard_map/all_to_all | solution.py:283
  130.6 6.0 %collective-permute-start.12 = (f32[32,512]{1,0:T(8,128)S(1)}, f32[32,512]{1,0:T(8,128)S(1)}, u32[]{:S(2)}, u32[]{:S(2)}) collective-permute-start(f32[32,512]{1,0:T(8,128)S(1)} %slice_bitcast_fusion), channel_id=1, source_target_pairs={{0,256},{64,320},{128,384},{192,448},{256,0},{320,64},{384,128},{4... | collective-permute-start | bytes 196616 | tf_op jit(solution)/shard_map/ppermute | solution.py:282
  136.6 4.1 %collective-permute-done.12 = f32[32,512]{1,0:T(8,128)S(1)} collective-permute-done((f32[32,512]{1,0:T(8,128)S(1)}, f32[32,512]{1,0:T(8,128)S(1)}, u32[]{:S(2)}, u32[]{:S(2)}) %collective-permute-start.12) | collective-permute-done | bytes 65568 | tf_op jit(solution)/shard_map/ppermute | solution.py:282
  141.3 4.2 %all-to-all-done.4 = f32[8,16,1024]{2,1,0:T(8,128)S(1)} async-done(((f32[8,16,1024]{2,1,0:T(8,128)}), f32[8,16,1024]{2,1,0:T(8,128)S(1)}, u32[]{:S(2)}, u32[]{:S(2)}) %all-to-all-start.4) | async-done | bytes 524320 | tf_op jit(solution)/shard_map/all_to_all | solution.py:283
  (24 shorter events, 7.1 us)
Async XLA Ops:
  2.3 27.8 %all-to-all-start = ((f32[8,16,1024]{2,1,0:T(8,128)}), f32[8,16,1024]{2,1,0:T(8,128)S(1)}, u32[]{:S(2)}, u32[]{:S(2)}) async-start(f32[8,16,1024]{2,1,0:T(8,128)} %broadcast_in_dim.4), calls=%async_computation | async-start | bytes 1048576 | tf_op jit(solution)/shard_map/all_to_all | solution.py:162
  12.6 10.6 %collective-permute-start = (f32[32,512]{1,0:T(8,128)}, f32[32,512]{1,0:T(8,128)S(1)}, u32[]{:S(2)}, u32[]{:S(2)}) collective-permute-start(f32[32,512]{1,0:T(8,128)} %bitcast.32), channel_id=1, source_target_pairs={{0,256},{64,320},{128,384},{192,448},{256,0},{320,64},{384,128},{4... | collective-permute-start | bytes 196616 | tf_op jit(solution)/shard_map/ppermute | solution.py:212
  30.1 11.1 %collective-permute-start.1 = (f32[128,1024]{1,0:T(8,128)S(1)}, f32[128,1024]{1,0:T(8,128)S(1)}, u32[]{:S(2)}, u32[]{:S(2)}) collective-permute-start(f32[128,1024]{1,0:T(8,128)S(1)} %after.2.own_ref), channel_id=1, source_target_pairs={{0,8},{8,0},{16,24},{24,16},{32,56},{40,48},{48,40},{56,32},{1,9},... | collective-permute-start | bytes 1572872 | tf_op jit(solution)/shard_map/ppermute | solution.py:217
  33.4 20.2 %all-to-all-start.1 = ((f32[4,2,32,512]{3,2,1,0:T(8,128)}), f32[4,2,32,512]{3,2,1,0:T(8,128)S(1)}, u32[]{:S(2)}, u32[]{:S(2)}) async-start(f32[4,2,32,512]{3,2,1,0:T(8,128)} %broadcast_in_dim.5), calls=%async_computation.1 | async-start | bytes 1048576 | tf_op jit(solution)/shard_map/all_to_all | solution.py:162
  41.2 11.1 %collective-permute-start.3 = (f32[128,1024]{1,0:T(8,128)S(1)}, f32[128,1024]{1,0:T(8,128)S(1)}, u32[]{:S(2)}, u32[]{:S(2)}) collective-permute-start(f32[128,1024]{1,0:T(8,128)S(1)} %collective-permute-done.1.first_ref), channel_id=1, source_target_pairs={{0,24},{8,16},{16,8},{24,0},{32,40},{40,32},{48,56},{56,48},{1,25}... | collective-permute-start | bytes 1572872 | tf_op jit(solution)/shard_map/ppermute | solution.py:219
  44.6 13.3 %collective-permute-start.2 = (f32[128,1024]{1,0:T(8,128)S(1)}, f32[128,1024]{1,0:T(8,128)S(1)}, u32[]{:S(2)}, u32[]{:S(2)}) collective-permute-start(f32[128,1024]{1,0:T(8,128)S(1)} %after.2.own_ref), channel_id=1, source_target_pairs={{0,24},{8,16},{16,8},{24,0},{32,40},{40,32},{48,56},{56,48},{1,25}... | collective-permute-start | bytes 1572872 | tf_op jit(solution)/shard_map/ppermute | solution.py:218
  54.5 4.0 %collective-permute-start.4 = (f32[8,32,512]{2,1,0:T(8,128)}, f32[8,32,512]{2,1,0:T(8,128)S(1)}, u32[]{:S(2)}, u32[]{:S(2)}) collective-permute-start(f32[8,32,512]{2,1,0:T(8,128)} %broadcast_add_fusion), channel_id=1, source_target_pairs={{0,32},{32,0},{1,33},{33,1},{2,34},{34,2},{3,35},{35,3},{4,36},{36... | collective-permute-start | bytes 1572872 | tf_op jit(solution)/shard_map/ppermute | solution.py:222
  97.0 11.1 %collective-permute-start.5 = (f32[128,1024]{1,0:T(8,128)S(1)}, f32[128,1024]{1,0:T(8,128)S(1)}, u32[]{:S(2)}, u32[]{:S(2)}) collective-permute-start(f32[128,1024]{1,0:T(8,128)S(1)} %get-tuple-element.18), channel_id=1, source_target_pairs={{0,24},{8,16},{16,8},{24,0},{32,40},{40,32},{48,56},{56,48},{1,25}... | collective-permute-start | bytes 1572872 | tf_op jit(solution)/shard_map/ppermute | solution.py:274
  102.2 10.5 %collective-permute-start.8 = (f32[8,32,512]{2,1,0:T(8,128)S(1)}, f32[8,32,512]{2,1,0:T(8,128)S(1)}, u32[]{:S(2)}, u32[]{:S(2)}) collective-permute-start(f32[8,32,512]{2,1,0:T(8,128)S(1)} %get-tuple-element.23), channel_id=1, source_target_pairs={{0,32},{32,0},{1,33},{33,1},{2,34},{34,2},{3,35},{35,3},{4,36},{36... | collective-permute-start | bytes 1572872 | tf_op jit(solution)/shard_map/ppermute | solution.py:277
  104.1 22.1 %collective-permute-start.7 = (f32[128,1024]{1,0:T(8,128)S(1)}, f32[128,1024]{1,0:T(8,128)S(1)}, u32[]{:S(2)}, u32[]{:S(2)}) collective-permute-start(f32[128,1024]{1,0:T(8,128)S(1)} %get-tuple-element.19), channel_id=1, source_target_pairs={{0,24},{8,16},{16,8},{24,0},{32,40},{40,32},{48,56},{56,48},{1,25}... | collective-permute-start | bytes 1572872 | tf_op jit(solution)/shard_map/ppermute | solution.py:275
  108.1 18.1 %collective-permute-start.6 = (f32[128,1024]{1,0:T(8,128)S(1)}, f32[128,1024]{1,0:T(8,128)S(1)}, u32[]{:S(2)}, u32[]{:S(2)}) collective-permute-start(f32[128,1024]{1,0:T(8,128)S(1)} %add.79), channel_id=1, source_target_pairs={{0,8},{8,0},{16,24},{24,16},{32,56},{40,48},{48,40},{56,32},{1,9},... | collective-permute-start | bytes 1572872 | tf_op jit(solution)/shard_map/ppermute | solution.py:276
  112.8 9.0 %collective-permute-start.11 = (f32[2,32,512]{2,1,0:T(8,128)S(1)}, f32[2,32,512]{2,1,0:T(8,128)S(1)}, u32[]{:S(2)}, u32[]{:S(2)}) collective-permute-start(f32[2,32,512]{2,1,0:T(8,128)S(1)} %get-tuple-element.24), channel_id=1, source_target_pairs={{0,128},{64,448},{128,256},{192,64},{256,384},{320,192},{384,0},{4... | collective-permute-start | bytes 393224 | tf_op jit(solution)/shard_map/ppermute | solution.py:279
  115.2 7.0 %collective-permute-start.10 = (f32[2,32,512]{2,1,0:T(8,128)S(1)}, f32[2,32,512]{2,1,0:T(8,128)S(1)}, u32[]{:S(2)}, u32[]{:S(2)}) collective-permute-start(f32[2,32,512]{2,1,0:T(8,128)S(1)} %get-tuple-element.25), channel_id=1, source_target_pairs={{0,448},{64,0},{128,64},{192,128},{256,192},{320,256},{384,320},{4... | collective-permute-start | bytes 393224 | tf_op jit(solution)/shard_map/ppermute | solution.py:279
  117.8 8.4 %collective-permute-start.9 = (f32[2,32,512]{2,1,0:T(8,128)S(1)}, f32[2,32,512]{2,1,0:T(8,128)S(1)}, u32[]{:S(2)}, u32[]{:S(2)}) collective-permute-start(f32[2,32,512]{2,1,0:T(8,128)S(1)} %get-tuple-element.26), channel_id=1, source_target_pairs={{0,64},{64,128},{128,192},{192,256},{256,320},{320,384},{384,448},... | collective-permute-start | bytes 393224 | tf_op jit(solution)/shard_map/ppermute | solution.py:279
  127.1 18.5 %all-to-all-start.4 = ((f32[8,16,1024]{2,1,0:T(8,128)}), f32[8,16,1024]{2,1,0:T(8,128)S(1)}, u32[]{:S(2)}, u32[]{:S(2)}) async-start(f32[8,16,1024]{2,1,0:T(8,128)} %bitcast.12), calls=%async_computation.4 | async-start | bytes 1048576 | tf_op jit(solution)/shard_map/all_to_all | solution.py:283
  130.6 10.1 %collective-permute-start.12 = (f32[32,512]{1,0:T(8,128)S(1)}, f32[32,512]{1,0:T(8,128)S(1)}, u32[]{:S(2)}, u32[]{:S(2)}) collective-permute-start(f32[32,512]{1,0:T(8,128)S(1)} %slice_bitcast_fusion), channel_id=1, source_target_pairs={{0,256},{64,320},{128,384},{192,448},{256,0},{320,64},{384,128},{4... | collective-permute-start | bytes 196616 | tf_op jit(solution)/shard_map/ppermute | solution.py:282

commit v7 on v6

--- a/solution.py
+++ b/solution.py
@@ -65,18 +65,22 @@
 
 
 def logits_kernel(
-    me_ref, allow_ref, own_ref, first_ref, second_ref, across_ref, near_ref, far_ref, logits_ref, row_ref, col_ref, texts_ref
+    me_ref, allow_ref, own_ref, first_ref, second_ref, across_ref, near_ref, far_ref,
+    logits_ref, row_ref, col_ref, images_high_ref, images_low_ref, texts_high_ref, texts_low_ref, texts_ref,
 ):
     rows = own_ref.shape[1]
     width, cols = texts_ref.shape
     inv = width ** (-0.5)
-    refs = (own_ref, first_ref, second_ref, across_ref)
     arrange(me_ref, near_ref, far_ref, texts_ref)
+    texts_high_ref[...], texts_low_ref[...] = split(texts_ref[...], 2)
     texts = split(texts_ref[...].T, 3)
     for i in range(rows // BLK):
         at = pl.ds(i * BLK, BLK)
-        images = jnp.concatenate([ref[:, at] for ref in refs])
-        part = product(texts, split(images, 3), NN, 2) * inv
+        images = jnp.concatenate([ref[:, at] for ref in (own_ref, first_ref, second_ref, across_ref)])
+        images = split(images, 3)
+        images_high_ref[:, at] = images[0]
+        images_low_ref[:, at] = images[1]
+        part = product(texts, images, NN, 2) * inv
         for j in range(cols // BLK):
             block = jnp.where(allow_ref[i, j] > 0, part[j * BLK : (j + 1) * BLK], NEG)
             logits_ref[pl.ds(j * BLK, BLK), at] = block
@@ -123,12 +127,11 @@
 
 
 def image_kernel(
-    me_ref, logits_ref, row_ref, col_ref, near_ref, far_ref, own_ref, first_ref, second_ref, across_ref, high_ref, low_ref,
-    texts_ref,
+    me_ref, logits_ref, row_ref, col_ref, texts_high_ref, texts_low_ref,
+    own_ref, first_ref, second_ref, across_ref, high_ref, low_ref,
 ):
-    inv = texts_ref.shape[0] ** (-0.5)
-    arrange(me_ref, near_ref, far_ref, texts_ref)
-    texts = split(texts_ref[...], 2)
+    inv = texts_high_ref.shape[0] ** (-0.5)
+    texts = [texts_high_ref[...], texts_low_ref[...]]
     chunk = own_ref.shape[0]
     for at, grad in gradient(me_ref, logits_ref, row_ref, col_ref):
         high, low = split(grad, 2)
@@ -139,18 +142,16 @@
             ref[:, at] = terms[k * chunk : (k + 1) * chunk]
 
 
-def text_kernel(
-    me_ref, high_ref, low_ref, own_ref, first_ref, second_ref, across_ref, keep_ref, send_ref, all_ref
-):
+def text_kernel(me_ref, high_ref, low_ref, images_high_ref, images_low_ref, keep_ref, send_ref, all_ref):
     inv = all_ref.shape[0] ** (-0.5)
-    images = jnp.concatenate([ref[...] for ref in (own_ref, first_ref, second_ref, across_ref)])
-    total = product(split(images, 2), [high_ref[...], low_ref[...]], NT, 1)
+    images = [images_high_ref[...], images_low_ref[...]]
+    total = product(images, [high_ref[...], low_ref[...]], NT, 1)
     all_ref[...] = total * inv
     n, step, _ = keep_ref.shape
     core, y = me_ref[0], me_ref[1]
     for k, there in enumerate(pairs(y, 1, n)):
         for other, ref in enumerate((keep_ref, send_ref)):
-            ref[k] = all_ref[place(me_ref, there, core ^ other, step, own_ref.shape[0]), :]
+            ref[k] = all_ref[place(me_ref, there, core ^ other, step, all_ref.shape[0] // 4), :]
 
 
 def sum_kernel(a_ref, b_ref, c_ref, after_ref, out_ref):
@@ -229,19 +230,23 @@
     row_ids = first_row + jnp.arange(row_blocks, dtype=jnp.int32)
     col_ids = first_col + jnp.arange(col_blocks, dtype=jnp.int32)
     allow = ((window > 0) | (row_ids[:, None] == col_ids[None, :])).astype(jnp.int32)
-    f32 = jnp.float32
+    f32, bf16 = jnp.float32, jnp.bfloat16
     passes = 2 * rows * cols * width
     me = [lax.axis_index("core"), lax.axis_index(Y), row_start, col_start, lax.axis_index("x")]
     me = jnp.stack(me).astype(jnp.int32)
-    logits, row_parts, col_parts = pl.pallas_call(
+    logits, row_parts, col_parts, images_high, images_low, texts_high, texts_low = pl.pallas_call(
         logits_kernel,
         out_shape=(
             jax.ShapeDtypeStruct((cols, rows), f32),
             jax.ShapeDtypeStruct((nx * nz, rows // LANES, LANES), f32),
             jax.ShapeDtypeStruct((ny * nc, rows // LANES, LANES), f32),
+            jax.ShapeDtypeStruct((width, rows), bf16),
+            jax.ShapeDtypeStruct((width, rows), bf16),
+            jax.ShapeDtypeStruct((width, cols), bf16),
+            jax.ShapeDtypeStruct((width, cols), bf16),
         ),
         in_specs=[SMEM, SMEM] + [VMEM] * 6,
-        out_specs=(VMEM, VMEM, VMEM),
+        out_specs=(VMEM,) * 7,
         scratch_shapes=[pltpu.VMEM((width, cols), f32)],
         compiler_params=PARAMS,
         cost_estimate=pl.CostEstimate(flops=6 * passes, bytes_accessed=5 << 20, transcendentals=0),
@@ -252,25 +257,24 @@
     own_terms, first, second, across, high, low = pl.pallas_call(
         image_kernel,
         out_shape=(jax.ShapeDtypeStruct((nz * own, rows), f32),) * 4
-        + (jax.ShapeDtypeStruct((cols, rows), jnp.bfloat16),) * 2,
+        + (jax.ShapeDtypeStruct((cols, rows), bf16),) * 2,
         in_specs=[SMEM] + [VMEM] * 5,
         out_specs=(VMEM,) * 6,
-        scratch_shapes=[pltpu.VMEM((width, cols), f32)],
         compiler_params=PARAMS,
         cost_estimate=pl.CostEstimate(flops=3 * passes, bytes_accessed=5 << 20, transcendentals=0),
         name="image_terms",
-    )(me, logits, row_parts, col_parts, near, far)
+    )(me, logits, row_parts, col_parts, texts_high, texts_low)
     half = jax.ShapeDtypeStruct((ny, own_text, cols), f32)
     keep, send = pl.pallas_call(
         text_kernel,
         out_shape=(half, half),
-        in_specs=[SMEM] + [VMEM] * 6,
+        in_specs=[SMEM] + [VMEM] * 4,
         out_specs=(VMEM, VMEM),
         scratch_shapes=[pltpu.VMEM((width, cols), f32)],
         compiler_params=PARAMS,
         cost_estimate=pl.CostEstimate(flops=3 * passes, bytes_accessed=5 << 20, transcendentals=0),
         name="text_terms",
-    )(me, high, low, *images)
+    )(me, high, low, images_high, images_low)
     across = lax.ppermute(across, ("core", "x"), to_second)
     second = lax.ppermute(second, ("core", "x"), to_second)
     first = lax.ppermute(first + across, ("core", "x"), to_first)

time: 147 us -> 147 us (level)
  no operation moved by 1% of the time
where the time goes in v7:
time: 147 us; the launch traced here: 146 us
  starting transfers between devices  63.1 us (43%)
  waiting for transfers between devices  32.7 us (22%)
  blocking collectives  30 us (20%)
  Pallas kernels  11.9 us (8%)
  other arithmetic  3.97 us (3%)
  local copies, waits for them, and re-layouts  3.19 us (2%)
  between operations  1.53 us (1%)
    all_to_all x1, blocking collectives, body(): row_parts = lax.all_to_all(row_parts, COL, 0, 0)  15.4 us
    all_to_all x2, starting transfers between devices, gather(): lax.all_to_all(jnp.broadcast_to(block[None], (n,) + block.shape), axis, 0...  15.2 us
    all_to_all x1, blocking collectives, body(): col_parts = lax.all_to_all(col_parts, ROW, 0, 0)  14.6 us
    ppermute x3, starting transfers between devices, body(): lax.ppermute(grad_text[k + 1], Y, perm)  8.29 us
    ppermute x1, starting transfers between devices, body(): far_half = lax.ppermute(texts, Y, flip(ny, ny // 2))  7.72 us
    all_to_all x2, waiting for transfers between devices, gather(): lax.all_to_all(jnp.broadcast_to(block[None], (n,) + block.shape), axis, 0...  6.28 us
    ppermute x1, starting transfers between devices, body(): grad_text = grad_text[0] + lax.ppermute(grad_text[1], Y, flip(ny, ny // 2))  5.96 us
    pallas_call x1, Pallas kernels, body(): pl.pallas_call(logits_kernel, out_shape=(jax.ShapeDtypeStruct((cols, rows...  5.53 us
  transfers between devices with their start and end apart: 16, of which 13 were waited for; matrix products, arithmetic and copies ran while one was open for 3% of the time, Pallas kernels for 2%

profile of v7, /device:TPU:2, one launch (start us, length us, event | category | flops | bytes accessed | tf_op | source)
XLA Modules:
  0.0 146.4 jit_solution(6001187701831162039)
XLA Ops:
  0.6 1.7 %broadcast_in_dim.4 = f32[8,16,1024]{2,1,0:T(8,128)} broadcast(f32[16,1024]{1,0:T(8,128)} %bitcast.30), dimensions={1,2} | broadcast | bytes 589824 | tf_op jit(solution)/shard_map/broadcast_in_dim | solution.py:163
  2.3 10.3 %all-to-all-start = ((f32[8,16,1024]{2,1,0:T(8,128)}), f32[8,16,1024]{2,1,0:T(8,128)S(1)}, u32[]{:S(2)}, u32[]{:S(2)}) async-start(f32[8,16,1024]{2,1,0:T(8,128)} %broadcast_in_dim.4), calls=%async_computation | async-start | bytes 1048576 | tf_op jit(solution)/shard_map/all_to_all | solution.py:163
  12.6 7.7 %collective-permute-start = (f32[32,512]{1,0:T(8,128)}, f32[32,512]{1,0:T(8,128)S(1)}, u32[]{:S(2)}, u32[]{:S(2)}) collective-permute-start(f32[32,512]{1,0:T(8,128)} %bitcast.31), channel_id=1, source_target_pairs={{0,256},{64,320},{128,384},{192,448},{256,0},{320,64},{384,128},{4... | collective-permute-start | bytes 196616 | tf_op jit(solution)/shard_map/ppermute | solution.py:213
  20.4 2.9 %collective-permute-done.refs_1_ = f32[32,512]{1,0:T(8,128)S(1)} collective-permute-done((f32[32,512]{1,0:T(8,128)}, f32[32,512]{1,0:T(8,128)S(1)}, u32[]{:S(2)}, u32[]{:S(2)}) %collective-permute-start) | collective-permute-done | bytes 65568 | tf_op jit(solution)/shard_map/ppermute | solution.py:213
  23.3 0.8 pad_maximum_fusion.refs_0_
  24.1 6.0 %all-to-all-done = f32[8,16,1024]{2,1,0:T(8,128)S(1)} async-done(((f32[8,16,1024]{2,1,0:T(8,128)}), f32[8,16,1024]{2,1,0:T(8,128)S(1)}, u32[]{:S(2)}, u32[]{:S(2)}) %all-to-all-start) | async-done | bytes 524320 | tf_op jit(solution)/shard_map/all_to_all | solution.py:163
  30.1 2.4 %collective-permute-start.1 = (f32[128,1024]{1,0:T(8,128)S(1)}, f32[128,1024]{1,0:T(8,128)S(1)}, u32[]{:S(2)}, u32[]{:S(2)}) collective-permute-start(f32[128,1024]{1,0:T(8,128)S(1)} %after.2.own_ref), channel_id=1, source_target_pairs={{0,8},{8,0},{16,24},{24,16},{32,56},{40,48},{48,40},{56,32},{1,9},... | collective-permute-start | bytes 1572872 | tf_op jit(solution)/shard_map/ppermute | solution.py:218
  32.6 0.9 broadcast_in_dim.5
  33.4 4.9 %all-to-all-start.1 = ((f32[4,2,32,512]{3,2,1,0:T(8,128)}), f32[4,2,32,512]{3,2,1,0:T(8,128)S(1)}, u32[]{:S(2)}, u32[]{:S(2)}) async-start(f32[4,2,32,512]{3,2,1,0:T(8,128)} %broadcast_in_dim.5), calls=%async_computation.1 | async-start | bytes 1048576 | tf_op jit(solution)/shard_map/all_to_all | solution.py:163
  38.3 2.9 %collective-permute-done.1.first_ref = f32[128,1024]{1,0:T(8,128)S(1)} collective-permute-done((f32[128,1024]{1,0:T(8,128)S(1)}, f32[128,1024]{1,0:T(8,128)S(1)}, u32[]{:S(2)}, u32[]{:S(2)}) %collective-permute-start.1) | collective-permute-done | bytes 524320 | tf_op jit(solution)/shard_map/ppermute | solution.py:218
  41.2 3.4 %collective-permute-start.3 = (f32[128,1024]{1,0:T(8,128)S(1)}, f32[128,1024]{1,0:T(8,128)S(1)}, u32[]{:S(2)}, u32[]{:S(2)}) collective-permute-start(f32[128,1024]{1,0:T(8,128)S(1)} %collective-permute-done.1.first_ref), channel_id=1, source_target_pairs={{0,24},{8,16},{16,8},{24,0},{32,40},{40,32},{48,56},{56,48},{1,25}... | collective-permute-start | bytes 1572872 | tf_op jit(solution)/shard_map/ppermute | solution.py:220
  44.6 2.4 %collective-permute-start.2 = (f32[128,1024]{1,0:T(8,128)S(1)}, f32[128,1024]{1,0:T(8,128)S(1)}, u32[]{:S(2)}, u32[]{:S(2)}) collective-permute-start(f32[128,1024]{1,0:T(8,128)S(1)} %after.2.own_ref), channel_id=1, source_target_pairs={{0,24},{8,16},{16,8},{24,0},{32,40},{40,32},{48,56},{56,48},{1,25}... | collective-permute-start | bytes 1572872 | tf_op jit(solution)/shard_map/ppermute | solution.py:219
  47.0 5.2 %collective-permute-done.3.across_ref = f32[128,1024]{1,0:T(8,128)S(1)} collective-permute-done((f32[128,1024]{1,0:T(8,128)S(1)}, f32[128,1024]{1,0:T(8,128)S(1)}, u32[]{:S(2)}, u32[]{:S(2)}) %collective-permute-start.3) | collective-permute-done | bytes 524320 | tf_op jit(solution)/shard_map/ppermute | solution.py:220
  54.5 1.9 %collective-permute-start.4 = (f32[8,32,512]{2,1,0:T(8,128)}, f32[8,32,512]{2,1,0:T(8,128)S(1)}, u32[]{:S(2)}, u32[]{:S(2)}) collective-permute-start(f32[8,32,512]{2,1,0:T(8,128)} %broadcast_add_fusion), channel_id=1, source_target_pairs={{0,32},{32,0},{1,33},{33,1},{2,34},{34,2},{3,35},{35,3},{4,36},{36... | collective-permute-start | bytes 1572872 | tf_op jit(solution)/shard_map/ppermute | solution.py:223
  58.5 5.5 %logits.1 = (f32[512,1024]{1,0:T(8,128)S(1)}, f32[32,8,128]{2,1,0:T(8,128)S(1)}, f32[16,8,128]{2,1,0:T(8,128)S(1)}, bf16[512,1024]{1,0:T(8,128)(2,1)S(1)}, bf16[...) custom-call(s32[5]{0:T(128)S(1)} %stack.32.me_ref, ...), custom_call_target="tpu_custom_call" | custom-call | flops 3221225472 | bytes 5242880 | tf_op jit(solution)/shard_map/logits/pallas_call | solution.py:237
  64.1 14.6 %all_to_all.25.col_ref = f32[16,8,128]{2,1,0:T(8,128)S(1)} all-to-all(f32[16,8,128]{2,1,0:T(8,128)S(1)} %get-tuple-element.19), channel_id=1, replica_groups=mesh['y_far'=2,'y_near'=4,'core'=2,'x'=4,'z'=8] {'y_far','y_near','core'}, dimensions={0} | all-to-all | bytes 131072 | tf_op jit(solution)/shard_map/all_to_all | solution.py:255
  78.7 15.4 %all_to_all.26.row_ref = f32[32,8,128]{2,1,0:T(8,128)S(1)} all-to-all(f32[32,8,128]{2,1,0:T(8,128)S(1)} %get-tuple-element.18), channel_id=1, replica_groups=mesh['y_far'=2,'y_near'=4,'core'=2,'x'=4,'z'=8] {'x','z'}, dimensions={0} | all-to-all | bytes 262144 | tf_op jit(solution)/shard_map/all_to_all | solution.py:256
  94.1 3.1 %image_terms.1 = (f32[128,1024]{1,0:T(8,128)S(1)}, f32[128,1024]{1,0:T(8,128)S(1)}, f32[128,1024]{1,0:T(8,128)S(1)}, f32[128,1024]{1,0:T(8,128)S(1)}, bf16[512,1...) custom-call(s32[5]{0:T(128)S(1)} %stack.32.me_ref, f32[512,1024]{1,0:T(8,128)S(1)} %get-tuple-element.17.logits_ref, ...), custom_call_target="tpu_custom_call" | custom-call | flops 1610612736 | bytes 5242880 | tf_op jit(solution)/shard_map/image_terms/pallas_call | solution.py:257
  97.1 2.7 %collective-permute-start.5 = (f32[128,1024]{1,0:T(8,128)S(1)}, f32[128,1024]{1,0:T(8,128)S(1)}, u32[]{:S(2)}, u32[]{:S(2)}) collective-permute-start(f32[128,1024]{1,0:T(8,128)S(1)} %get-tuple-element.24), channel_id=1, source_target_pairs={{0,24},{8,16},{16,8},{24,0},{32,40},{40,32},{48,56},{56,48},{1,25}... | collective-permute-start | bytes 1572872 | tf_op jit(solution)/shard_map/ppermute | solution.py:278
  99.8 2.5 %text_terms.1 = (f32[8,32,512]{2,1,0:T(8,128)S(1)}, f32[8,32,512]{2,1,0:T(8,128)S(1)}) custom-call(s32[5]{0:T(128)S(1)} %stack.32.me_ref, bf16[512,1024]{1,0:T(8,128)(2,1)S(1)} %get-tuple-element.26.high_ref, bf16[512,1024]{1,0:T(8,128)(2,1)S(1)} %get-tuple-element.27.low_ref, bf16[512,1024]{1,0:T(8,128)(2,1)S(1)} %get-tuple-element.28.images_high_ref, ...), custom_call_target="tpu_custom_call" | custom-call | flops 1610612736 | bytes 5242880 | tf_op jit(solution)/shard_map/text_terms/pallas_call | solution.py:268
  102.3 1.9 %collective-permute-start.8 = (f32[8,32,512]{2,1,0:T(8,128)S(1)}, f32[8,32,512]{2,1,0:T(8,128)S(1)}, u32[]{:S(2)}, u32[]{:S(2)}) collective-permute-start(f32[8,32,512]{2,1,0:T(8,128)S(1)} %get-tuple-element.31), channel_id=1, source_target_pairs={{0,32},{32,0},{1,33},{33,1},{2,34},{34,2},{3,35},{35,3},{4,36},{36... | collective-permute-start | bytes 1572872 | tf_op jit(solution)/shard_map/ppermute | solution.py:281
  104.2 3.1 %collective-permute-start.7 = (f32[128,1024]{1,0:T(8,128)S(1)}, f32[128,1024]{1,0:T(8,128)S(1)}, u32[]{:S(2)}, u32[]{:S(2)}) collective-permute-start(f32[128,1024]{1,0:T(8,128)S(1)} %get-tuple-element.25), channel_id=1, source_target_pairs={{0,24},{8,16},{16,8},{24,0},{32,40},{40,32},{48,56},{56,48},{1,25}... | collective-permute-start | bytes 1572872 | tf_op jit(solution)/shard_map/ppermute | solution.py:279
  108.3 4.5 %collective-permute-start.6 = (f32[128,1024]{1,0:T(8,128)S(1)}, f32[128,1024]{1,0:T(8,128)S(1)}, u32[]{:S(2)}, u32[]{:S(2)}) collective-permute-start(f32[128,1024]{1,0:T(8,128)S(1)} %add.79), channel_id=1, source_target_pairs={{0,8},{8,0},{16,24},{24,16},{32,56},{40,48},{48,40},{56,32},{1,9},... | collective-permute-start | bytes 1572872 | tf_op jit(solution)/shard_map/ppermute | solution.py:280
  113.0 2.4 %collective-permute-start.11 = (f32[2,32,512]{2,1,0:T(8,128)S(1)}, f32[2,32,512]{2,1,0:T(8,128)S(1)}, u32[]{:S(2)}, u32[]{:S(2)}) collective-permute-start(f32[2,32,512]{2,1,0:T(8,128)S(1)} %get-tuple-element.32), channel_id=1, source_target_pairs={{0,128},{64,448},{128,256},{192,64},{256,384},{320,192},{384,0},{4... | collective-permute-start | bytes 393224 | tf_op jit(solution)/shard_map/ppermute | solution.py:283
  115.4 2.5 %collective-permute-start.10 = (f32[2,32,512]{2,1,0:T(8,128)S(1)}, f32[2,32,512]{2,1,0:T(8,128)S(1)}, u32[]{:S(2)}, u32[]{:S(2)}) collective-permute-start(f32[2,32,512]{2,1,0:T(8,128)S(1)} %get-tuple-element.33), channel_id=1, source_target_pairs={{0,448},{64,0},{128,64},{192,128},{256,192},{320,256},{384,320},{4... | collective-permute-start | bytes 393224 | tf_op jit(solution)/shard_map/ppermute | solution.py:283
  117.9 3.3 %collective-permute-start.9 = (f32[2,32,512]{2,1,0:T(8,128)S(1)}, f32[2,32,512]{2,1,0:T(8,128)S(1)}, u32[]{:S(2)}, u32[]{:S(2)}) collective-permute-start(f32[2,32,512]{2,1,0:T(8,128)S(1)} %get-tuple-element.34), channel_id=1, source_target_pairs={{0,64},{64,128},{128,192},{192,256},{256,320},{320,384},{384,448},... | collective-permute-start | bytes 393224 | tf_op jit(solution)/shard_map/ppermute | solution.py:283
  122.4 4.0 %collective-permute-done.9 = f32[2,32,512]{2,1,0:T(8,128)S(1)} collective-permute-done((f32[2,32,512]{2,1,0:T(8,128)S(1)}, f32[2,32,512]{2,1,0:T(8,128)S(1)}, u32[]{:S(2)}, u32[]{:S(2)}) %collective-permute-start.9) | collective-permute-done | bytes 131104 | tf_op jit(solution)/shard_map/ppermute | solution.py:283
  126.4 0.9 sum.1
  127.3 3.5 %all-to-all-start.4 = ((f32[8,16,1024]{2,1,0:T(8,128)}), f32[8,16,1024]{2,1,0:T(8,128)S(1)}, u32[]{:S(2)}, u32[]{:S(2)}) async-start(f32[8,16,1024]{2,1,0:T(8,128)} %bitcast.12), calls=%async_computation.4 | async-start | bytes 1048576 | tf_op jit(solution)/shard_map/all_to_all | solution.py:287
  130.8 6.0 %collective-permute-start.12 = (f32[32,512]{1,0:T(8,128)S(1)}, f32[32,512]{1,0:T(8,128)S(1)}, u32[]{:S(2)}, u32[]{:S(2)}) collective-permute-start(f32[32,512]{1,0:T(8,128)S(1)} %slice_bitcast_fusion), channel_id=1, source_target_pairs={{0,256},{64,320},{128,384},{192,448},{256,0},{320,64},{384,128},{4... | collective-permute-start | bytes 196616 | tf_op jit(solution)/shard_map/ppermute | solution.py:286
  136.8 4.1 %collective-permute-done.12 = f32[32,512]{1,0:T(8,128)S(1)} collective-permute-done((f32[32,512]{1,0:T(8,128)S(1)}, f32[32,512]{1,0:T(8,128)S(1)}, u32[]{:S(2)}, u32[]{:S(2)}) %collective-permute-start.12) | collective-permute-done | bytes 65568 | tf_op jit(solution)/shard_map/ppermute | solution.py:286
  141.5 4.2 %all-to-all-done.4 = f32[8,16,1024]{2,1,0:T(8,128)S(1)} async-done(((f32[8,16,1024]{2,1,0:T(8,128)}), f32[8,16,1024]{2,1,0:T(8,128)S(1)}, u32[]{:S(2)}, u32[]{:S(2)}) %all-to-all-start.4) | async-done | bytes 524320 | tf_op jit(solution)/shard_map/all_to_all | solution.py:287
  (24 shorter events, 7.1 us)
Async XLA Ops:
  2.3 27.8 %all-to-all-start = ((f32[8,16,1024]{2,1,0:T(8,128)}), f32[8,16,1024]{2,1,0:T(8,128)S(1)}, u32[]{:S(2)}, u32[]{:S(2)}) async-start(f32[8,16,1024]{2,1,0:T(8,128)} %broadcast_in_dim.4), calls=%async_computation | async-start | bytes 1048576 | tf_op jit(solution)/shard_map/all_to_all | solution.py:163
  12.6 10.6 %collective-permute-start = (f32[32,512]{1,0:T(8,128)}, f32[32,512]{1,0:T(8,128)S(1)}, u32[]{:S(2)}, u32[]{:S(2)}) collective-permute-start(f32[32,512]{1,0:T(8,128)} %bitcast.31), channel_id=1, source_target_pairs={{0,256},{64,320},{128,384},{192,448},{256,0},{320,64},{384,128},{4... | collective-permute-start | bytes 196616 | tf_op jit(solution)/shard_map/ppermute | solution.py:213
  30.1 11.1 %collective-permute-start.1 = (f32[128,1024]{1,0:T(8,128)S(1)}, f32[128,1024]{1,0:T(8,128)S(1)}, u32[]{:S(2)}, u32[]{:S(2)}) collective-permute-start(f32[128,1024]{1,0:T(8,128)S(1)} %after.2.own_ref), channel_id=1, source_target_pairs={{0,8},{8,0},{16,24},{24,16},{32,56},{40,48},{48,40},{56,32},{1,9},... | collective-permute-start | bytes 1572872 | tf_op jit(solution)/shard_map/ppermute | solution.py:218
  33.4 20.2 %all-to-all-start.1 = ((f32[4,2,32,512]{3,2,1,0:T(8,128)}), f32[4,2,32,512]{3,2,1,0:T(8,128)S(1)}, u32[]{:S(2)}, u32[]{:S(2)}) async-start(f32[4,2,32,512]{3,2,1,0:T(8,128)} %broadcast_in_dim.5), calls=%async_computation.1 | async-start | bytes 1048576 | tf_op jit(solution)/shard_map/all_to_all | solution.py:163
  41.2 11.1 %collective-permute-start.3 = (f32[128,1024]{1,0:T(8,128)S(1)}, f32[128,1024]{1,0:T(8,128)S(1)}, u32[]{:S(2)}, u32[]{:S(2)}) collective-permute-start(f32[128,1024]{1,0:T(8,128)S(1)} %collective-permute-done.1.first_ref), channel_id=1, source_target_pairs={{0,24},{8,16},{16,8},{24,0},{32,40},{40,32},{48,56},{56,48},{1,25}... | collective-permute-start | bytes 1572872 | tf_op jit(solution)/shard_map/ppermute | solution.py:220
  44.6 13.3 %collective-permute-start.2 = (f32[128,1024]{1,0:T(8,128)S(1)}, f32[128,1024]{1,0:T(8,128)S(1)}, u32[]{:S(2)}, u32[]{:S(2)}) collective-permute-start(f32[128,1024]{1,0:T(8,128)S(1)} %after.2.own_ref), channel_id=1, source_target_pairs={{0,24},{8,16},{16,8},{24,0},{32,40},{40,32},{48,56},{56,48},{1,25}... | collective-permute-start | bytes 1572872 | tf_op jit(solution)/shard_map/ppermute | solution.py:219
  54.5 4.0 %collective-permute-start.4 = (f32[8,32,512]{2,1,0:T(8,128)}, f32[8,32,512]{2,1,0:T(8,128)S(1)}, u32[]{:S(2)}, u32[]{:S(2)}) collective-permute-start(f32[8,32,512]{2,1,0:T(8,128)} %broadcast_add_fusion), channel_id=1, source_target_pairs={{0,32},{32,0},{1,33},{33,1},{2,34},{34,2},{3,35},{35,3},{4,36},{36... | collective-permute-start | bytes 1572872 | tf_op jit(solution)/shard_map/ppermute | solution.py:223
  97.1 11.1 %collective-permute-start.5 = (f32[128,1024]{1,0:T(8,128)S(1)}, f32[128,1024]{1,0:T(8,128)S(1)}, u32[]{:S(2)}, u32[]{:S(2)}) collective-permute-start(f32[128,1024]{1,0:T(8,128)S(1)} %get-tuple-element.24), channel_id=1, source_target_pairs={{0,24},{8,16},{16,8},{24,0},{32,40},{40,32},{48,56},{56,48},{1,25}... | collective-permute-start | bytes 1572872 | tf_op jit(solution)/shard_map/ppermute | solution.py:278
  102.3 10.5 %collective-permute-start.8 = (f32[8,32,512]{2,1,0:T(8,128)S(1)}, f32[8,32,512]{2,1,0:T(8,128)S(1)}, u32[]{:S(2)}, u32[]{:S(2)}) collective-permute-start(f32[8,32,512]{2,1,0:T(8,128)S(1)} %get-tuple-element.31), channel_id=1, source_target_pairs={{0,32},{32,0},{1,33},{33,1},{2,34},{34,2},{3,35},{35,3},{4,36},{36... | collective-permute-start | bytes 1572872 | tf_op jit(solution)/shard_map/ppermute | solution.py:281
  104.2 22.1 %collective-permute-start.7 = (f32[128,1024]{1,0:T(8,128)S(1)}, f32[128,1024]{1,0:T(8,128)S(1)}, u32[]{:S(2)}, u32[]{:S(2)}) collective-permute-start(f32[128,1024]{1,0:T(8,128)S(1)} %get-tuple-element.25), channel_id=1, source_target_pairs={{0,24},{8,16},{16,8},{24,0},{32,40},{40,32},{48,56},{56,48},{1,25}... | collective-permute-start | bytes 1572872 | tf_op jit(solution)/shard_map/ppermute | solution.py:279
  108.3 18.1 %collective-permute-start.6 = (f32[128,1024]{1,0:T(8,128)S(1)}, f32[128,1024]{1,0:T(8,128)S(1)}, u32[]{:S(2)}, u32[]{:S(2)}) collective-permute-start(f32[128,1024]{1,0:T(8,128)S(1)} %add.79), channel_id=1, source_target_pairs={{0,8},{8,0},{16,24},{24,16},{32,56},{40,48},{48,40},{56,32},{1,9},... | collective-permute-start | bytes 1572872 | tf_op jit(solution)/shard_map/ppermute | solution.py:280
  113.0 9.0 %collective-permute-start.11 = (f32[2,32,512]{2,1,0:T(8,128)S(1)}, f32[2,32,512]{2,1,0:T(8,128)S(1)}, u32[]{:S(2)}, u32[]{:S(2)}) collective-permute-start(f32[2,32,512]{2,1,0:T(8,128)S(1)} %get-tuple-element.32), channel_id=1, source_target_pairs={{0,128},{64,448},{128,256},{192,64},{256,384},{320,192},{384,0},{4... | collective-permute-start | bytes 393224 | tf_op jit(solution)/shard_map/ppermute | solution.py:283
  115.4 7.0 %collective-permute-start.10 = (f32[2,32,512]{2,1,0:T(8,128)S(1)}, f32[2,32,512]{2,1,0:T(8,128)S(1)}, u32[]{:S(2)}, u32[]{:S(2)}) collective-permute-start(f32[2,32,512]{2,1,0:T(8,128)S(1)} %get-tuple-element.33), channel_id=1, source_target_pairs={{0,448},{64,0},{128,64},{192,128},{256,192},{320,256},{384,320},{4... | collective-permute-start | bytes 393224 | tf_op jit(solution)/shard_map/ppermute | solution.py:283
  117.9 8.4 %collective-permute-start.9 = (f32[2,32,512]{2,1,0:T(8,128)S(1)}, f32[2,32,512]{2,1,0:T(8,128)S(1)}, u32[]{:S(2)}, u32[]{:S(2)}) collective-permute-start(f32[2,32,512]{2,1,0:T(8,128)S(1)} %get-tuple-element.34), channel_id=1, source_target_pairs={{0,64},{64,128},{128,192},{192,256},{256,320},{320,384},{384,448},... | collective-permute-start | bytes 393224 | tf_op jit(solution)/shard_map/ppermute | solution.py:283
  127.3 18.4 %all-to-all-start.4 = ((f32[8,16,1024]{2,1,0:T(8,128)}), f32[8,16,1024]{2,1,0:T(8,128)S(1)}, u32[]{:S(2)}, u32[]{:S(2)}) async-start(f32[8,16,1024]{2,1,0:T(8,128)} %bitcast.12), calls=%async_computation.4 | async-start | bytes 1048576 | tf_op jit(solution)/shard_map/all_to_all | solution.py:287
  130.8 10.1 %collective-permute-start.12 = (f32[32,512]{1,0:T(8,128)S(1)}, f32[32,512]{1,0:T(8,128)S(1)}, u32[]{:S(2)}, u32[]{:S(2)}) collective-permute-start(f32[32,512]{1,0:T(8,128)S(1)} %slice_bitcast_fusion), channel_id=1, source_target_pairs={{0,256},{64,320},{128,384},{192,448},{256,0},{320,64},{384,128},{4... | collective-permute-start | bytes 196616 | tf_op jit(solution)/shard_map/ppermute | solution.py:286

commit v8 on v7

--- a/solution.py
+++ b/solution.py
@@ -252,8 +252,8 @@
         cost_estimate=pl.CostEstimate(flops=6 * passes, bytes_accessed=5 << 20, transcendentals=0),
         name="logits",
     )(me, allow, *images, near, far)
-    col_parts = lax.all_to_all(col_parts, ROW, 0, 0)
     row_parts = lax.all_to_all(row_parts, COL, 0, 0)
+    col_parts = lax.all_to_all(after(col_parts, row_parts), ROW, 0, 0)
     own_terms, first, second, across, high, low = pl.pallas_call(
         image_kernel,
         out_shape=(jax.ShapeDtypeStruct((nz * own, rows), f32),) * 4

time: 147 us -> 147 us (level)
  no operation moved by 1% of the time
where the time goes in v8:
time: 147 us; the launch traced here: 146 us
  starting transfers between devices  63.2 us (43%)
  waiting for transfers between devices  32.6 us (22%)
  blocking collectives  29.8 us (20%)
  Pallas kernels  11.9 us (8%)
  other arithmetic  3.97 us (3%)
  local copies, waits for them, and re-layouts  3.19 us (2%)
  between operations  1.53 us (1%)
    all_to_all x2, starting transfers between devices, gather(): lax.all_to_all(jnp.broadcast_to(block[None], (n,) + block.shape), axis, 0...  15.2 us
    all_to_all x1, blocking collectives, body(): row_parts = lax.all_to_all(row_parts, COL, 0, 0)  14.9 us
    all_to_all x1, blocking collectives, body(): col_parts = lax.all_to_all(after(col_parts, row_parts), ROW, 0, 0)  14.9 us
    ppermute x3, starting transfers between devices, body(): lax.ppermute(grad_text[k + 1], Y, perm)  8.5 us
    ppermute x1, starting transfers between devices, body(): far_half = lax.ppermute(texts, Y, flip(ny, ny // 2))  7.72 us
    all_to_all x2, waiting for transfers between devices, gather(): lax.all_to_all(jnp.broadcast_to(block[None], (n,) + block.shape), axis, 0...  6.28 us
    ppermute x1, starting transfers between devices, body(): grad_text = grad_text[0] + lax.ppermute(grad_text[1], Y, flip(ny, ny // 2))  5.83 us
    pallas_call x1, Pallas kernels, body(): pl.pallas_call(logits_kernel, out_shape=(jax.ShapeDtypeStruct((cols, rows...  5.53 us
  transfers between devices with their start and end apart: 16, of which 13 were waited for; matrix products, arithmetic and copies ran while one was open for 3% of the time, Pallas kernels for 2%

profile of v8, /device:TPU:2, one launch (start us, length us, event | category | flops | bytes accessed | tf_op | source)
XLA Modules:
  0.0 146.2 jit_solution(11296080524757046258)
XLA Ops:
  0.6 1.7 %broadcast_in_dim.4 = f32[8,16,1024]{2,1,0:T(8,128)} broadcast(f32[16,1024]{1,0:T(8,128)} %bitcast.30), dimensions={1,2} | broadcast | bytes 589824 | tf_op jit(solution)/shard_map/broadcast_in_dim | solution.py:163
  2.3 10.3 %all-to-all-start = ((f32[8,16,1024]{2,1,0:T(8,128)}), f32[8,16,1024]{2,1,0:T(8,128)S(1)}, u32[]{:S(2)}, u32[]{:S(2)}) async-start(f32[8,16,1024]{2,1,0:T(8,128)} %broadcast_in_dim.4), calls=%async_computation | async-start | bytes 1048576 | tf_op jit(solution)/shard_map/all_to_all | solution.py:163
  12.6 7.7 %collective-permute-start = (f32[32,512]{1,0:T(8,128)}, f32[32,512]{1,0:T(8,128)S(1)}, u32[]{:S(2)}, u32[]{:S(2)}) collective-permute-start(f32[32,512]{1,0:T(8,128)} %bitcast.31), channel_id=1, source_target_pairs={{0,256},{64,320},{128,384},{192,448},{256,0},{320,64},{384,128},{4... | collective-permute-start | bytes 196616 | tf_op jit(solution)/shard_map/ppermute | solution.py:213
  20.4 2.9 %collective-permute-done.refs_1_ = f32[32,512]{1,0:T(8,128)S(1)} collective-permute-done((f32[32,512]{1,0:T(8,128)}, f32[32,512]{1,0:T(8,128)S(1)}, u32[]{:S(2)}, u32[]{:S(2)}) %collective-permute-start) | collective-permute-done | bytes 65568 | tf_op jit(solution)/shard_map/ppermute | solution.py:213
  23.3 0.8 pad_maximum_fusion.refs_0_
  24.1 6.0 %all-to-all-done = f32[8,16,1024]{2,1,0:T(8,128)S(1)} async-done(((f32[8,16,1024]{2,1,0:T(8,128)}), f32[8,16,1024]{2,1,0:T(8,128)S(1)}, u32[]{:S(2)}, u32[]{:S(2)}) %all-to-all-start) | async-done | bytes 524320 | tf_op jit(solution)/shard_map/all_to_all | solution.py:163
  30.1 2.4 %collective-permute-start.1 = (f32[128,1024]{1,0:T(8,128)S(1)}, f32[128,1024]{1,0:T(8,128)S(1)}, u32[]{:S(2)}, u32[]{:S(2)}) collective-permute-start(f32[128,1024]{1,0:T(8,128)S(1)} %after.3.own_ref), channel_id=1, source_target_pairs={{0,8},{8,0},{16,24},{24,16},{32,56},{40,48},{48,40},{56,32},{1,9},... | collective-permute-start | bytes 1572872 | tf_op jit(solution)/shard_map/ppermute | solution.py:218
  32.6 0.9 broadcast_in_dim.5
  33.4 4.9 %all-to-all-start.1 = ((f32[4,2,32,512]{3,2,1,0:T(8,128)}), f32[4,2,32,512]{3,2,1,0:T(8,128)S(1)}, u32[]{:S(2)}, u32[]{:S(2)}) async-start(f32[4,2,32,512]{3,2,1,0:T(8,128)} %broadcast_in_dim.5), calls=%async_computation.1 | async-start | bytes 1048576 | tf_op jit(solution)/shard_map/all_to_all | solution.py:163
  38.3 2.9 %collective-permute-done.1.first_ref = f32[128,1024]{1,0:T(8,128)S(1)} collective-permute-done((f32[128,1024]{1,0:T(8,128)S(1)}, f32[128,1024]{1,0:T(8,128)S(1)}, u32[]{:S(2)}, u32[]{:S(2)}) %collective-permute-start.1) | collective-permute-done | bytes 524320 | tf_op jit(solution)/shard_map/ppermute | solution.py:218
  41.2 3.4 %collective-permute-start.3 = (f32[128,1024]{1,0:T(8,128)S(1)}, f32[128,1024]{1,0:T(8,128)S(1)}, u32[]{:S(2)}, u32[]{:S(2)}) collective-permute-start(f32[128,1024]{1,0:T(8,128)S(1)} %collective-permute-done.1.first_ref), channel_id=1, source_target_pairs={{0,24},{8,16},{16,8},{24,0},{32,40},{40,32},{48,56},{56,48},{1,25}... | collective-permute-start | bytes 1572872 | tf_op jit(solution)/shard_map/ppermute | solution.py:220
  44.6 2.4 %collective-permute-start.2 = (f32[128,1024]{1,0:T(8,128)S(1)}, f32[128,1024]{1,0:T(8,128)S(1)}, u32[]{:S(2)}, u32[]{:S(2)}) collective-permute-start(f32[128,1024]{1,0:T(8,128)S(1)} %after.3.own_ref), channel_id=1, source_target_pairs={{0,24},{8,16},{16,8},{24,0},{32,40},{40,32},{48,56},{56,48},{1,25}... | collective-permute-start | bytes 1572872 | tf_op jit(solution)/shard_map/ppermute | solution.py:219
  47.0 5.2 %collective-permute-done.3.across_ref = f32[128,1024]{1,0:T(8,128)S(1)} collective-permute-done((f32[128,1024]{1,0:T(8,128)S(1)}, f32[128,1024]{1,0:T(8,128)S(1)}, u32[]{:S(2)}, u32[]{:S(2)}) %collective-permute-start.3) | collective-permute-done | bytes 524320 | tf_op jit(solution)/shard_map/ppermute | solution.py:220
  54.5 1.9 %collective-permute-start.4 = (f32[8,32,512]{2,1,0:T(8,128)}, f32[8,32,512]{2,1,0:T(8,128)S(1)}, u32[]{:S(2)}, u32[]{:S(2)}) collective-permute-start(f32[8,32,512]{2,1,0:T(8,128)} %broadcast_add_fusion), channel_id=1, source_target_pairs={{0,32},{32,0},{1,33},{33,1},{2,34},{34,2},{3,35},{35,3},{4,36},{36... | collective-permute-start | bytes 1572872 | tf_op jit(solution)/shard_map/ppermute | solution.py:223
  58.5 5.5 %logits.1 = (f32[512,1024]{1,0:T(8,128)S(1)}, f32[32,8,128]{2,1,0:T(8,128)S(1)}, f32[16,8,128]{2,1,0:T(8,128)S(1)}, bf16[512,1024]{1,0:T(8,128)(2,1)S(1)}, bf16[...) custom-call(s32[5]{0:T(128)S(1)} %stack.32.me_ref, ...), custom_call_target="tpu_custom_call" | custom-call | flops 3221225472 | bytes 5242880 | tf_op jit(solution)/shard_map/logits/pallas_call | solution.py:237
  64.1 14.9 %all_to_all.25.refs_1_.row_ref = f32[32,8,128]{2,1,0:T(8,128)S(1)} all-to-all(f32[32,8,128]{2,1,0:T(8,128)S(1)} %get-tuple-element.18), channel_id=1, replica_groups=mesh['y_far'=2,'y_near'=4,'core'=2,'x'=4,'z'=8] {'x','z'}, dimensions={0} | all-to-all | bytes 262144 | tf_op jit(solution)/shard_map/all_to_all | solution.py:255
  79.0 14.9 %all_to_all.26.col_ref = f32[16,8,128]{2,1,0:T(8,128)S(1)} all-to-all(f32[16,8,128]{2,1,0:T(8,128)S(1)} %after.5), channel_id=1, replica_groups=mesh['y_far'=2,'y_near'=4,'core'=2,'x'=4,'z'=8] {'y_far','y_near','core'}, dimensions={0} | all-to-all | bytes 131072 | tf_op jit(solution)/shard_map/all_to_all | solution.py:256
  93.9 3.1 %image_terms.1 = (f32[128,1024]{1,0:T(8,128)S(1)}, f32[128,1024]{1,0:T(8,128)S(1)}, f32[128,1024]{1,0:T(8,128)S(1)}, f32[128,1024]{1,0:T(8,128)S(1)}, bf16[512,1...) custom-call(s32[5]{0:T(128)S(1)} %stack.32.me_ref, f32[512,1024]{1,0:T(8,128)S(1)} %get-tuple-element.17.logits_ref, ...), custom_call_target="tpu_custom_call" | custom-call | flops 1610612736 | bytes 5242880 | tf_op jit(solution)/shard_map/image_terms/pallas_call | solution.py:257
  96.9 2.6 %collective-permute-start.5 = (f32[128,1024]{1,0:T(8,128)S(1)}, f32[128,1024]{1,0:T(8,128)S(1)}, u32[]{:S(2)}, u32[]{:S(2)}) collective-permute-start(f32[128,1024]{1,0:T(8,128)S(1)} %get-tuple-element.24), channel_id=1, source_target_pairs={{0,24},{8,16},{16,8},{24,0},{32,40},{40,32},{48,56},{56,48},{1,25}... | collective-permute-start | bytes 1572872 | tf_op jit(solution)/shard_map/ppermute | solution.py:278
  99.6 2.5 %text_terms.1 = (f32[8,32,512]{2,1,0:T(8,128)S(1)}, f32[8,32,512]{2,1,0:T(8,128)S(1)}) custom-call(s32[5]{0:T(128)S(1)} %stack.32.me_ref, bf16[512,1024]{1,0:T(8,128)(2,1)S(1)} %get-tuple-element.26.high_ref, bf16[512,1024]{1,0:T(8,128)(2,1)S(1)} %get-tuple-element.27.low_ref, bf16[512,1024]{1,0:T(8,128)(2,1)S(1)} %get-tuple-element.28.images_high_ref, ...), custom_call_target="tpu_custom_call" | custom-call | flops 1610612736 | bytes 5242880 | tf_op jit(solution)/shard_map/text_terms/pallas_call | solution.py:268
  102.0 2.7 %collective-permute-start.8 = (f32[8,32,512]{2,1,0:T(8,128)S(1)}, f32[8,32,512]{2,1,0:T(8,128)S(1)}, u32[]{:S(2)}, u32[]{:S(2)}) collective-permute-start(f32[8,32,512]{2,1,0:T(8,128)S(1)} %get-tuple-element.31), channel_id=1, source_target_pairs={{0,32},{32,0},{1,33},{33,1},{2,34},{34,2},{3,35},{35,3},{4,36},{36... | collective-permute-start | bytes 1572872 | tf_op jit(solution)/shard_map/ppermute | solution.py:281
  104.7 2.5 %collective-permute-start.7 = (f32[128,1024]{1,0:T(8,128)S(1)}, f32[128,1024]{1,0:T(8,128)S(1)}, u32[]{:S(2)}, u32[]{:S(2)}) collective-permute-start(f32[128,1024]{1,0:T(8,128)S(1)} %get-tuple-element.25), channel_id=1, source_target_pairs={{0,24},{8,16},{16,8},{24,0},{32,40},{40,32},{48,56},{56,48},{1,25}... | collective-permute-start | bytes 1572872 | tf_op jit(solution)/shard_map/ppermute | solution.py:279
  108.1 4.5 %collective-permute-start.6 = (f32[128,1024]{1,0:T(8,128)S(1)}, f32[128,1024]{1,0:T(8,128)S(1)}, u32[]{:S(2)}, u32[]{:S(2)}) collective-permute-start(f32[128,1024]{1,0:T(8,128)S(1)} %add.79), channel_id=1, source_target_pairs={{0,8},{8,0},{16,24},{24,16},{32,56},{40,48},{48,40},{56,32},{1,9},... | collective-permute-start | bytes 1572872 | tf_op jit(solution)/shard_map/ppermute | solution.py:280
  112.7 2.7 %collective-permute-start.11 = (f32[2,32,512]{2,1,0:T(8,128)S(1)}, f32[2,32,512]{2,1,0:T(8,128)S(1)}, u32[]{:S(2)}, u32[]{:S(2)}) collective-permute-start(f32[2,32,512]{2,1,0:T(8,128)S(1)} %get-tuple-element.32), channel_id=1, source_target_pairs={{0,128},{64,448},{128,256},{192,64},{256,384},{320,192},{384,0},{4... | collective-permute-start | bytes 393224 | tf_op jit(solution)/shard_map/ppermute | solution.py:283
  115.4 2.9 %collective-permute-start.10 = (f32[2,32,512]{2,1,0:T(8,128)S(1)}, f32[2,32,512]{2,1,0:T(8,128)S(1)}, u32[]{:S(2)}, u32[]{:S(2)}) collective-permute-start(f32[2,32,512]{2,1,0:T(8,128)S(1)} %get-tuple-element.33), channel_id=1, source_target_pairs={{0,448},{64,0},{128,64},{192,128},{256,192},{320,256},{384,320},{4... | collective-permute-start | bytes 393224 | tf_op jit(solution)/shard_map/ppermute | solution.py:283
  118.3 3.0 %collective-permute-start.9 = (f32[2,32,512]{2,1,0:T(8,128)S(1)}, f32[2,32,512]{2,1,0:T(8,128)S(1)}, u32[]{:S(2)}, u32[]{:S(2)}) collective-permute-start(f32[2,32,512]{2,1,0:T(8,128)S(1)} %get-tuple-element.34), channel_id=1, source_target_pairs={{0,64},{64,128},{128,192},{192,256},{256,320},{320,384},{384,448},... | collective-permute-start | bytes 393224 | tf_op jit(solution)/shard_map/ppermute | solution.py:283
  122.3 4.0 %collective-permute-done.9 = f32[2,32,512]{2,1,0:T(8,128)S(1)} collective-permute-done((f32[2,32,512]{2,1,0:T(8,128)S(1)}, f32[2,32,512]{2,1,0:T(8,128)S(1)}, u32[]{:S(2)}, u32[]{:S(2)}) %collective-permute-start.9) | collective-permute-done | bytes 131104 | tf_op jit(solution)/shard_map/ppermute | solution.py:283
  126.4 0.9 sum.1
  127.3 3.5 %all-to-all-start.4 = ((f32[8,16,1024]{2,1,0:T(8,128)}), f32[8,16,1024]{2,1,0:T(8,128)S(1)}, u32[]{:S(2)}, u32[]{:S(2)}) async-start(f32[8,16,1024]{2,1,0:T(8,128)} %bitcast.12), calls=%async_computation.4 | async-start | bytes 1048576 | tf_op jit(solution)/shard_map/all_to_all | solution.py:287
  130.8 5.8 %collective-permute-start.12 = (f32[32,512]{1,0:T(8,128)S(1)}, f32[32,512]{1,0:T(8,128)S(1)}, u32[]{:S(2)}, u32[]{:S(2)}) collective-permute-start(f32[32,512]{1,0:T(8,128)S(1)} %slice_bitcast_fusion), channel_id=1, source_target_pairs={{0,256},{64,320},{128,384},{192,448},{256,0},{320,64},{384,128},{4... | collective-permute-start | bytes 196616 | tf_op jit(solution)/shard_map/ppermute | solution.py:286
  136.7 4.2 %collective-permute-done.12 = f32[32,512]{1,0:T(8,128)S(1)} collective-permute-done((f32[32,512]{1,0:T(8,128)S(1)}, f32[32,512]{1,0:T(8,128)S(1)}, u32[]{:S(2)}, u32[]{:S(2)}) %collective-permute-start.12) | collective-permute-done | bytes 65568 | tf_op jit(solution)/shard_map/ppermute | solution.py:286
  141.5 4.0 %all-to-all-done.4 = f32[8,16,1024]{2,1,0:T(8,128)S(1)} async-done(((f32[8,16,1024]{2,1,0:T(8,128)}), f32[8,16,1024]{2,1,0:T(8,128)S(1)}, u32[]{:S(2)}, u32[]{:S(2)}) %all-to-all-start.4) | async-done | bytes 524320 | tf_op jit(solution)/shard_map/all_to_all | solution.py:287
  (25 shorter events, 7.1 us)
Async XLA Ops:
  2.3 27.8 %all-to-all-start = ((f32[8,16,1024]{2,1,0:T(8,128)}), f32[8,16,1024]{2,1,0:T(8,128)S(1)}, u32[]{:S(2)}, u32[]{:S(2)}) async-start(f32[8,16,1024]{2,1,0:T(8,128)} %broadcast_in_dim.4), calls=%async_computation | async-start | bytes 1048576 | tf_op jit(solution)/shard_map/all_to_all | solution.py:163
  12.6 10.6 %collective-permute-start = (f32[32,512]{1,0:T(8,128)}, f32[32,512]{1,0:T(8,128)S(1)}, u32[]{:S(2)}, u32[]{:S(2)}) collective-permute-start(f32[32,512]{1,0:T(8,128)} %bitcast.31), channel_id=1, source_target_pairs={{0,256},{64,320},{128,384},{192,448},{256,0},{320,64},{384,128},{4... | collective-permute-start | bytes 196616 | tf_op jit(solution)/shard_map/ppermute | solution.py:213
  30.1 11.1 %collective-permute-start.1 = (f32[128,1024]{1,0:T(8,128)S(1)}, f32[128,1024]{1,0:T(8,128)S(1)}, u32[]{:S(2)}, u32[]{:S(2)}) collective-permute-start(f32[128,1024]{1,0:T(8,128)S(1)} %after.3.own_ref), channel_id=1, source_target_pairs={{0,8},{8,0},{16,24},{24,16},{32,56},{40,48},{48,40},{56,32},{1,9},... | collective-permute-start | bytes 1572872 | tf_op jit(solution)/shard_map/ppermute | solution.py:218
  33.4 20.2 %all-to-all-start.1 = ((f32[4,2,32,512]{3,2,1,0:T(8,128)}), f32[4,2,32,512]{3,2,1,0:T(8,128)S(1)}, u32[]{:S(2)}, u32[]{:S(2)}) async-start(f32[4,2,32,512]{3,2,1,0:T(8,128)} %broadcast_in_dim.5), calls=%async_computation.1 | async-start | bytes 1048576 | tf_op jit(solution)/shard_map/all_to_all | solution.py:163
  41.2 11.1 %collective-permute-start.3 = (f32[128,1024]{1,0:T(8,128)S(1)}, f32[128,1024]{1,0:T(8,128)S(1)}, u32[]{:S(2)}, u32[]{:S(2)}) collective-permute-start(f32[128,1024]{1,0:T(8,128)S(1)} %collective-permute-done.1.first_ref), channel_id=1, source_target_pairs={{0,24},{8,16},{16,8},{24,0},{32,40},{40,32},{48,56},{56,48},{1,25}... | collective-permute-start | bytes 1572872 | tf_op jit(solution)/shard_map/ppermute | solution.py:220
  44.6 13.3 %collective-permute-start.2 = (f32[128,1024]{1,0:T(8,128)S(1)}, f32[128,1024]{1,0:T(8,128)S(1)}, u32[]{:S(2)}, u32[]{:S(2)}) collective-permute-start(f32[128,1024]{1,0:T(8,128)S(1)} %after.3.own_ref), channel_id=1, source_target_pairs={{0,24},{8,16},{16,8},{24,0},{32,40},{40,32},{48,56},{56,48},{1,25}... | collective-permute-start | bytes 1572872 | tf_op jit(solution)/shard_map/ppermute | solution.py:219
  54.5 4.0 %collective-permute-start.4 = (f32[8,32,512]{2,1,0:T(8,128)}, f32[8,32,512]{2,1,0:T(8,128)S(1)}, u32[]{:S(2)}, u32[]{:S(2)}) collective-permute-start(f32[8,32,512]{2,1,0:T(8,128)} %broadcast_add_fusion), channel_id=1, source_target_pairs={{0,32},{32,0},{1,33},{33,1},{2,34},{34,2},{3,35},{35,3},{4,36},{36... | collective-permute-start | bytes 1572872 | tf_op jit(solution)/shard_map/ppermute | solution.py:223
  96.9 11.1 %collective-permute-start.5 = (f32[128,1024]{1,0:T(8,128)S(1)}, f32[128,1024]{1,0:T(8,128)S(1)}, u32[]{:S(2)}, u32[]{:S(2)}) collective-permute-start(f32[128,1024]{1,0:T(8,128)S(1)} %get-tuple-element.24), channel_id=1, source_target_pairs={{0,24},{8,16},{16,8},{24,0},{32,40},{40,32},{48,56},{56,48},{1,25}... | collective-permute-start | bytes 1572872 | tf_op jit(solution)/shard_map/ppermute | solution.py:278
  102.0 10.6 %collective-permute-start.8 = (f32[8,32,512]{2,1,0:T(8,128)S(1)}, f32[8,32,512]{2,1,0:T(8,128)S(1)}, u32[]{:S(2)}, u32[]{:S(2)}) collective-permute-start(f32[8,32,512]{2,1,0:T(8,128)S(1)} %get-tuple-element.31), channel_id=1, source_target_pairs={{0,32},{32,0},{1,33},{33,1},{2,34},{34,2},{3,35},{35,3},{4,36},{36... | collective-permute-start | bytes 1572872 | tf_op jit(solution)/shard_map/ppermute | solution.py:281
  104.7 21.7 %collective-permute-start.7 = (f32[128,1024]{1,0:T(8,128)S(1)}, f32[128,1024]{1,0:T(8,128)S(1)}, u32[]{:S(2)}, u32[]{:S(2)}) collective-permute-start(f32[128,1024]{1,0:T(8,128)S(1)} %get-tuple-element.25), channel_id=1, source_target_pairs={{0,24},{8,16},{16,8},{24,0},{32,40},{40,32},{48,56},{56,48},{1,25}... | collective-permute-start | bytes 1572872 | tf_op jit(solution)/shard_map/ppermute | solution.py:279
  108.1 18.3 %collective-permute-start.6 = (f32[128,1024]{1,0:T(8,128)S(1)}, f32[128,1024]{1,0:T(8,128)S(1)}, u32[]{:S(2)}, u32[]{:S(2)}) collective-permute-start(f32[128,1024]{1,0:T(8,128)S(1)} %add.79), channel_id=1, source_target_pairs={{0,8},{8,0},{16,24},{24,16},{32,56},{40,48},{48,40},{56,32},{1,9},... | collective-permute-start | bytes 1572872 | tf_op jit(solution)/shard_map/ppermute | solution.py:280
  112.7 9.0 %collective-permute-start.11 = (f32[2,32,512]{2,1,0:T(8,128)S(1)}, f32[2,32,512]{2,1,0:T(8,128)S(1)}, u32[]{:S(2)}, u32[]{:S(2)}) collective-permute-start(f32[2,32,512]{2,1,0:T(8,128)S(1)} %get-tuple-element.32), channel_id=1, source_target_pairs={{0,128},{64,448},{128,256},{192,64},{256,384},{320,192},{384,0},{4... | collective-permute-start | bytes 393224 | tf_op jit(solution)/shard_map/ppermute | solution.py:283
  115.4 6.9 %collective-permute-start.10 = (f32[2,32,512]{2,1,0:T(8,128)S(1)}, f32[2,32,512]{2,1,0:T(8,128)S(1)}, u32[]{:S(2)}, u32[]{:S(2)}) collective-permute-start(f32[2,32,512]{2,1,0:T(8,128)S(1)} %get-tuple-element.33), channel_id=1, source_target_pairs={{0,448},{64,0},{128,64},{192,128},{256,192},{320,256},{384,320},{4... | collective-permute-start | bytes 393224 | tf_op jit(solution)/shard_map/ppermute | solution.py:283
  118.3 8.1 %collective-permute-start.9 = (f32[2,32,512]{2,1,0:T(8,128)S(1)}, f32[2,32,512]{2,1,0:T(8,128)S(1)}, u32[]{:S(2)}, u32[]{:S(2)}) collective-permute-start(f32[2,32,512]{2,1,0:T(8,128)S(1)} %get-tuple-element.34), channel_id=1, source_target_pairs={{0,64},{64,128},{128,192},{192,256},{256,320},{320,384},{384,448},... | collective-permute-start | bytes 393224 | tf_op jit(solution)/shard_map/ppermute | solution.py:283
  127.3 18.2 %all-to-all-start.4 = ((f32[8,16,1024]{2,1,0:T(8,128)}), f32[8,16,1024]{2,1,0:T(8,128)S(1)}, u32[]{:S(2)}, u32[]{:S(2)}) async-start(f32[8,16,1024]{2,1,0:T(8,128)} %bitcast.12), calls=%async_computation.4 | async-start | bytes 1048576 | tf_op jit(solution)/shard_map/all_to_all | solution.py:287
  130.8 10.1 %collective-permute-start.12 = (f32[32,512]{1,0:T(8,128)S(1)}, f32[32,512]{1,0:T(8,128)S(1)}, u32[]{:S(2)}, u32[]{:S(2)}) collective-permute-start(f32[32,512]{1,0:T(8,128)S(1)} %slice_bitcast_fusion), channel_id=1, source_target_pairs={{0,256},{64,320},{128,384},{192,448},{256,0},{320,64},{384,128},{4... | collective-permute-start | bytes 196616 | tf_op jit(solution)/shard_map/ppermute | solution.py:286

commit v9 on v8

--- a/solution.py
+++ b/solution.py
@@ -175,6 +175,21 @@
     )(x, *others)
 
 
+def copy_kernel(*refs):
+    refs[-1][...] = refs[0][...]
+
+
+def copy_after(x, *others):
+    return pl.pallas_call(
+        copy_kernel,
+        out_shape=jax.ShapeDtypeStruct(x.shape, x.dtype),
+        in_specs=[VMEM] + [ANY] * len(others),
+        out_specs=VMEM,
+        compiler_params=PARAMS,
+        name="copy",
+    )(x, *others)
+
+
 def sum_of(a, b, c, then):
     return pl.pallas_call(
         sum_kernel,
@@ -220,7 +235,8 @@
     across = lax.ppermute(first, ("core", "x"), to_second)
     images = (images, first, second, across)
     near = gather(texts, "y_near", ny // 2).reshape(ny, own_text, cols)
-    far = lax.ppermute(near + 0.0 * across[0, 0], "core", flip(nc, 1))
+    near = copy_after(near, across)
+    far = lax.ppermute(near, "core", flip(nc, 1))
     width = nx * nz * own
     row_start = lax.axis_index(ROW) * rows
     col_start = lax.axis_index(COL) * cols

time: 147 us -> 147 us (level)
    all_to_all x2, waiting for transfers between devices: 6.28 us -> 12.7 us  [gather(): lax.all_to_all(jnp.broadcast_to(block[None], (n,) + block.shape), axis, 0...]
    ppermute x1, waiting for transfers between devices: 5.22 us -> 0.01 us  [body(): across = lax.ppermute(first, ('core', 'x'), to_second)]
  transfers between devices with their start and end apart: 16 -> 16, of which waited for: 13 -> 11; matrix products, arithmetic and copies ran while one was open for 3% -> 2% of each run, Pallas kernels for 2% -> 2%
where the time goes in v9:
time: 147 us; the launch traced here: 146 us
  starting transfers between devices  63.2 us (43%)
  waiting for transfers between devices  33.9 us (23%)
  blocking collectives  29.8 us (20%)
  Pallas kernels  12.4 us (8%)
  other arithmetic  3.13 us (2%)
  local copies, waits for them, and re-layouts  2.68 us (2%)
    all_to_all x2, starting transfers between devices, gather(): lax.all_to_all(jnp.broadcast_to(block[None], (n,) + block.shape), axis, 0...  15.2 us
    all_to_all x1, blocking collectives, body(): row_parts = lax.all_to_all(row_parts, COL, 0, 0)  15 us
    all_to_all x1, blocking collectives, body(): col_parts = lax.all_to_all(after(col_parts, row_parts), ROW, 0, 0)  14.9 us
    all_to_all x2, waiting for transfers between devices, gather(): lax.all_to_all(jnp.broadcast_to(block[None], (n,) + block.shape), axis, 0...  12.7 us
    ppermute x3, starting transfers between devices, body(): lax.ppermute(grad_text[k + 1], Y, perm)  8.49 us
    ppermute x1, starting transfers between devices, body(): far_half = lax.ppermute(texts, Y, flip(ny, ny // 2))  7.72 us
    pallas_call x1, Pallas kernels, body(): pl.pallas_call(logits_kernel, out_shape=(jax.ShapeDtypeStruct((cols, rows...  5.99 us
    ppermute x1, starting transfers between devices, body(): grad_text = grad_text[0] + lax.ppermute(grad_text[1], Y, flip(ny, ny // 2))  5.83 us
  transfers between devices with their start and end apart: 16, of which 11 were waited for; matrix products, arithmetic and copies ran while one was open for 2% of the time, Pallas kernels for 2%

profile of v9, /device:TPU:2, one launch (start us, length us, event | category | flops | bytes accessed | tf_op | source)
XLA Modules:
  0.0 146.0 jit_solution(16419505864874394193)
XLA Ops:
  0.6 1.7 %broadcast_in_dim.4 = f32[8,16,1024]{2,1,0:T(8,128)} broadcast(f32[16,1024]{1,0:T(8,128)} %bitcast.28), dimensions={1,2} | broadcast | bytes 589824 | tf_op jit(solution)/shard_map/broadcast_in_dim | solution.py:163
  2.3 10.3 %all-to-all-start = ((f32[8,16,1024]{2,1,0:T(8,128)}), f32[8,16,1024]{2,1,0:T(8,128)S(1)}, u32[]{:S(2)}, u32[]{:S(2)}) async-start(f32[8,16,1024]{2,1,0:T(8,128)} %broadcast_in_dim.4), calls=%async_computation | async-start | bytes 1048576 | tf_op jit(solution)/shard_map/all_to_all | solution.py:163
  12.6 7.7 %collective-permute-start = (f32[32,512]{1,0:T(8,128)}, f32[32,512]{1,0:T(8,128)S(1)}, u32[]{:S(2)}, u32[]{:S(2)}) collective-permute-start(f32[32,512]{1,0:T(8,128)} %bitcast.29), channel_id=1, source_target_pairs={{0,256},{64,320},{128,384},{192,448},{256,0},{320,64},{384,128},{4... | collective-permute-start | bytes 196616 | tf_op jit(solution)/shard_map/ppermute | solution.py:228
  20.4 2.9 %collective-permute-done.refs_1_ = f32[32,512]{1,0:T(8,128)S(1)} collective-permute-done((f32[32,512]{1,0:T(8,128)}, f32[32,512]{1,0:T(8,128)S(1)}, u32[]{:S(2)}, u32[]{:S(2)}) %collective-permute-start) | collective-permute-done | bytes 65568 | tf_op jit(solution)/shard_map/ppermute | solution.py:228
  24.1 6.0 %all-to-all-done = f32[8,16,1024]{2,1,0:T(8,128)S(1)} async-done(((f32[8,16,1024]{2,1,0:T(8,128)}), f32[8,16,1024]{2,1,0:T(8,128)S(1)}, u32[]{:S(2)}, u32[]{:S(2)}) %all-to-all-start) | async-done | bytes 524320 | tf_op jit(solution)/shard_map/all_to_all | solution.py:163
  30.1 2.4 %collective-permute-start.1 = (f32[128,1024]{1,0:T(8,128)S(1)}, f32[128,1024]{1,0:T(8,128)S(1)}, u32[]{:S(2)}, u32[]{:S(2)}) collective-permute-start(f32[128,1024]{1,0:T(8,128)S(1)} %after.3.own_ref), channel_id=1, source_target_pairs={{0,8},{8,0},{16,24},{24,16},{32,56},{40,48},{48,40},{56,32},{1,9},... | collective-permute-start | bytes 1572872 | tf_op jit(solution)/shard_map/ppermute | solution.py:233
  32.6 0.9 broadcast_in_dim.5
  33.4 4.9 %all-to-all-start.1 = ((f32[4,2,32,512]{3,2,1,0:T(8,128)}), f32[4,2,32,512]{3,2,1,0:T(8,128)S(1)}, u32[]{:S(2)}, u32[]{:S(2)}) async-start(f32[4,2,32,512]{3,2,1,0:T(8,128)} %broadcast_in_dim.5), calls=%async_computation.1 | async-start | bytes 1048576 | tf_op jit(solution)/shard_map/all_to_all | solution.py:163
  38.3 2.9 %collective-permute-done.1.first_ref = f32[128,1024]{1,0:T(8,128)S(1)} collective-permute-done((f32[128,1024]{1,0:T(8,128)S(1)}, f32[128,1024]{1,0:T(8,128)S(1)}, u32[]{:S(2)}, u32[]{:S(2)}) %collective-permute-start.1) | collective-permute-done | bytes 524320 | tf_op jit(solution)/shard_map/ppermute | solution.py:233
  41.2 3.4 %collective-permute-start.3 = (f32[128,1024]{1,0:T(8,128)S(1)}, f32[128,1024]{1,0:T(8,128)S(1)}, u32[]{:S(2)}, u32[]{:S(2)}) collective-permute-start(f32[128,1024]{1,0:T(8,128)S(1)} %collective-permute-done.1.first_ref), channel_id=1, source_target_pairs={{0,24},{8,16},{16,8},{24,0},{32,40},{40,32},{48,56},{56,48},{1,25}... | collective-permute-start | bytes 1572872 | tf_op jit(solution)/shard_map/ppermute | solution.py:235
  44.6 2.4 %collective-permute-start.2 = (f32[128,1024]{1,0:T(8,128)S(1)}, f32[128,1024]{1,0:T(8,128)S(1)}, u32[]{:S(2)}, u32[]{:S(2)}) collective-permute-start(f32[128,1024]{1,0:T(8,128)S(1)} %after.3.own_ref), channel_id=1, source_target_pairs={{0,24},{8,16},{16,8},{24,0},{32,40},{40,32},{48,56},{56,48},{1,25}... | collective-permute-start | bytes 1572872 | tf_op jit(solution)/shard_map/ppermute | solution.py:234
  47.0 6.6 %all-to-all-done.1 = f32[4,2,32,512]{3,2,1,0:T(8,128)S(1)} async-done(((f32[4,2,32,512]{3,2,1,0:T(8,128)}), f32[4,2,32,512]{3,2,1,0:T(8,128)S(1)}, u32[]{:S(2)}, u32[]{:S(2)}) %all-to-all-start.1) | async-done | bytes 524320 | tf_op jit(solution)/shard_map/all_to_all | solution.py:163
  53.7 1.9 %collective-permute-start.4 = (f32[8,32,512]{2,1,0:T(8,128)S(1)}, f32[8,32,512]{2,1,0:T(8,128)}, u32[]{:S(2)}, u32[]{:S(2)}) collective-permute-start(f32[8,32,512]{2,1,0:T(8,128)S(1)} %copy.12.near_ref), channel_id=1, source_target_pairs={{0,32},{32,0},{1,33},{33,1},{2,34},{34,2},{3,35},{35,3},{4,36},{36... | collective-permute-start | bytes 1572872 | tf_op jit(solution)/shard_map/ppermute | solution.py:239
  56.6 1.3 collective-permute-done.2.second_ref
  57.9 6.0 %logits.1 = (f32[512,1024]{1,0:T(8,128)S(1)}, f32[32,8,128]{2,1,0:T(8,128)S(1)}, f32[16,8,128]{2,1,0:T(8,128)S(1)}, bf16[512,1024]{1,0:T(8,128)(2,1)S(1)}, bf16[...) custom-call(s32[5]{0:T(128)S(1)} %stack.32.me_ref, ...), custom_call_target="tpu_custom_call" | custom-call | flops 3221225472 | bytes 5242880 | tf_op jit(solution)/shard_map/logits/pallas_call | solution.py:253
  63.9 15.0 %all_to_all.25.refs_1_.row_ref = f32[32,8,128]{2,1,0:T(8,128)S(1)} all-to-all(f32[32,8,128]{2,1,0:T(8,128)S(1)} %get-tuple-element.18), channel_id=1, replica_groups=mesh['y_far'=2,'y_near'=4,'core'=2,'x'=4,'z'=8] {'x','z'}, dimensions={0} | all-to-all | bytes 262144 | tf_op jit(solution)/shard_map/all_to_all | solution.py:271
  78.9 14.9 %all_to_all.26.col_ref = f32[16,8,128]{2,1,0:T(8,128)S(1)} all-to-all(f32[16,8,128]{2,1,0:T(8,128)S(1)} %after.5), channel_id=1, replica_groups=mesh['y_far'=2,'y_near'=4,'core'=2,'x'=4,'z'=8] {'y_far','y_near','core'}, dimensions={0} | all-to-all | bytes 131072 | tf_op jit(solution)/shard_map/all_to_all | solution.py:272
  93.7 3.1 %image_terms.1 = (f32[128,1024]{1,0:T(8,128)S(1)}, f32[128,1024]{1,0:T(8,128)S(1)}, f32[128,1024]{1,0:T(8,128)S(1)}, f32[128,1024]{1,0:T(8,128)S(1)}, bf16[512,1...) custom-call(s32[5]{0:T(128)S(1)} %stack.32.me_ref, f32[512,1024]{1,0:T(8,128)S(1)} %get-tuple-element.17.logits_ref, ...), custom_call_target="tpu_custom_call" | custom-call | flops 1610612736 | bytes 5242880 | tf_op jit(solution)/shard_map/image_terms/pallas_call | solution.py:273
  96.8 2.6 %collective-permute-start.5 = (f32[128,1024]{1,0:T(8,128)S(1)}, f32[128,1024]{1,0:T(8,128)S(1)}, u32[]{:S(2)}, u32[]{:S(2)}) collective-permute-start(f32[128,1024]{1,0:T(8,128)S(1)} %get-tuple-element.24), channel_id=1, source_target_pairs={{0,24},{8,16},{16,8},{24,0},{32,40},{40,32},{48,56},{56,48},{1,25}... | collective-permute-start | bytes 1572872 | tf_op jit(solution)/shard_map/ppermute | solution.py:294
  99.4 2.5 %text_terms.1 = (f32[8,32,512]{2,1,0:T(8,128)S(1)}, f32[8,32,512]{2,1,0:T(8,128)S(1)}) custom-call(s32[5]{0:T(128)S(1)} %stack.32.me_ref, bf16[512,1024]{1,0:T(8,128)(2,1)S(1)} %get-tuple-element.26.high_ref, bf16[512,1024]{1,0:T(8,128)(2,1)S(1)} %get-tuple-element.27.low_ref, bf16[512,1024]{1,0:T(8,128)(2,1)S(1)} %get-tuple-element.28.images_high_ref, ...), custom_call_target="tpu_custom_call" | custom-call | flops 1610612736 | bytes 5242880 | tf_op jit(solution)/shard_map/text_terms/pallas_call | solution.py:284
  101.9 2.7 %collective-permute-start.8 = (f32[8,32,512]{2,1,0:T(8,128)S(1)}, f32[8,32,512]{2,1,0:T(8,128)S(1)}, u32[]{:S(2)}, u32[]{:S(2)}) collective-permute-start(f32[8,32,512]{2,1,0:T(8,128)S(1)} %get-tuple-element.31), channel_id=1, source_target_pairs={{0,32},{32,0},{1,33},{33,1},{2,34},{34,2},{3,35},{35,3},{4,36},{36... | collective-permute-start | bytes 1572872 | tf_op jit(solution)/shard_map/ppermute | solution.py:297
  104.6 2.5 %collective-permute-start.7 = (f32[128,1024]{1,0:T(8,128)S(1)}, f32[128,1024]{1,0:T(8,128)S(1)}, u32[]{:S(2)}, u32[]{:S(2)}) collective-permute-start(f32[128,1024]{1,0:T(8,128)S(1)} %get-tuple-element.25), channel_id=1, source_target_pairs={{0,24},{8,16},{16,8},{24,0},{32,40},{40,32},{48,56},{56,48},{1,25}... | collective-permute-start | bytes 1572872 | tf_op jit(solution)/shard_map/ppermute | solution.py:295
  107.9 4.5 %collective-permute-start.6 = (f32[128,1024]{1,0:T(8,128)S(1)}, f32[128,1024]{1,0:T(8,128)S(1)}, u32[]{:S(2)}, u32[]{:S(2)}) collective-permute-start(f32[128,1024]{1,0:T(8,128)S(1)} %add.71), channel_id=1, source_target_pairs={{0,8},{8,0},{16,24},{24,16},{32,56},{40,48},{48,40},{56,32},{1,9},... | collective-permute-start | bytes 1572872 | tf_op jit(solution)/shard_map/ppermute | solution.py:296
  112.6 2.7 %collective-permute-start.11 = (f32[2,32,512]{2,1,0:T(8,128)S(1)}, f32[2,32,512]{2,1,0:T(8,128)S(1)}, u32[]{:S(2)}, u32[]{:S(2)}) collective-permute-start(f32[2,32,512]{2,1,0:T(8,128)S(1)} %get-tuple-element.32), channel_id=1, source_target_pairs={{0,128},{64,448},{128,256},{192,64},{256,384},{320,192},{384,0},{4... | collective-permute-start | bytes 393224 | tf_op jit(solution)/shard_map/ppermute | solution.py:299
  115.3 2.9 %collective-permute-start.10 = (f32[2,32,512]{2,1,0:T(8,128)S(1)}, f32[2,32,512]{2,1,0:T(8,128)S(1)}, u32[]{:S(2)}, u32[]{:S(2)}) collective-permute-start(f32[2,32,512]{2,1,0:T(8,128)S(1)} %get-tuple-element.33), channel_id=1, source_target_pairs={{0,448},{64,0},{128,64},{192,128},{256,192},{320,256},{384,320},{4... | collective-permute-start | bytes 393224 | tf_op jit(solution)/shard_map/ppermute | solution.py:299
  118.1 3.0 %collective-permute-start.9 = (f32[2,32,512]{2,1,0:T(8,128)S(1)}, f32[2,32,512]{2,1,0:T(8,128)S(1)}, u32[]{:S(2)}, u32[]{:S(2)}) collective-permute-start(f32[2,32,512]{2,1,0:T(8,128)S(1)} %get-tuple-element.34), channel_id=1, source_target_pairs={{0,64},{64,128},{128,192},{192,256},{256,320},{320,384},{384,448},... | collective-permute-start | bytes 393224 | tf_op jit(solution)/shard_map/ppermute | solution.py:299
  122.2 4.0 %collective-permute-done.9 = f32[2,32,512]{2,1,0:T(8,128)S(1)} collective-permute-done((f32[2,32,512]{2,1,0:T(8,128)S(1)}, f32[2,32,512]{2,1,0:T(8,128)S(1)}, u32[]{:S(2)}, u32[]{:S(2)}) %collective-permute-start.9) | collective-permute-done | bytes 131104 | tf_op jit(solution)/shard_map/ppermute | solution.py:299
  126.3 0.9 sum.1
  127.2 3.5 %all-to-all-start.4 = ((f32[8,16,1024]{2,1,0:T(8,128)}), f32[8,16,1024]{2,1,0:T(8,128)S(1)}, u32[]{:S(2)}, u32[]{:S(2)}) async-start(f32[8,16,1024]{2,1,0:T(8,128)} %bitcast.11), calls=%async_computation.4 | async-start | bytes 1048576 | tf_op jit(solution)/shard_map/all_to_all | solution.py:303
  130.7 5.8 %collective-permute-start.12 = (f32[32,512]{1,0:T(8,128)S(1)}, f32[32,512]{1,0:T(8,128)S(1)}, u32[]{:S(2)}, u32[]{:S(2)}) collective-permute-start(f32[32,512]{1,0:T(8,128)S(1)} %slice_bitcast_fusion), channel_id=1, source_target_pairs={{0,256},{64,320},{128,384},{192,448},{256,0},{320,64},{384,128},{4... | collective-permute-start | bytes 196616 | tf_op jit(solution)/shard_map/ppermute | solution.py:302
  136.5 4.2 %collective-permute-done.12 = f32[32,512]{1,0:T(8,128)S(1)} collective-permute-done((f32[32,512]{1,0:T(8,128)S(1)}, f32[32,512]{1,0:T(8,128)S(1)}, u32[]{:S(2)}, u32[]{:S(2)}) %collective-permute-start.12) | collective-permute-done | bytes 65568 | tf_op jit(solution)/shard_map/ppermute | solution.py:302
  141.4 4.0 %all-to-all-done.4 = f32[8,16,1024]{2,1,0:T(8,128)S(1)} async-done(((f32[8,16,1024]{2,1,0:T(8,128)}), f32[8,16,1024]{2,1,0:T(8,128)S(1)}, u32[]{:S(2)}, u32[]{:S(2)}) %all-to-all-start.4) | async-done | bytes 524320 | tf_op jit(solution)/shard_map/all_to_all | solution.py:303
  (24 shorter events, 5.2 us)
Async XLA Ops:
  2.3 27.8 %all-to-all-start = ((f32[8,16,1024]{2,1,0:T(8,128)}), f32[8,16,1024]{2,1,0:T(8,128)S(1)}, u32[]{:S(2)}, u32[]{:S(2)}) async-start(f32[8,16,1024]{2,1,0:T(8,128)} %broadcast_in_dim.4), calls=%async_computation | async-start | bytes 1048576 | tf_op jit(solution)/shard_map/all_to_all | solution.py:163
  12.6 10.6 %collective-permute-start = (f32[32,512]{1,0:T(8,128)}, f32[32,512]{1,0:T(8,128)S(1)}, u32[]{:S(2)}, u32[]{:S(2)}) collective-permute-start(f32[32,512]{1,0:T(8,128)} %bitcast.29), channel_id=1, source_target_pairs={{0,256},{64,320},{128,384},{192,448},{256,0},{320,64},{384,128},{4... | collective-permute-start | bytes 196616 | tf_op jit(solution)/shard_map/ppermute | solution.py:228
  30.1 11.1 %collective-permute-start.1 = (f32[128,1024]{1,0:T(8,128)S(1)}, f32[128,1024]{1,0:T(8,128)S(1)}, u32[]{:S(2)}, u32[]{:S(2)}) collective-permute-start(f32[128,1024]{1,0:T(8,128)S(1)} %after.3.own_ref), channel_id=1, source_target_pairs={{0,8},{8,0},{16,24},{24,16},{32,56},{40,48},{48,40},{56,32},{1,9},... | collective-permute-start | bytes 1572872 | tf_op jit(solution)/shard_map/ppermute | solution.py:233
  33.4 20.2 %all-to-all-start.1 = ((f32[4,2,32,512]{3,2,1,0:T(8,128)}), f32[4,2,32,512]{3,2,1,0:T(8,128)S(1)}, u32[]{:S(2)}, u32[]{:S(2)}) async-start(f32[4,2,32,512]{3,2,1,0:T(8,128)} %broadcast_in_dim.5), calls=%async_computation.1 | async-start | bytes 1048576 | tf_op jit(solution)/shard_map/all_to_all | solution.py:163
  41.2 12.5 %collective-permute-start.3 = (f32[128,1024]{1,0:T(8,128)S(1)}, f32[128,1024]{1,0:T(8,128)S(1)}, u32[]{:S(2)}, u32[]{:S(2)}) collective-permute-start(f32[128,1024]{1,0:T(8,128)S(1)} %collective-permute-done.1.first_ref), channel_id=1, source_target_pairs={{0,24},{8,16},{16,8},{24,0},{32,40},{40,32},{48,56},{56,48},{1,25}... | collective-permute-start | bytes 1572872 | tf_op jit(solution)/shard_map/ppermute | solution.py:235
  44.6 13.3 %collective-permute-start.2 = (f32[128,1024]{1,0:T(8,128)S(1)}, f32[128,1024]{1,0:T(8,128)S(1)}, u32[]{:S(2)}, u32[]{:S(2)}) collective-permute-start(f32[128,1024]{1,0:T(8,128)S(1)} %after.3.own_ref), channel_id=1, source_target_pairs={{0,24},{8,16},{16,8},{24,0},{32,40},{40,32},{48,56},{56,48},{1,25}... | collective-permute-start | bytes 1572872 | tf_op jit(solution)/shard_map/ppermute | solution.py:234
  53.7 4.2 %collective-permute-start.4 = (f32[8,32,512]{2,1,0:T(8,128)S(1)}, f32[8,32,512]{2,1,0:T(8,128)}, u32[]{:S(2)}, u32[]{:S(2)}) collective-permute-start(f32[8,32,512]{2,1,0:T(8,128)S(1)} %copy.12.near_ref), channel_id=1, source_target_pairs={{0,32},{32,0},{1,33},{33,1},{2,34},{34,2},{3,35},{35,3},{4,36},{36... | collective-permute-start | bytes 1572872 | tf_op jit(solution)/shard_map/ppermute | solution.py:239
  96.8 11.1 %collective-permute-start.5 = (f32[128,1024]{1,0:T(8,128)S(1)}, f32[128,1024]{1,0:T(8,128)S(1)}, u32[]{:S(2)}, u32[]{:S(2)}) collective-permute-start(f32[128,1024]{1,0:T(8,128)S(1)} %get-tuple-element.24), channel_id=1, source_target_pairs={{0,24},{8,16},{16,8},{24,0},{32,40},{40,32},{48,56},{56,48},{1,25}... | collective-permute-start | bytes 1572872 | tf_op jit(solution)/shard_map/ppermute | solution.py:294
  101.9 10.6 %collective-permute-start.8 = (f32[8,32,512]{2,1,0:T(8,128)S(1)}, f32[8,32,512]{2,1,0:T(8,128)S(1)}, u32[]{:S(2)}, u32[]{:S(2)}) collective-permute-start(f32[8,32,512]{2,1,0:T(8,128)S(1)} %get-tuple-element.31), channel_id=1, source_target_pairs={{0,32},{32,0},{1,33},{33,1},{2,34},{34,2},{3,35},{35,3},{4,36},{36... | collective-permute-start | bytes 1572872 | tf_op jit(solution)/shard_map/ppermute | solution.py:297
  104.6 21.7 %collective-permute-start.7 = (f32[128,1024]{1,0:T(8,128)S(1)}, f32[128,1024]{1,0:T(8,128)S(1)}, u32[]{:S(2)}, u32[]{:S(2)}) collective-permute-start(f32[128,1024]{1,0:T(8,128)S(1)} %get-tuple-element.25), channel_id=1, source_target_pairs={{0,24},{8,16},{16,8},{24,0},{32,40},{40,32},{48,56},{56,48},{1,25}... | collective-permute-start | bytes 1572872 | tf_op jit(solution)/shard_map/ppermute | solution.py:295
  107.9 18.3 %collective-permute-start.6 = (f32[128,1024]{1,0:T(8,128)S(1)}, f32[128,1024]{1,0:T(8,128)S(1)}, u32[]{:S(2)}, u32[]{:S(2)}) collective-permute-start(f32[128,1024]{1,0:T(8,128)S(1)} %add.71), channel_id=1, source_target_pairs={{0,8},{8,0},{16,24},{24,16},{32,56},{40,48},{48,40},{56,32},{1,9},... | collective-permute-start | bytes 1572872 | tf_op jit(solution)/shard_map/ppermute | solution.py:296
  112.6 9.0 %collective-permute-start.11 = (f32[2,32,512]{2,1,0:T(8,128)S(1)}, f32[2,32,512]{2,1,0:T(8,128)S(1)}, u32[]{:S(2)}, u32[]{:S(2)}) collective-permute-start(f32[2,32,512]{2,1,0:T(8,128)S(1)} %get-tuple-element.32), channel_id=1, source_target_pairs={{0,128},{64,448},{128,256},{192,64},{256,384},{320,192},{384,0},{4... | collective-permute-start | bytes 393224 | tf_op jit(solution)/shard_map/ppermute | solution.py:299
  115.3 6.9 %collective-permute-start.10 = (f32[2,32,512]{2,1,0:T(8,128)S(1)}, f32[2,32,512]{2,1,0:T(8,128)S(1)}, u32[]{:S(2)}, u32[]{:S(2)}) collective-permute-start(f32[2,32,512]{2,1,0:T(8,128)S(1)} %get-tuple-element.33), channel_id=1, source_target_pairs={{0,448},{64,0},{128,64},{192,128},{256,192},{320,256},{384,320},{4... | collective-permute-start | bytes 393224 | tf_op jit(solution)/shard_map/ppermute | solution.py:299
  118.1 8.1 %collective-permute-start.9 = (f32[2,32,512]{2,1,0:T(8,128)S(1)}, f32[2,32,512]{2,1,0:T(8,128)S(1)}, u32[]{:S(2)}, u32[]{:S(2)}) collective-permute-start(f32[2,32,512]{2,1,0:T(8,128)S(1)} %get-tuple-element.34), channel_id=1, source_target_pairs={{0,64},{64,128},{128,192},{192,256},{256,320},{320,384},{384,448},... | collective-permute-start | bytes 393224 | tf_op jit(solution)/shard_map/ppermute | solution.py:299
  127.2 18.2 %all-to-all-start.4 = ((f32[8,16,1024]{2,1,0:T(8,128)}), f32[8,16,1024]{2,1,0:T(8,128)S(1)}, u32[]{:S(2)}, u32[]{:S(2)}) async-start(f32[8,16,1024]{2,1,0:T(8,128)} %bitcast.11), calls=%async_computation.4 | async-start | bytes 1048576 | tf_op jit(solution)/shard_map/all_to_all | solution.py:303
  130.7 10.1 %collective-permute-start.12 = (f32[32,512]{1,0:T(8,128)S(1)}, f32[32,512]{1,0:T(8,128)S(1)}, u32[]{:S(2)}, u32[]{:S(2)}) collective-permute-start(f32[32,512]{1,0:T(8,128)S(1)} %slice_bitcast_fusion), channel_id=1, source_target_pairs={{0,256},{64,320},{128,384},{192,448},{256,0},{320,64},{384,128},{4... | collective-permute-start | bytes 196616 | tf_op jit(solution)/shard_map/ppermute | solution.py:302
